TPU v7x, 32 devices: a whole 2x2x4 slice. The times are simulated.
32 devices in a mesh: group: 4 (over y, x), batch: 8 (over z, core).
Axes of the slice: x: 2, y: 2, z: 4, core: 2. Of those that a mesh axis runs over, the one named last changes fastest.
Arguments:
- pixels: bfloat16 [4, 32, 16, 196, 256], P('group', 'batch'), may hold values from -18 to 18, as said below
- band_count: int32 [4, 32], P('group', 'batch'), may hold values from 2 to 16, as said below
- band_bin: int32 [4, 32, 16], P('group', 'batch'), may hold values from 0 to 511, as said below
- bin_wave: float32 [512], replicated, may hold values from 0.4 to 14
- run_mean: float32 [512], replicated, may hold values from -4 to 4
- run_var: float32 [512], replicated, may hold values from 0.5 to 4
- weight_tokens: float32 [128, 128], replicated, may hold values from -5 to 5
- bias_token: float32 [128], replicated, may hold values from -5 to 5
- hyper_in: float32 [128, 384], replicated, may hold values from -0.5 to 0.5
- hyper_qv_bias: float32 [2, 128], replicated, may hold values from -2 to 2
- hyper_out: float32 [128, 128], replicated, may hold values from -1 to 1
- hyper_out_bias: float32 [128], replicated, may hold values from -2 to 2
- hyper_gain: float32 [2, 128], replicated, may hold values from 0.5 to 1.5
- hyper_shift: float32 [2, 128], replicated, may hold values from -2 to 2
- hyper_up: float32 [128, 2048], replicated, may hold values from -0.5 to 0.5
- hyper_up_bias: float32 [2048], replicated, may hold values from -2 to 2
- hyper_down: float32 [2048, 128], replicated, may hold values from -0.1875 to 0.1875
- hyper_down_bias: float32 [128], replicated, may hold values from -2 to 2
- kernel_weight: bfloat16 [256, 768, 128], P('batch'), may hold values from -0.01171875 to 0.01171875
- bias_weight: float32 [128, 768], replicated, may hold values from -0.5 to 0.5
- bias_offset: float32 [768], replicated, may hold values from -2 to 2
- norm_gain: float32 [2, 768], replicated, may hold values from 0.5 to 1.5
- norm_shift: float32 [2, 768], replicated, may hold values from -2 to 2
- w_qkv: bfloat16 [768, 2304], replicated, may hold values from -0.21875 to 0.21875
- qv_bias: float32 [2, 768], replicated, may hold values from -2 to 2
- w_out: bfloat16 [768, 768], replicated, may hold values from -0.875 to 0.875
- out_bias: float32 [768], replicated, may hold values from -2 to 2
- w_up: bfloat16 [768, 3072], replicated, may hold values from -0.21875 to 0.21875
- up_bias: float32 [3072], replicated, may hold values from -2 to 2
- w_down: bfloat16 [3072, 768], replicated, may hold values from -0.15625 to 0.15625
- down_bias: float32 [768], replicated, may hold values from -2 to 2
- cotangent: bfloat16 [4, 32, 196, 768], P('group', 'batch'), may hold values from -6 to 6
Outputs:
- block_out: bfloat16 [4, 32, 196, 768], P('group', 'batch')
- pixel_grad: bfloat16 [4, 32, 16, 196, 256], P('group', 'batch')
- batch_mean: float32 [512], replicated
- batch_var: float32 [512], replicated
- grad_weight_tokens: float32 [128, 128], replicated
- grad_bias_token: float32 [128], replicated
- grad_hyper_in: float32 [128, 384], replicated
- grad_hyper_qv_bias: float32 [2, 128], replicated
- grad_hyper_out: float32 [128, 128], replicated
- grad_hyper_out_bias: float32 [128], replicated
- grad_hyper_gain: float32 [2, 128], replicated
- grad_hyper_shift: float32 [2, 128], replicated
- grad_hyper_up: float32 [128, 2048], replicated
- grad_hyper_up_bias: float32 [2048], replicated
- grad_hyper_down: float32 [2048, 128], replicated
- grad_hyper_down_bias: float32 [128], replicated
- grad_kernel_weight: float32 [256, 768, 128], P('batch')
- grad_bias_weight: float32 [128, 768], replicated
- grad_bias_offset: float32 [768], replicated
- grad_norm_gain: float32 [2, 768], replicated
- grad_norm_shift: float32 [2, 768], replicated
- grad_w_qkv: float32 [768, 2304], P('group')
- grad_qv_bias: float32 [2, 768], replicated
- grad_w_out: float32 [768, 768], P('group')
- grad_out_bias: float32 [768], replicated
- grad_w_up: float32 [768, 3072], P('group')
- grad_up_bias: float32 [3072], replicated
- grad_w_down: float32 [3072, 768], P('group')
- grad_down_bias: float32 [768], replicated
Inputs may be any that keep to these rules, and one draw needn't show every extreme that they name: `band_count`: live bands fill an image's first slots. With c = 2 for group 0 and c = max(2, (g + 1) * 4) for group g > 0, every image of group g has between c - c // 3 and c live bands, and in each group one image, drawn from the seed, has exactly c. `band_bin`: max(2, 32) bins, drawn from the seed, are named by no slot of any image. `pixels`: each band slot has its own offset and scale.
All inputs are finite; a program needn't handle non-finite values.
Results may differ from a plain program's by a relative error of at most 0.015.
Values may be sent and summed in bfloat16 or wider, within the bound.
No kernel may reach another device: no remote copies, remote signals or barrier semaphores. Data moves between devices by JAX's collectives and lax.ppermute only.
A program may use at most 512 MiB of HBM per device.

v0:
```python
from functools import partial

import jax
import jax.numpy as jnp
from jax import lax
from jax.sharding import PartitionSpec as P

HEADS = 12
HHEADS = 4


highest = lax.Precision.HIGHEST
stat_eps = 1e-05
hyper_eps = 1e-05
block_eps = 1e-06
wave_scale = 1000.0


def layer_norm(values, gain, shift, epsilon):
    center = values - jnp.mean(values, axis=-1, keepdims=True)
    return (
        center * lax.rsqrt(jnp.mean(center * center, axis=-1, keepdims=True) + epsilon) * gain
        + shift
    )


def norm_parts(values, epsilon):
    center = values - jnp.mean(values, axis=-1, keepdims=True)
    factor = lax.rsqrt(jnp.mean(center * center, axis=-1, keepdims=True) + epsilon)
    return (center * factor, factor)


def norm_back(grad_hat, normal_hat, factor):
    return factor * (
        grad_hat
        - jnp.mean(grad_hat, axis=-1, keepdims=True)
        - normal_hat * jnp.mean(grad_hat * normal_hat, axis=-1, keepdims=True)
    )


def wave_embed(band_wave, model_width):
    half_width = model_width // 2
    ladder = jnp.arange(half_width, dtype=jnp.float32) / half_width
    frequency = 1.0 / 10000.0**ladder
    phase_arg = band_wave[..., None] * wave_scale * frequency
    return jnp.concatenate([jnp.sin(phase_arg), jnp.cos(phase_arg)], axis=-1)


def bin_stats(total_sums, squares, counts, cell_count):
    scaled = jnp.maximum(counts * cell_count, 1.0)
    bin_mean = total_sums / scaled
    bin_var = squares / scaled - bin_mean * bin_mean
    return (bin_mean, bin_var)


def hypernet(params, wave_emb, live_band):
    (
        tokens_w,
        token_b,
        w_in,
        in_bias,
        w_proj,
        proj_bias,
        gain_pair,
        shifts,
        w_expand,
        expand_bias,
        w_reduce,
        reduce_bias,
    ) = params
    image_count = wave_emb.shape[0]
    band_slots = wave_emb.shape[1]
    model_width = wave_emb.shape[2]
    head_count = HHEADS
    head_size = model_width // head_count
    token_rows = tokens_w.shape[0]
    sequence = jnp.concatenate(
        [
            jnp.broadcast_to(tokens_w[None], (image_count, token_rows, model_width)),
            wave_emb,
            jnp.broadcast_to(token_b[None, None, :], (image_count, 1, model_width)),
        ],
        axis=1,
    )
    key_live = (
        jnp.concatenate(
            [
                jnp.ones((image_count, token_rows), jnp.float32),
                live_band,
                jnp.ones((image_count, 1), jnp.float32),
            ],
            axis=1,
        )
        > 0.5
    )
    projected = jnp.einsum("nsk,kj->nsj", sequence, w_in, precision=highest)
    query_heads = (projected[..., :model_width] + in_bias[0]).reshape(
        image_count, -1, head_count, head_size
    )
    keyed = projected[..., model_width : 2 * model_width].reshape(
        image_count, -1, head_count, head_size
    )
    valued = (projected[..., 2 * model_width :] + in_bias[1]).reshape(
        image_count, -1, head_count, head_size
    )
    scores = jnp.einsum("nqhd,nkhd->nhqk", query_heads, keyed, precision=highest) * head_size ** (
        -0.5
    )
    scores = jnp.where(key_live[:, None, None, :], scores, -1e30)
    attn_probs = jax.nn.softmax(scores, axis=-1)
    mixed_heads = jnp.einsum("nhqk,nkhd->nqhd", attn_probs, valued, precision=highest).reshape(
        image_count, -1, model_width
    )
    first_out = layer_norm(
        sequence + jnp.einsum("nsk,kj->nsj", mixed_heads, w_proj, precision=highest) + proj_bias,
        gain_pair[0],
        shifts[0],
        hyper_eps,
    )
    inner_act = jax.nn.gelu(
        jnp.einsum("nsk,kf->nsf", first_out, w_expand, precision=highest) + expand_bias,
        approximate=False,
    )
    second_out = layer_norm(
        first_out + jnp.einsum("nsf,fk->nsk", inner_act, w_reduce, precision=highest) + reduce_bias,
        gain_pair[1],
        shifts[1],
        hyper_eps,
    )
    return (
        second_out[:, token_rows : token_rows + band_slots] + wave_emb,
        second_out[:, token_rows + band_slots],
    )


def per_device(
    pixels,
    band_count,
    band_bin,
    bin_wave,
    run_mean,
    run_var,
    weight_tokens,
    bias_token,
    hyper_in,
    hyper_qv_bias,
    hyper_out,
    hyper_out_bias,
    hyper_gain,
    hyper_shift,
    hyper_up,
    hyper_up_bias,
    hyper_down,
    hyper_down_bias,
    kernel_weight,
    bias_weight,
    bias_offset,
    norm_gain,
    norm_shift,
    w_qkv,
    qv_bias,
    w_out,
    out_bias,
    w_up,
    up_bias,
    w_down,
    down_bias,
    cotangent,
):
    pixel_data = pixels[0]
    images, band_slots, patches, pixel_cells = pixel_data.shape
    bin_total = bin_wave.shape[0]
    model_width = w_qkv.shape[0]
    head_size = model_width // HEADS
    score_scale = head_size ** (-0.5)
    token_rows = images * patches
    live_band = (
        lax.broadcasted_iota(jnp.int32, (images, band_slots), 1) < band_count[0][:, None]
    ).astype(jnp.float32)
    bin_onehot = (
        band_bin[0][..., None]
        == lax.broadcasted_iota(jnp.int32, (images, band_slots, bin_total), 2)
    ).astype(jnp.float32)
    chosen = bin_onehot * live_band[..., None]
    values32 = pixel_data.astype(jnp.float32)
    band_total = jnp.sum(values32, axis=(2, 3))
    band_square = jnp.sum(values32 * values32, axis=(2, 3))
    total_sums, squares, counts = lax.psum(
        (
            jnp.einsum("ib,ibn->n", band_total, chosen, precision=highest),
            jnp.einsum("ib,ibn->n", band_square, chosen, precision=highest),
            jnp.sum(chosen, axis=(0, 1)),
        ),
        ("group", "batch"),
    )
    batch_mean, batch_var = bin_stats(total_sums, squares, counts, patches * pixel_cells)
    run_rstd = lax.rsqrt(run_var + stat_eps)
    band_mean = jnp.einsum("ibn,n->ib", chosen, run_mean, precision=highest)
    band_rstd = jnp.einsum("ibn,n->ib", chosen, run_rstd, precision=highest)
    normed = ((values32 - band_mean[:, :, None, None]) * band_rstd[:, :, None, None]).astype(
        jnp.bfloat16
    )
    band_wave = jnp.einsum("ibn,n->ib", bin_onehot, bin_wave, precision=highest)
    wave_emb = wave_embed(band_wave, hyper_in.shape[0])
    hyper_params = (
        weight_tokens,
        bias_token,
        hyper_in,
        hyper_qv_bias,
        hyper_out,
        hyper_out_bias,
        hyper_gain,
        hyper_shift,
        hyper_up,
        hyper_up_bias,
        hyper_down,
        hyper_down_bias,
    )
    (band_vec, bias_vec), hyper_back = jax.vjp(
        partial(hypernet, wave_emb=wave_emb, live_band=live_band), hyper_params
    )
    band_low = band_vec.astype(jnp.bfloat16)
    image_bias = jnp.dot(bias_vec, bias_weight, precision=highest) + bias_offset

    def kernel_piece(weight_rows):
        return jnp.einsum(
            "ibk,xek->ibxe", band_low, weight_rows, preferred_element_type=jnp.float32
        ).astype(jnp.bfloat16)

    embed_conv = jnp.einsum(
        "ibpx,ibxe->ipe",
        normed,
        kernel_piece(lax.all_gather(kernel_weight, "batch", axis=0, tiled=True)),
        preferred_element_type=jnp.float32,
    )
    embedded = embed_conv + image_bias[:, None, :]
    hat1, factor1 = norm_parts(embedded.reshape(token_rows, model_width), block_eps)
    normed1 = (hat1 * norm_gain[0] + norm_shift[0]).astype(jnp.bfloat16)
    joint_proj = jnp.dot(normed1, w_qkv, preferred_element_type=jnp.float32)
    query_heads = (
        (joint_proj[:, :model_width] + qv_bias[0])
        .astype(jnp.bfloat16)
        .reshape(images, patches, HEADS, head_size)
    )
    keyed = (
        joint_proj[:, model_width : 2 * model_width]
        .astype(jnp.bfloat16)
        .reshape(images, patches, HEADS, head_size)
    )
    valued = (
        (joint_proj[:, 2 * model_width :] + qv_bias[1])
        .astype(jnp.bfloat16)
        .reshape(images, patches, HEADS, head_size)
    )
    scores = (
        jnp.einsum("iqhd,ikhd->ihqk", query_heads, keyed, preferred_element_type=jnp.float32)
        * score_scale
    )
    row_top = jnp.max(scores, axis=-1, keepdims=True)
    log_total = row_top + jnp.log(jnp.sum(jnp.exp(scores - row_top), axis=-1, keepdims=True))
    attn_probs = jnp.exp(scores - log_total).astype(jnp.bfloat16)
    attended = (
        jnp.einsum("ihqk,ikhd->iqhd", attn_probs, valued, preferred_element_type=jnp.float32)
        .astype(jnp.bfloat16)
        .reshape(token_rows, model_width)
    )
    branch = jnp.dot(attended, w_out, preferred_element_type=jnp.float32) + out_bias
    residual = embedded.reshape(token_rows, model_width) + branch
    hat2, factor2 = norm_parts(residual, block_eps)
    normed2 = (hat2 * norm_gain[1] + norm_shift[1]).astype(jnp.bfloat16)
    pre_act = jnp.dot(normed2, w_up, preferred_element_type=jnp.float32) + up_bias
    gelu_out, gelu_back = jax.vjp(partial(jax.nn.gelu, approximate=False), pre_act)
    activated = gelu_out.astype(jnp.bfloat16)
    block_out = (
        (residual + jnp.dot(activated, w_down, preferred_element_type=jnp.float32) + down_bias)
        .astype(jnp.bfloat16)
        .reshape(1, images, patches, model_width)
    )
    grad_out = cotangent[0].reshape(token_rows, model_width)
    grad_w_down = jnp.einsum("rf,rd->fd", activated, grad_out, preferred_element_type=jnp.float32)
    grad_down_bias = jnp.sum(grad_out.astype(jnp.float32), axis=0)
    grad_act = jnp.einsum("rd,fd->rf", grad_out, w_down, preferred_element_type=jnp.float32)
    grad_pre = gelu_back(grad_act)[0].astype(jnp.bfloat16)
    grad_w_up = jnp.einsum("rd,rf->df", normed2, grad_pre, preferred_element_type=jnp.float32)
    grad_up_bias = jnp.sum(grad_pre.astype(jnp.float32), axis=0)
    grad_n2 = jnp.einsum("rf,df->rd", grad_pre, w_up, preferred_element_type=jnp.float32)
    grad_gain_two = jnp.sum(grad_n2 * hat2, axis=0)
    grad_shift_two = jnp.sum(grad_n2, axis=0)
    grad_resid = grad_out.astype(jnp.float32) + norm_back(grad_n2 * norm_gain[1], hat2, factor2)
    grad_branch = grad_resid.astype(jnp.bfloat16)
    grad_w_out = jnp.einsum("rd,re->de", attended, grad_branch, preferred_element_type=jnp.float32)
    grad_out_bias = jnp.sum(grad_branch.astype(jnp.float32), axis=0)
    grad_att = (
        jnp.einsum("re,de->rd", grad_branch, w_out, preferred_element_type=jnp.float32)
        .astype(jnp.bfloat16)
        .reshape(images, patches, HEADS, head_size)
    )
    again_scores = (
        jnp.einsum("iqhd,ikhd->ihqk", query_heads, keyed, preferred_element_type=jnp.float32)
        * score_scale
    )
    again_probs = jnp.exp(again_scores - log_total)
    grad_valued = jnp.einsum(
        "ihqk,iqhd->ikhd",
        again_probs.astype(jnp.bfloat16),
        grad_att,
        preferred_element_type=jnp.float32,
    ).astype(jnp.bfloat16)
    grad_probs = jnp.einsum("iqhd,ikhd->ihqk", grad_att, valued, preferred_element_type=jnp.float32)
    grad_scores = (
        again_probs * (grad_probs - jnp.sum(again_probs * grad_probs, axis=-1, keepdims=True))
    ).astype(jnp.bfloat16)
    grad_query = (
        jnp.einsum("ihqk,ikhd->iqhd", grad_scores, keyed, preferred_element_type=jnp.float32)
        * score_scale
    ).astype(jnp.bfloat16)
    grad_keyed = (
        jnp.einsum("ihqk,iqhd->ikhd", grad_scores, query_heads, preferred_element_type=jnp.float32)
        * score_scale
    ).astype(jnp.bfloat16)
    grad_joint = jnp.concatenate(
        [
            grad_query.reshape(token_rows, model_width),
            grad_keyed.reshape(token_rows, model_width),
            grad_valued.reshape(token_rows, model_width),
        ],
        axis=1,
    )
    grad_w_qkv = jnp.einsum("rd,rj->dj", normed1, grad_joint, preferred_element_type=jnp.float32)
    grad_qv_bias = jnp.stack(
        [
            jnp.sum(grad_query.reshape(token_rows, model_width).astype(jnp.float32), axis=0),
            jnp.sum(grad_valued.reshape(token_rows, model_width).astype(jnp.float32), axis=0),
        ]
    )
    grad_n1 = jnp.einsum("rj,dj->rd", grad_joint, w_qkv, preferred_element_type=jnp.float32)
    grad_gain_one = jnp.sum(grad_n1 * hat1, axis=0)
    grad_shift_one = jnp.sum(grad_n1, axis=0)
    grad_emb = (
        (grad_resid + norm_back(grad_n1 * norm_gain[0], hat1, factor1))
        .astype(jnp.bfloat16)
        .reshape(images, patches, model_width)
    )
    grad_kernels = jnp.einsum(
        "ibpx,ipe->ibxe", normed, grad_emb, preferred_element_type=jnp.float32
    ).astype(jnp.bfloat16)
    grad_image_bias = jnp.sum(grad_emb.astype(jnp.float32), axis=1)
    grad_bias_weight = jnp.einsum("ik,ie->ke", bias_vec, grad_image_bias, precision=highest)
    grad_bias_offset = jnp.sum(grad_image_bias, axis=0)
    grad_bias_vec = jnp.einsum("ie,ke->ik", grad_image_bias, bias_weight, precision=highest)
    weight_rows = lax.all_gather(kernel_weight, "batch", axis=0, tiled=True)
    grad_slab = grad_kernels
    grad_columns = jnp.einsum(
        "ipe,ibxe->ibpx", grad_emb, kernel_piece(weight_rows), preferred_element_type=jnp.float32
    )
    grad_vectors = jnp.einsum(
        "ibxe,xek->ibk", grad_slab, weight_rows, preferred_element_type=jnp.float32
    )
    grad_slab = grad_kernels
    kernel_share = lax.psum_scatter(
        jnp.einsum("ibxe,ibk->xek", grad_slab, band_low, preferred_element_type=jnp.float32),
        "batch",
        scatter_dimension=0,
        tiled=True,
    )
    kernel_total = lax.psum(kernel_share.astype(jnp.bfloat16), "group").astype(jnp.float32)
    hyper_grads = hyper_back((grad_vectors, grad_bias_vec))[0]
    row_share = (
        lax.psum_scatter(
            grad_w_qkv.astype(jnp.bfloat16), "group", scatter_dimension=0, tiled=True
        ).astype(jnp.float32),
        lax.psum_scatter(
            grad_w_out.astype(jnp.bfloat16), "group", scatter_dimension=0, tiled=True
        ).astype(jnp.float32),
        lax.psum_scatter(
            grad_w_up.astype(jnp.bfloat16), "group", scatter_dimension=0, tiled=True
        ).astype(jnp.float32),
        lax.psum_scatter(
            grad_w_down.astype(jnp.bfloat16), "group", scatter_dimension=0, tiled=True
        ).astype(jnp.float32),
    )
    block_sum = lax.psum((row_share[0], row_share[1], row_share[2], row_share[3]), "batch")
    reduced = lax.psum(
        (
            hyper_grads[0],
            hyper_grads[1],
            hyper_grads[2],
            hyper_grads[3],
            hyper_grads[4],
            hyper_grads[5],
            hyper_grads[6],
            hyper_grads[7],
            hyper_grads[8],
            hyper_grads[9],
            hyper_grads[10],
            hyper_grads[11],
            grad_bias_weight,
            grad_bias_offset,
            jnp.stack([grad_gain_one, grad_gain_two]),
            jnp.stack([grad_shift_one, grad_shift_two]),
            grad_qv_bias,
            grad_out_bias,
            grad_up_bias,
            grad_down_bias,
        ),
        ("group", "batch"),
    )
    pixel_grad = (grad_columns * band_rstd[:, :, None, None]).astype(jnp.bfloat16)[None]
    return (
        block_out,
        pixel_grad,
        batch_mean,
        batch_var,
        reduced[0],
        reduced[1],
        reduced[2],
        reduced[3],
        reduced[4],
        reduced[5],
        reduced[6],
        reduced[7],
        reduced[8],
        reduced[9],
        reduced[10],
        reduced[11],
        kernel_total,
        reduced[12],
        reduced[13],
        reduced[14],
        reduced[15],
        block_sum[0],
        reduced[16],
        block_sum[1],
        reduced[17],
        block_sum[2],
        reduced[18],
        block_sum[3],
        reduced[19],
    )


def solution(mesh):
    return jax.shard_map(
        per_device,
        mesh=mesh,
        in_specs=(
            P("group", "batch", None, None, None),
            P("group", "batch"),
            P("group", "batch", None),
            P(),
            P(),
            P(),
            P(),
            P(),
            P(),
            P(),
            P(),
            P(),
            P(),
            P(),
            P(),
            P(),
            P(),
            P(),
            P("batch", None, None),
            P(),
            P(),
            P(),
            P(),
            P(),
            P(),
            P(),
            P(),
            P(),
            P(),
            P(),
            P(),
            P("group", "batch", None, None),
        ),
        out_specs=(
            P("group", "batch", None, None),
            P("group", "batch", None, None, None),
            P(),
            P(),
            P(),
            P(),
            P(),
            P(),
            P(),
            P(),
            P(),
            P(),
            P(),
            P(),
            P(),
            P(),
            P("batch", None, None),
            P(),
            P(),
            P(),
            P(),
            P("group", None),
            P(),
            P("group", None),
            P(),
            P("group", None),
            P(),
            P("group", None),
            P(),
        ),
        check_vma=False,
    )
```

profile of v0, /device:TPU:0, one launch (start us, length us, event | category | flops | bytes accessed | tf_op | source)
XLA Modules:
  0.0 2215.8 jit_solution(2230966048599727095)
XLA Ops:
  42.0 10.9 fusion.26
  66.7 15.0 copy.188
  87.1 352.8 %all-gather.2.cloned.1.call-done = bf16[256,768,128]{2,1,0:T(8,128)(2,1)} async-done(((bf16[32,768,128]{2,1,0:T(8,128)(2,1)}), bf16[256,768,128]{2,1,0:T(8,128)(2,1)}) %all-gather.2.cloned.1.call-update) | async-done | bytes 50331664 | tf_op jit(solution)/shard_map/all_gather | solution.py:233
  439.9 32.2 %fusion.10 = bf16[4,16,256,768]{3,1,2,0:T(8,128)(2,1)} fusion(bf16[256,768,128]{2,1,0:T(8,128)(2,1)} %all-gather.2.cloned.1.call-done, bf16[4,16,128]{2,1,0:T(8,128)(2,1)} %fusion.111), kind=kOutput, calls=%fused_computation.15 | convolution fusion | flops 3233808384 | bytes 75513856 | tf_op jit(solution)/shard_map/ibk,xek->ibxe/dot_general | solution.py:226
  472.1 15.1 fusion.145
  560.0 27.9 %convert_reduce_fusion.1 = (f32[3072]{0:T(1024)}, bf16[784,3072]{1,0:T(8,128)(2,1)S(1)}, f32[784,3072]{1,0:T(8,128)}) fusion(f32[784,3072]{1,0:T(8,128)S(1)} %fusion.138, f32[3072]{0:T(1024)S(1)} %copy-done.121, bf16[784,768]{1,0:T(8,128)(2,1)S(1)} %copy-done.30, bf16[3072,768]{1,0:T(8,128)(2,1)S(1)} %bitcast.258), kind=kOutput, calls=%fused_computation.25 | convolution fusion | flops 3880006656 | bytes 30031872 | tf_op jit(solution)/shard_map/rd,fd->rf/dot_general | solution.py:282
  628.0 11.6 multiply_convert_fusion.1
  684.2 20.1 convolution_convert_fusion
  704.3 47.2 %convolution_bitcast_fusion = f32[256,768,128]{2,1,0:T(8,128)} fusion(bf16[4,16,256,768]{3,2,1,0:T(8,128)(2,1)} %convolution_convert_fusion, bf16[4,16,128]{2,1,0:T(8,128)(2,1)} %fusion.111), kind=kOutput, calls=%fused_computation.4 | convolution fusion | flops 3221225472 | bytes 125845504 | tf_op jit(solution)/shard_map/ibxe,ibk->xek/dot_general | solution.py:361
  756.1 9.3 convolution_convert_fusion.3
  765.7 11.3 multiply_convert_fusion.2
  777.0 8.9 convolution_convert_fusion.1
  786.0 9.9 convolution_convert_fusion.2
  808.7 9.5 add_convert_fusion.2
  829.6 18.0 fusion.32
  852.9 31.8 %fusion.50 = f32[4,16,128]{2,1,0:T(8,128)} fusion(bf16[256,768,128]{2,1,0:T(8,128)(2,1)} %all-gather.2.cloned.1.call-done, bf16[4,16,256,768]{3,2,1,0:T(8,128)(2,1)} %convolution_convert_fusion), kind=kOutput, calls=%fused_computation.128 | convolution fusion | flops 3221225472 | bytes 75530240 | tf_op jit(solution)/shard_map/ibxe,xek->ibk/dot_general | solution.py:356
  888.9 816.0 %reduce-scatter.16.cloned.1.call-done = f32[32,768,128]{2,1,0:T(8,128)} async-done(((f32[256,768,128]{2,1,0:T(8,128)}), f32[32,768,128]{2,1,0:T(8,128)}) %reduce-scatter.16.cloned.1.call-update) | async-done | bytes 12582928
  1713.3 10.3 fusion.147
  1785.2 14.0 convolution_bitcast_fusion.1
  1802.3 40.4 %all-reduce.12 = (f32[512]{0:T(512)S(1)}, f32[512]{0:T(512)}, f32[512]{0:T(512)}, f32[128]{0:T(128)}, f32[2,128]{1,0:T(2,128)}, /*index=5*/f32[128]{0:T(128)}, f...) all-reduce(f32[512]{0:T(512)} %bitcast.250, ...), channel_id=1, replica_groups=mesh['group'=4,'batch'=8] {'group','batch'}, use_global_device_ids=true, to_apply=%region_18.19 | all-reduce | flops 14720 | bytes 117760 | tf_op jit(solution)/shard_map/psum | solution.py:188
  1846.9 60.2 %reduce-scatter.12.cloned.1.call-done = bf16[192,3072]{1,0:T(8,128)(2,1)} async-done(((bf16[768,3072]{1,0:T(8,128)(2,1)}), bf16[192,3072]{1,0:T(8,128)(2,1)}) %reduce-scatter.12.cloned.1.call-update) | async-done | bytes 1179664 | tf_op jit(solution)/shard_map/reduce_scatter | solution.py:375
  1907.2 144.1 %all-reduce.22 = (f32[192,2304]{1,0:T(8,128)}, f32[192,768]{1,0:T(8,128)}, f32[192,3072]{1,0:T(8,128)}, f32[768,768]{1,0:T(8,128)}) all-reduce(bf16[192,2304]{1,0:T(8,128)(2,1)} %reduce-scatter.8.cloned.1.call-done, bf16[192,768]{1,0:T(8,128)(2,1)} %reduce-scatter.10.cloned.1.call-done, ...), channel_id=1, replica_groups=mesh['group'=4,'batch'=8] {'batch'}, use_global_device_ids=true, to_apply=%region_64.65 | all-reduce | flops 1769472 | bytes 10616832 | tf_op jit(solution)/shard_map/psum | solution.py:382
  2051.3 9.1 convert_element_type.186
  2060.3 138.5 %all-reduce.21.cloned.1.call-done = (f32[128,128]{1,0:T(8,128)}, f32[128,384]{1,0:T(8,128)}, f32[128,128]{1,0:T(8,128)}, f32[128,2048]{1,0:T(8,128)}, f32[2048,128]{1,0:T(8,128)}, /*index=5*/f32[128,768]{1,0:T(8,128)}) async-done(((f32[128,128]{1,0:T(8,128)}, f32[128,384]{1,0:T(8,128)}, f32[128,128]{1,0:T(8,128)}, f32[128,2048]{1,0:T(8,128)}, f32[2048,128]{1,0:T(8,128)}, /*index=5*/f32[128,768]{1,0:T(8,128)}), ...) | async-done | bytes 2818064 | tf_op jit(solution)/shard_map/psum | solution.py:383
  (469 shorter events, 335.6 us)
Async XLA Ops:
  7.2 488.9 %copy-start = (bf16[768,2304]{1,0:T(8,128)(2,1)S(1)}, bf16[768,2304]{1,0:T(8,128)(2,1)}, u32[]{:S(2)}) copy-start(bf16[768,2304]{1,0:T(8,128)(2,1)} %param.55) | copy-start | bytes 10616836
  7.2 432.6 %all-gather.2.cloned.1.call-start = ((), (), s32[]{:S(2)}) async-start(), calls=%async_computation.5 | async-start | bytes 56623104 | tf_op jit(solution)/shard_map/all_gather | solution.py:233
  8.0 1696.9 %reduce-scatter.16.cloned.1.call-start = ((), (), s32[]{:S(2)}) async-start(), calls=%async_computation.11 | async-start | bytes 113246208
  10.3 23.9 %copy-start.101 = (f32[4,1,128]{2,1,0:T(1,128)}, f32[4,1,128]{2,1,0:T(1,128)S(1)}, u32[]{:S(2)}) copy-start(f32[4,1,128]{2,1,0:T(1,128)S(1)} %broadcast_in_dim.50) | copy-start | bytes 6148
  27.3 32.8 %copy-start.104 = (f32[4,16]{1,0:T(4,128)}, f32[4,16]{1,0:T(4,128)S(1)}, u32[]{:S(2)}) copy-start(f32[4,16]{1,0:T(4,128)S(1)} %fusion.116) | copy-start | bytes 772
  59.4 25.8 %copy-start.102 = (f32[4,1,128]{2,1,0:T(1,128)}, f32[4,1,128]{2,1,0:T(1,128)S(1)}, u32[]{:S(2)}) copy-start(f32[4,1,128]{2,1,0:T(1,128)S(1)} %slice.87) | copy-start | bytes 6148
  83.7 412.4 %copy-start.108 = (f32[768]{0:T(1024)}, f32[768]{0:T(1024)S(1)}, u32[]{:S(2)}) copy-start(f32[768]{0:T(1024)S(1)} %get-tuple-element.252) | copy-start | bytes 9220
  83.7 469.7 %copy-start.106 = (f32[768]{0:T(1024)}, f32[768]{0:T(1024)S(1)}, u32[]{:S(2)}) copy-start(f32[768]{0:T(1024)S(1)} %get-tuple-element.253) | copy-start | bytes 9220
  560.0 28.0 %copy-start.20 = (f32[784,3072]{1,0:T(8,128)}, f32[784,3072]{1,0:T(8,128)S(1)}, u32[]{:S(2)}) copy-start(f32[784,3072]{1,0:T(8,128)S(1)} %fusion.138) | copy-start | bytes 28901380
  560.0 28.0 %copy-start.107 = (f32[768]{0:T(1024)S(1)}, f32[768]{0:T(1024)}, u32[]{:S(2)}) copy-start(f32[768]{0:T(1024)} %copy-done.106) | copy-start | bytes 9220
  560.0 28.0 %copy-start.137 = (bf16[768,3072]{1,0:T(8,128)(2,1)S(1)}, bf16[768,3072]{1,0:T(8,128)(2,1)}, u32[]{:S(2)}) copy-start(bf16[768,3072]{1,0:T(8,128)(2,1)} %param.59) | copy-start | bytes 14155780
  751.5 1092.6 %reduce-scatter.10.cloned.1.call-start = ((), (), s32[]{:S(2)}) async-start(), calls=%async_computation.8 | async-start | bytes 1474560 | tf_op jit(solution)/shard_map/reduce_scatter | solution.py:372
  756.1 1088.0 %reduce-scatter.8.cloned.1.call-start = ((), (), s32[]{:S(2)}) async-start(), calls=%async_computation.7 | async-start | bytes 4423680 | tf_op jit(solution)/shard_map/reduce_scatter | solution.py:369
  765.4 1081.5 %reduce-scatter.14.cloned.1.call-start = ((), (), s32[]{:S(2)}) async-start(), calls=%async_computation.10 | async-start | bytes 5898240 | tf_op jit(solution)/shard_map/reduce_scatter | solution.py:378
  785.9 1121.2 %reduce-scatter.12.cloned.1.call-start = ((), (), s32[]{:S(2)}) async-start(), calls=%async_computation.9 | async-start | bytes 5898240 | tf_op jit(solution)/shard_map/reduce_scatter | solution.py:375
  795.9 1255.4 %all-reduce.19.cloned.1.call-start = ((), (), s32[]{:S(2)}) async-start(), calls=%async_computation.6 | async-start | bytes 12582912 | tf_op jit(solution)/shard_map/psum | solution.py:366
  852.9 860.3 %copy-start.81 = (f32[4,128]{1,0:T(4,128)}, f32[4,128]{1,0:T(4,128)S(1)}, u32[]{:S(2)}) copy-start(f32[4,128]{1,0:T(4,128)S(1)} %fusion.148) | copy-start | bytes 6148
  852.9 31.8 %copy-start.58 = (f32[4,145]{1,0:T(4,128)S(1)}, f32[4,145]{1,0:T(4,128)}, u32[]{:S(2)}) copy-start(f32[4,145]{1,0:T(4,128)} %copy-done.57) | copy-start | bytes 6964
  852.9 31.8 %copy-start.98 = (f32[128]{0:T(128)S(1)}, f32[128]{0:T(128)}, u32[]{:S(2)}) copy-start(f32[128]{0:T(128)} %copy-done.97) | copy-start | bytes 1540
  852.9 33.8 %copy-start.66 = (f32[4,145]{1,0:T(4,128)S(1)}, f32[4,145]{1,0:T(4,128)}, u32[]{:S(2)}) copy-start(f32[4,145]{1,0:T(4,128)} %copy-done.65) | copy-start | bytes 6964
  886.8 826.4 %copy-start.76 = (f32[4,145]{1,0:T(4,128)}, f32[4,145]{1,0:T(4,128)S(1)}, u32[]{:S(2)}) copy-start(f32[4,145]{1,0:T(4,128)S(1)} %multiply_multiply_fusion.18) | copy-start | bytes 6964
  1713.1 485.8 %all-reduce.21.cloned.1.call-start = ((), (), s32[]{:S(2)}) async-start(), calls=%async_computation.12 | async-start | bytes 5636096 | tf_op jit(solution)/shard_map/psum | solution.py:383
  1747.0 23.9 %copy-start.75 = (f32[4,145]{1,0:T(4,128)S(1)}, f32[4,145]{1,0:T(4,128)}, u32[]{:S(2)}) copy-start(f32[4,145]{1,0:T(4,128)} %copy-done.74) | copy-start | bytes 6964
  1752.3 26.2 %copy-start.71 = (f32[4,145]{1,0:T(4,128)S(1)}, f32[4,145]{1,0:T(4,128)}, u32[]{:S(2)}) copy-start(f32[4,145]{1,0:T(4,128)} %copy-done.69) | copy-start | bytes 6964
  (130 other events, 1016.8 us)
Sparse Core Ops, SparseCore 0:
  9.7 430.0 all-gather.1
  751.6 953.1 reduce-scatter.15
  1708.0 26.8 reduce-scatter.9
  1738.2 47.2 reduce-scatter.7
  1788.5 58.3 reduce-scatter.13
  1850.1 57.0 reduce-scatter.11
  1911.4 138.4 all-reduce.18
  2059.2 139.6 all-reduce.20
where the time goes:
time: 2220 us
  waiting for transfers between devices  1370 us (62%)
  matrix products  386 us (17%)
  blocking collectives  185 us (8%)
  local copies, waits for them, and re-layouts  154 us (7%)
  other arithmetic  102 us (5%)
    unnamed x9, waiting for transfers between devices  817 us
    all_gather x1, waiting for transfers between devices, per_device(): lax.all_gather(kernel_weight, 'batch', axis=0, tiled=True)  353 us
    psum x1, blocking collectives, per_device(): lax.psum((row_share[0], row_share[1], row_share[2], row_share[3]), 'batch')  144 us
    psum x1, waiting for transfers between devices, per_device(): lax.psum((hyper_grads[0], hyper_grads[1], hyper_grads[2], hyper_grads[3],...  139 us
    reduce_scatter x1, waiting for transfers between devices, per_device(): lax.psum_scatter(grad_w_up.astype(jnp.bfloat16), 'group', scatter_dimensi...  60.2 us
    dot_general x1, matrix products, per_device(): jnp.einsum('ibxe,ibk->xek', grad_slab, band_low, preferred_element_type=j...  47.2 us
  transfers between devices with their start and end apart: 8, of which 5 were waited for; matrix products, arithmetic and copies ran while one was open for 14% of the time, Pallas kernels for 0%

commit v1 on v0

v1 whole, which is shorter than its diff:
```python
from functools import partial

import jax
import jax.numpy as jnp
from jax import lax
from jax.experimental import pallas as pl
from jax.experimental.pallas import tpu as pltpu
from jax.sharding import PartitionSpec as P

HEADS = 12
HHEADS = 4


highest = lax.Precision.HIGHEST
high = lax.Precision.HIGH
stat_eps = 1e-05
hyper_eps = 1e-05
block_eps = 1e-06
wave_scale = 1000.0


def layer_norm(values, gain, shift, epsilon):
    center = values - jnp.mean(values, axis=-1, keepdims=True)
    return (
        center * lax.rsqrt(jnp.mean(center * center, axis=-1, keepdims=True) + epsilon) * gain
        + shift
    )


def norm_parts(values, epsilon):
    center = values - jnp.mean(values, axis=-1, keepdims=True)
    factor = lax.rsqrt(jnp.mean(center * center, axis=-1, keepdims=True) + epsilon)
    return (center * factor, factor)


def norm_back(grad_hat, normal_hat, factor):
    return factor * (
        grad_hat
        - jnp.mean(grad_hat, axis=-1, keepdims=True)
        - normal_hat * jnp.mean(grad_hat * normal_hat, axis=-1, keepdims=True)
    )


def wave_embed(band_wave, model_width):
    half_width = model_width // 2
    ladder = jnp.arange(half_width, dtype=jnp.float32) / half_width
    frequency = 1.0 / 10000.0**ladder
    phase_arg = band_wave[..., None] * wave_scale * frequency
    return jnp.concatenate([jnp.sin(phase_arg), jnp.cos(phase_arg)], axis=-1)


def bin_stats(total_sums, squares, counts, cell_count):
    scaled = jnp.maximum(counts * cell_count, 1.0)
    bin_mean = total_sums / scaled
    bin_var = squares / scaled - bin_mean * bin_mean
    return (bin_mean, bin_var)


def hypernet(params, wave_emb, live_band):
    (
        tokens_w,
        token_b,
        w_in,
        in_bias,
        w_proj,
        proj_bias,
        gain_pair,
        shifts,
        w_expand,
        expand_bias,
        w_reduce,
        reduce_bias,
    ) = params
    image_count = wave_emb.shape[0]
    band_slots = wave_emb.shape[1]
    model_width = wave_emb.shape[2]
    head_count = HHEADS
    head_size = model_width // head_count
    token_rows = tokens_w.shape[0]
    sequence = jnp.concatenate(
        [
            jnp.broadcast_to(tokens_w[None], (image_count, token_rows, model_width)),
            wave_emb,
            jnp.broadcast_to(token_b[None, None, :], (image_count, 1, model_width)),
        ],
        axis=1,
    )
    key_live = (
        jnp.concatenate(
            [
                jnp.ones((image_count, token_rows), jnp.float32),
                live_band,
                jnp.ones((image_count, 1), jnp.float32),
            ],
            axis=1,
        )
        > 0.5
    )
    projected = jnp.einsum("nsk,kj->nsj", sequence, w_in, precision=high)
    query_heads = (projected[..., :model_width] + in_bias[0]).reshape(
        image_count, -1, head_count, head_size
    )
    keyed = projected[..., model_width : 2 * model_width].reshape(
        image_count, -1, head_count, head_size
    )
    valued = (projected[..., 2 * model_width :] + in_bias[1]).reshape(
        image_count, -1, head_count, head_size
    )
    scores = jnp.einsum("nqhd,nkhd->nhqk", query_heads, keyed, precision=high) * head_size ** (
        -0.5
    )
    scores = jnp.where(key_live[:, None, None, :], scores, -1e30)
    attn_probs = jax.nn.softmax(scores, axis=-1)
    mixed_heads = jnp.einsum("nhqk,nkhd->nqhd", attn_probs, valued, precision=high).reshape(
        image_count, -1, model_width
    )
    first_out = layer_norm(
        sequence + jnp.einsum("nsk,kj->nsj", mixed_heads, w_proj, precision=high) + proj_bias,
        gain_pair[0],
        shifts[0],
        hyper_eps,
    )
    inner_act = jax.nn.gelu(
        jnp.einsum("nsk,kf->nsf", first_out, w_expand, precision=high) + expand_bias,
        approximate=False,
    )
    second_out = layer_norm(
        first_out + jnp.einsum("nsf,fk->nsk", inner_act, w_reduce, precision=high) + reduce_bias,
        gain_pair[1],
        shifts[1],
        hyper_eps,
    )
    return (
        second_out[:, token_rows : token_rows + band_slots] + wave_emb,
        second_out[:, token_rows + band_slots],
    )


def swap_group(value, bits):
    return lax.ppermute(value, "group", [(at, at ^ bits) for at in range(4)])


def swap_batch(value, bits):
    count = lax.axis_size("batch")
    return lax.ppermute(value, "batch", [(at, at ^ bits) for at in range(count)])


def tuned_mesh():
    return lax.axis_size("group") == 4 and lax.axis_size("batch") == 8


def same_core():
    count = lax.axis_size("batch")
    return [list(range(0, count, 2)), list(range(1, count, 2))]


def in_order(bit, first, second):
    return jnp.where(
        bit == 0, jnp.concatenate([first, second]), jnp.concatenate([second, first])
    )


def four_in_order(index, pieces):
    low, high = (index & 1, index >> 1)
    return in_order(
        high, in_order(low, pieces[0], pieces[1]), in_order(low, pieces[2], pieces[3])
    )


def part_of(value, index, parts):
    rows = value.shape[0] // parts
    return lax.dynamic_slice_in_dim(value, index * rows, rows)


def tie(*values):
    return lax.optimization_barrier(values)


def along_line(value, step):
    count = lax.axis_size("batch")
    pairs = [(at, at + 2 * step) for at in range(count) if 0 <= at + 2 * step < count]
    return lax.ppermute(value, "batch", pairs)


def of_chip(chip, values):
    return jnp.array(values, jnp.int32)[chip]


def plain_weight_pieces(weight):
    core = lax.axis_index("batch") & 1
    shards = lax.all_gather(weight, "batch", axis=0)
    shards = shards.reshape((-1, 2) + weight.shape)
    mine = lax.dynamic_index_in_dim(shards, core, 1, keepdims=False)
    return mine.reshape((4, -1) + weight.shape[1:])


def plain_line_cells(pixels):
    pieces, images, rows, lanes = pixels.shape
    chips = lax.axis_size("batch") // 2
    parts = pixels.reshape(pieces, images, rows, chips // pieces, -1)
    parts = parts.transpose(0, 3, 1, 2, 4).reshape(chips, images, rows, -1)
    came = lax.all_to_all(parts, "batch", 0, 0, axis_index_groups=same_core(), tiled=True)
    return [came.reshape((chips * images,) + came.shape[2:])]


def plain_line_images(value, beside):
    both = jnp.concatenate([value, beside])
    return [lax.all_gather(both, "batch", axis=0, axis_index_groups=same_core(), tiled=True)]


def line_rows(low):
    if not tuned_mesh():
        return lax.all_gather(low, "batch", axis=0, axis_index_groups=same_core(), tiled=True)
    return jnp.concatenate([low] + [swap_batch(low, 2 * hop) for hop in (1, 2, 3)])


def core_sum(grad):
    core = lax.axis_index("batch") & 1
    split = grad.reshape(4, 2, -1, grad.shape[1])
    keep = lax.dynamic_index_in_dim(split, core, 1, keepdims=False)
    send = lax.dynamic_index_in_dim(split, 1 - core, 1, keepdims=False)
    came = swap_batch(send, 1)
    return (
        (keep.astype(jnp.float32) + came.astype(jnp.float32))
        .astype(jnp.bfloat16)
        .reshape(-1, grad.shape[1])
    )


def row_share(half):
    return lax.psum_scatter(half, "group", scatter_dimension=0, tiled=True)


def row_mine(share):
    return lax.psum(share, "batch", axis_index_groups=same_core())


def row_both(mine):
    core = lax.axis_index("batch") & 1
    return in_order(core, mine, swap_batch(mine, 1)).astype(jnp.float32)


def add_low(left, right):
    return (left.astype(jnp.float32) + right.astype(jnp.float32)).astype(left.dtype)


def ring_sides():
    group = lax.axis_index("group")
    side, level = (group & 1, group >> 1)
    return (1, side), (2, level)


def sum_out(parts, flip):
    order = ring_sides()[::-1] if flip else ring_sides()
    return [swap_group(part_of(part, 1 - bit, 2), way) for part, (way, bit) in zip(parts, order)]


def sum_in(parts, came, flip):
    order = ring_sides()[::-1] if flip else ring_sides()
    return [
        add_low(part_of(part, bit, 2), other)
        for part, other, (way, bit) in zip(parts, came, order)
    ]


def share_out(parts, flip):
    order = ring_sides()[::-1] if flip else ring_sides()
    return [swap_group(part, way) for part, (way, bit) in zip(parts, order)]


def share_in(parts, came, flip):
    order = ring_sides()[::-1] if flip else ring_sides()
    return [in_order(bit, part, other) for part, other, (way, bit) in zip(parts, came, order)]


def block_rows(value):
    rows, lanes = value.shape
    return value.reshape(rows, lanes // 128, 128).transpose(1, 0, 2).reshape(-1, 128)


def unblock_rows(value, rows):
    return value.reshape(-1, rows, 128).transpose(1, 0, 2).reshape(rows, -1)


def grid_params(mebibytes, semantics=1):
    return pltpu.CompilerParams(
        dimension_semantics=("arbitrary",) * semantics,
        vmem_limit_bytes=mebibytes * 1024 * 1024,
    )


def dot_nn(left, right):
    return lax.dot_general(
        left, right, (((1,), (0,)), ((), ())), preferred_element_type=jnp.float32
    )


def dot_nt(left, right):
    return lax.dot_general(
        left, right, (((1,), (1,)), ((), ())), preferred_element_type=jnp.float32
    )


def dot_tn(left, right):
    return lax.dot_general(
        left, right, (((0,), (0,)), ((), ())), preferred_element_type=jnp.float32
    )


def split_kernel(cells, core_ref, pixel_ref, mean_ref, rate_ref, *refs):
    out_refs, scratch = (refs[:2], refs[2:])
    patches, bands, lanes = pixel_ref.shape[1:]
    pieces, _, rows, _ = out_refs[0].shape
    share = lanes // (2 * pieces * cells)
    span = cells * bands
    tile = 128
    columns, tiles = (lanes // tile, -(-rows // tile))
    flat, turned = (scratch[:columns], scratch[columns:])
    values = (pixel_ref[0].astype(jnp.float32) - mean_ref[0]) * rate_ref[0]
    values = values.astype(jnp.bfloat16).astype(jnp.float32).reshape(patches * bands, lanes)
    for column in range(columns):
        flat[column][: patches * bands] = values[:, column * tile : (column + 1) * tile]
        flat[column][patches * bands :] = jnp.zeros(
            (flat[column].shape[0] - patches * bands, tile), jnp.float32
        )
    for band in range(bands):
        for column in range(columns):
            for at in range(tiles):
                block = flat[column][pl.ds(at * tile * bands + band, tile, stride=bands), :]
                turned[at][pl.ds(column * tile * bands + band, tile, stride=bands), :] = block.T
    for out_ref, side in zip(out_refs, (core_ref[0], 1 - core_ref[0])):
        for piece in range(pieces):
            for at in range(tiles):
                count = min(tile, rows - at * tile)
                parts = []
                for one in range(share):
                    first = ((piece * share + one) * 2 + side) * span
                    place = pl.ds(pl.multiple_of(first, span), span)
                    parts.append(turned[at][place, :].T[:count])
                block = parts[0] if share == 1 else jnp.concatenate(parts, axis=1)
                out_ref[piece, 0, at * tile : at * tile + count, :] = block.astype(jnp.bfloat16)


def turn_scratch(rows, bands, lanes):
    tiles = -(-rows // 128)
    return [pltpu.VMEM((tiles * 128 * bands, 128), jnp.float32)] * (lanes // 128) + [
        pltpu.VMEM((lanes * bands, 128), jnp.float32)
    ] * tiles


def split_pixels(pixels, means, rates, core, rows, cells):
    images, bands, patches, lanes = pixels.shape
    wide = bands * lanes // 8
    side = jax.ShapeDtypeStruct((4, images, rows, wide), jnp.bfloat16)
    return pl.pallas_call(
        partial(split_kernel, cells),
        grid_spec=pltpu.PrefetchScalarGridSpec(
            num_scalar_prefetch=1,
            grid=(images,),
            in_specs=[
                pl.BlockSpec((1, patches, bands, lanes), lambda i, core: (i, 0, 0, 0)),
                pl.BlockSpec((1, bands, 1), lambda i, core: (i, 0, 0)),
                pl.BlockSpec((1, bands, 1), lambda i, core: (i, 0, 0)),
            ],
            out_specs=[pl.BlockSpec((4, 1, rows, wide), lambda i, core: (0, i, 0, 0))] * 2,
            scratch_shapes=turn_scratch(rows, bands, lanes),
        ),
        out_shape=[side, side],
        compiler_params=grid_params(40),
        cost_estimate=pl.CostEstimate(flops=1, bytes_accessed=1, transcendentals=0),
        name="split_pixels",
    )(core.reshape(1), pixels.transpose(0, 2, 1, 3), means[:, :, None], rates[:, :, None])


def join_kernel(cells, patches, core_ref, mine_ref, other_ref, out_ref, *scratch):
    rows = mine_ref.shape[2]
    bands, lanes = out_ref.shape[2:]
    pieces = mine_ref.shape[0]
    share = lanes // (2 * pieces * cells)
    span = cells * bands
    tile = 128
    columns, tiles = (lanes // tile, -(-rows // tile))
    flat, turned = (scratch[:columns], scratch[columns:])
    core = core_ref[0]
    for piece in range(pieces):
        for ref, flip in ((mine_ref, core), (other_ref, 1 - core)):
            for one in range(share):
                first = ((piece * share + one) * 2 + flip) * span
                place = pl.ds(pl.multiple_of(first, span), span)
                for at in range(tiles):
                    count = min(tile, rows - at * tile)
                    block = ref[
                        piece, 0, at * tile : at * tile + count, one * span : (one + 1) * span
                    ].astype(jnp.float32)
                    if count < tile:
                        block = jnp.concatenate(
                            [block, jnp.zeros((tile - count, span), jnp.float32)]
                        )
                    turned[at][place, :] = block.T
    for band in range(bands):
        for column in range(columns):
            for at in range(tiles):
                block = turned[at][pl.ds(column * tile * bands + band, tile, stride=bands), :]
                flat[column][pl.ds(at * tile * bands + band, tile, stride=bands), :] = block.T
    for column in range(columns):
        out_ref[0, :, :, column * tile : (column + 1) * tile] = (
            flat[column][: patches * bands].reshape(patches, bands, tile).astype(jnp.bfloat16)
        )


def join_pixels(mine, other, core, patches, cells, lanes, bands):
    pieces, images, rows, wide = mine.shape
    block = pl.BlockSpec((pieces, 1, rows, wide), lambda i, core: (0, i, 0, 0))
    joined = pl.pallas_call(
        partial(join_kernel, cells, patches),
        grid_spec=pltpu.PrefetchScalarGridSpec(
            num_scalar_prefetch=1,
            grid=(images,),
            in_specs=[block, block],
            out_specs=pl.BlockSpec((1, patches, bands, lanes), lambda i, core: (i, 0, 0, 0)),
            scratch_shapes=turn_scratch(rows, bands, lanes),
        ),
        out_shape=jax.ShapeDtypeStruct((images, patches, bands, lanes), jnp.bfloat16),
        compiler_params=grid_params(40),
        cost_estimate=pl.CostEstimate(flops=1, bytes_accessed=1, transcendentals=0),
        name="join_pixels",
    )(core.reshape(1), mine, other)
    return joined.transpose(0, 2, 1, 3)


def embed_kernel(first, count, at_ref, low_ref, *refs):
    weight_refs, pixel_refs = refs[:count], refs[count : count + 2]
    if first:
        total_ref, kernel_ref, weight_now = refs[count + 2 :]
    else:
        before_ref, _, total_ref, kernel_ref, weight_now = refs[count + 2 :]
    share = pixel_refs[0].shape[1]
    images = 2 * share
    cells = weight_now.shape[0]
    bands = pixel_refs[0].shape[3] // cells

    @pl.when(pl.program_id(0) == 0)
    def _():
        if first:
            total_ref[...] = jnp.zeros_like(total_ref)
        else:
            total_ref[...] = before_ref[...]

    for at in range(count):

        @pl.when((pl.program_id(0) == at) | (count == 1))
        def _(at=at):
            weight_now[...] = weight_refs[at][...]

    low = low_ref[...]
    for cell in range(cells):
        made = dot_nt(low, weight_now[cell]).astype(jnp.bfloat16)
        for image in range(images):
            kernel_ref[0, image, cell * bands : (cell + 1) * bands, :] = made[
                image * bands : (image + 1) * bands
            ]
    for image in range(images):
        block = pixel_refs[image // share][0, image % share]
        total_ref[image] += dot_nn(block, kernel_ref[0, image])


def embed_piece(place, low, weights, pixels, total, kernels):
    pieces, share, rows, lanes = pixels[0].shape
    images = 2 * share
    cells, width, depth = weights[0].shape
    step = lanes // (4 * 16)
    count = len(weights)
    steps = max(count, cells // step)
    bands = lanes // (4 * step)
    first = total is None
    any_spec = pl.BlockSpec(memory_space=pl.ANY)
    whole_total = pl.BlockSpec((images, rows, width), lambda t, at: (0, 0, 0))
    if count == 1:
        weight_specs = [pl.BlockSpec((step, width, depth), lambda t, at: (t, 0, 0))]
    else:
        weight_specs = [pl.BlockSpec((step, width, depth), lambda t, at: (0, 0, 0))] * count
    return pl.pallas_call(
        partial(embed_kernel, first, count),
        grid_spec=pltpu.PrefetchScalarGridSpec(
            num_scalar_prefetch=1,
            grid=(steps,),
            in_specs=[pl.BlockSpec(low.shape, lambda t, at: (0, 0))]
            + weight_specs
            + [
                pl.BlockSpec(
                    (1, share, rows, step * bands), lambda t, at: (at[0], 0, 0, at[1 + t])
                ),
            ]
            * 2
            + ([] if first else [whole_total, any_spec]),
            out_specs=[
                whole_total,
                pl.BlockSpec(
                    (1, images, step * bands, width), lambda t, at: (at[0], 0, at[1 + t], 0)
                ),
            ],
            scratch_shapes=[pltpu.VMEM((step, width, depth), jnp.bfloat16)],
        ),
        out_shape=[
            jax.ShapeDtypeStruct((images, rows, width), jnp.float32),
            jax.ShapeDtypeStruct((pieces, images, lanes, width), jnp.bfloat16),
        ],
        input_output_aliases={} if first else {4 + count: 0, 5 + count: 1},
        compiler_params=grid_params(48),
        cost_estimate=pl.CostEstimate(flops=1, bytes_accessed=1, transcendentals=0),
        name="embed_piece",
    )(place, low, *weights, *pixels, *(() if first else (total, kernels)))


def pixel_grad_kernel(grad_ref, kernel_ref, rate_ref, out_ref):
    for image in range(grad_ref.shape[0]):
        out_ref[0, image] = (
            dot_nt(grad_ref[image], kernel_ref[0, image]) * rate_ref[image]
        ).astype(jnp.bfloat16)


def pixel_grads(grads, kernels, rates):
    pieces, images, lanes, width = kernels.shape
    rows = grads.shape[1]
    share = images // 2
    return pl.pallas_call(
        pixel_grad_kernel,
        grid=(2, pieces),
        in_specs=[
            pl.BlockSpec((share, rows, width), lambda i, j: (i, 0, 0)),
            pl.BlockSpec((1, share, lanes, width), lambda i, j: (j, i, 0, 0)),
            pl.BlockSpec((share, 1, lanes), lambda i, j: (i, 0, 0)),
        ],
        out_specs=pl.BlockSpec((1, share, rows, lanes), lambda i, j: (j, i, 0, 0)),
        out_shape=jax.ShapeDtypeStruct((pieces, images, rows, lanes), jnp.bfloat16),
        compiler_params=grid_params(40, 2),
        cost_estimate=pl.CostEstimate(flops=1, bytes_accessed=1, transcendentals=0),
        name="pixel_grads",
    )(grads, kernels, rates)


def line_kernel(half, halves, low_ref, pixel_refs, grad_refs, out_ref, made):
    cells = out_ref.shape[0]
    lanes = pixel_refs[0].shape[2] // halves
    bands = lanes // cells
    columns = slice(half * lanes, (half + 1) * lanes)
    image = 0
    for pixel_ref, grad_ref in zip(pixel_refs, grad_refs):
        count = pixel_ref.shape[0]

        @pl.loop(0, count, unroll=count if count <= 4 else 2)
        def _(at, image=image):
            grads = dot_tn(pixel_ref[at, :, columns], grad_ref[at]).astype(jnp.bfloat16)
            row = pl.multiple_of((image + at) * bands, bands)
            for cell in range(cells):
                made[cell, pl.ds(row, bands), :] = grads[cell * bands : (cell + 1) * bands]

        image += count

    @pl.loop(0, cells, unroll=4)
    def _(cell):
        out_ref[cell] = dot_nn(low_ref[...], made[cell]).T.astype(jnp.bfloat16)


def line_grads(low_turned, cells, pixels, grads, half, halves):
    step_cells = cells // halves
    depth = low_turned.shape[0]
    width = grads[0].shape[2]
    bands = pixels[0].shape[2] // cells
    images = sum(piece.shape[0] for piece in pixels)
    vmem = pl.BlockSpec(memory_space=pltpu.VMEM)

    def body(*refs):
        pixel_refs = refs[1 : 1 + len(pixels)]
        grad_refs = refs[1 + len(pixels) : 1 + 2 * len(pixels)]
        line_kernel(half, halves, refs[0], pixel_refs, grad_refs, *refs[-2:])

    return pl.pallas_call(
        body,
        in_specs=[vmem] * (1 + 2 * len(pixels)),
        out_specs=vmem,
        out_shape=jax.ShapeDtypeStruct((step_cells, width, depth), jnp.bfloat16),
        scratch_shapes=[pltpu.VMEM((step_cells, images * bands, width), jnp.bfloat16)],
        compiler_params=pltpu.CompilerParams(vmem_limit_bytes=48 * 1024 * 1024),
        cost_estimate=pl.CostEstimate(flops=1, bytes_accessed=1, transcendentals=0),
        name="line_grads",
    )(low_turned, *pixels, *grads)


def band_kernel(first, count, at_ref, grad_ref, *refs):
    weight_refs, pixel_refs = refs[:count], refs[count : count + 2]
    if first:
        total_ref, weight_now, made = refs[count + 2 :]
    else:
        before_ref, total_ref, weight_now, made = refs[count + 2 :]
    share = pixel_refs[0].shape[1]
    images = 2 * share
    cells = weight_now.shape[0]
    bands = pixel_refs[0].shape[3] // cells

    @pl.when(pl.program_id(0) == 0)
    def _():
        if first:
            total_ref[...] = jnp.zeros_like(total_ref)
        else:
            total_ref[...] = before_ref[...]

    for at in range(count):

        @pl.when((pl.program_id(0) == at) | (count == 1))
        def _(at=at):
            weight_now[...] = weight_refs[at][...]

    for image in range(images):
        block = pixel_refs[image // share][0, image % share]
        grads = dot_tn(block, grad_ref[image]).astype(jnp.bfloat16)
        for cell in range(cells):
            made[cell, image * bands : (image + 1) * bands, :] = grads[
                cell * bands : (cell + 1) * bands
            ]
    for cell in range(cells):
        total_ref[...] += dot_nn(made[cell], weight_now[cell])


def band_piece(place, grads, weights, pixels, total):
    pieces, share, rows, lanes = pixels[0].shape
    images = 2 * share
    cells, width, depth = weights[0].shape
    step = lanes // (4 * 16)
    count = len(weights)
    steps = max(count, cells // step)
    bands = lanes // (4 * step)
    first = total is None
    whole_total = pl.BlockSpec((images * bands, depth), lambda t, at: (0, 0))
    if count == 1:
        weight_specs = [pl.BlockSpec((step, width, depth), lambda t, at: (t, 0, 0))]
    else:
        weight_specs = [pl.BlockSpec((step, width, depth), lambda t, at: (0, 0, 0))] * count
    return pl.pallas_call(
        partial(band_kernel, first, count),
        grid_spec=pltpu.PrefetchScalarGridSpec(
            num_scalar_prefetch=1,
            grid=(steps,),
            in_specs=[pl.BlockSpec(grads.shape, lambda t, at: (0, 0, 0))]
            + weight_specs
            + [
                pl.BlockSpec(
                    (1, share, rows, step * bands), lambda t, at: (at[0], 0, 0, at[1 + t])
                ),
            ]
            * 2
            + ([] if first else [whole_total]),
            out_specs=whole_total,
            scratch_shapes=[
                pltpu.VMEM((step, width, depth), jnp.bfloat16),
                pltpu.VMEM((step, images * bands, width), jnp.bfloat16),
            ],
        ),
        out_shape=jax.ShapeDtypeStruct((images * bands, depth), jnp.float32),
        compiler_params=grid_params(40),
        cost_estimate=pl.CostEstimate(flops=1, bytes_accessed=1, transcendentals=0),
        name="band_piece",
    )(place, grads, *weights, *pixels, *(() if first else (total,)))


def head_probs(patches, query, keyed, mine):
    rows = query.shape[0]
    scores = dot_nt(jnp.where(mine, query, jnp.zeros_like(query)), keyed)
    column = lax.broadcasted_iota(jnp.int32, (1, rows), 1)
    scores = jnp.where(column < patches, scores, -1e30)
    powers = jnp.exp(scores - jnp.max(scores, axis=-1, keepdims=True))
    return powers * (1.0 / jnp.sum(powers, axis=-1, keepdims=True))


def attend_kernel(patches, head_size, joint_ref, out_ref):
    width = out_ref.shape[2]
    pair = 2 * head_size
    lane = lax.broadcasted_iota(jnp.int32, (1, pair), 1)
    scale = jnp.asarray(head_size ** (-0.5), jnp.bfloat16)
    for at in range(0, width, pair):
        query = joint_ref[0, :, at : at + pair] * scale
        keyed = joint_ref[0, :, width + at : width + at + pair]
        valued = joint_ref[0, :, 2 * width + at : 2 * width + at + pair]
        mixed = []
        for head in range(2):
            mine = (lane >= head * head_size) & (lane < (head + 1) * head_size)
            probs = head_probs(patches, query, keyed, mine)
            mixed.append(dot_nn(probs.astype(jnp.bfloat16), valued))
        out_ref[0, :, at : at + pair] = jnp.where(lane < head_size, mixed[0], mixed[1]).astype(
            jnp.bfloat16
        )


def attend(joint, patches, head_size):
    images, rows, triple = joint.shape
    width = triple // 3
    return pl.pallas_call(
        partial(attend_kernel, patches, head_size),
        grid=(images,),
        in_specs=[pl.BlockSpec((1, rows, triple), lambda i: (i, 0, 0))],
        out_specs=pl.BlockSpec((1, rows, width), lambda i: (i, 0, 0)),
        out_shape=jax.ShapeDtypeStruct((images, rows, width), jnp.bfloat16),
        compiler_params=grid_params(24),
        cost_estimate=pl.CostEstimate(flops=1, bytes_accessed=1, transcendentals=0),
        name="attend",
    )(joint)


def attend_back_kernel(patches, head_size, joint_ref, grad_ref, out_ref, sum_ref):
    width = grad_ref.shape[2]
    pair = 2 * head_size
    lane = lax.broadcasted_iota(jnp.int32, (1, pair), 1)
    scale = jnp.asarray(head_size ** (-0.5), jnp.bfloat16)

    @pl.when(pl.program_id(0) == 0)
    def _():
        sum_ref[...] = jnp.zeros_like(sum_ref)

    for at in range(0, width, pair):
        query = joint_ref[0, :, at : at + pair] * scale
        keyed = joint_ref[0, :, width + at : width + at + pair]
        valued = joint_ref[0, :, 2 * width + at : 2 * width + at + pair]
        grads = grad_ref[0, :, at : at + pair]
        none = jnp.zeros_like(grads)
        parts = []
        for head in range(2):
            mine = (lane >= head * head_size) & (lane < (head + 1) * head_size)
            probs = head_probs(patches, query, keyed, mine)
            grad = jnp.where(mine, grads, none)
            to_probs = dot_nt(grad, valued)
            inner = jnp.sum(probs * to_probs, axis=-1, keepdims=True)
            to_scores = (probs * (to_probs - inner)).astype(jnp.bfloat16)
            parts.append(
                (
                    dot_nn(to_scores, jnp.where(mine, keyed, none)),
                    dot_tn(to_scores, jnp.where(mine, query, none)),
                    dot_tn(probs.astype(jnp.bfloat16), grad),
                )
            )
        to_query = (parts[0][0] + parts[1][0]) * (head_size ** (-0.5))
        to_keyed = parts[0][1] + parts[1][1]
        to_valued = parts[0][2] + parts[1][2]
        for slot, value in enumerate((to_query, to_keyed, to_valued)):
            value = value.astype(jnp.bfloat16)
            out_ref[0, :, slot * width + at : slot * width + at + pair] = value
            sum_ref[:, slot * width + at : slot * width + at + pair] += jnp.sum(
                value.astype(jnp.float32), axis=0, keepdims=True
            )


def attend_back(joint, grads, patches, head_size):
    images, rows, triple = joint.shape
    width = triple // 3
    return pl.pallas_call(
        partial(attend_back_kernel, patches, head_size),
        grid=(images,),
        in_specs=[
            pl.BlockSpec((1, rows, triple), lambda i: (i, 0, 0)),
            pl.BlockSpec((1, rows, width), lambda i: (i, 0, 0)),
        ],
        out_specs=[
            pl.BlockSpec((1, rows, triple), lambda i: (i, 0, 0)),
            pl.BlockSpec((1, triple), lambda i: (0, 0)),
        ],
        out_shape=[
            jax.ShapeDtypeStruct((images, rows, triple), jnp.bfloat16),
            jax.ShapeDtypeStruct((1, triple), jnp.float32),
        ],
        compiler_params=grid_params(24),
        cost_estimate=pl.CostEstimate(flops=1, bytes_accessed=1, transcendentals=0),
        name="attend_back",
    )(joint, grads)


def norm_inside(values, epsilon):
    center = values - jnp.mean(values, axis=-1, keepdims=True)
    factor = lax.rsqrt(jnp.mean(center * center, axis=-1, keepdims=True) + epsilon)
    return center * factor, factor


def small_call(kernel, name, grid, in_specs, out_specs, out_shape, scratch=(), limit=40):
    return pl.pallas_call(
        kernel,
        grid=grid,
        in_specs=in_specs,
        out_specs=out_specs,
        out_shape=out_shape,
        scratch_shapes=list(scratch),
        compiler_params=grid_params(limit),
        cost_estimate=pl.CostEstimate(flops=1, bytes_accessed=1, transcendentals=0),
        name=name,
    )


def whole_spec(shape):
    return pl.BlockSpec(shape, lambda i: (0,) * len(shape))


def image_spec(rows, width):
    return pl.BlockSpec((1, rows, width), lambda i: (i, 0, 0))


def joint_kernel(
    own_ref, beside_ref, bias_ref, gain_ref, shift_ref, weight_ref, joint_bias_ref,
    embedded_ref, normed_ref, joint_ref,
):
    embedded = own_ref[0] + beside_ref[0] + bias_ref[0]
    embedded_ref[0] = embedded
    normed = norm_inside(embedded, block_eps)[0] * gain_ref[...] + shift_ref[...]
    normed = normed.astype(jnp.bfloat16)
    normed_ref[0] = normed
    joint = dot_nn(normed, weight_ref[...]) + joint_bias_ref[...]
    joint_ref[0] = joint.astype(jnp.bfloat16)


def make_joint(total, beside, image_bias, gain, shift, weight, joint_bias):
    images, rows, width = beside.shape
    triple = weight.shape[1]
    return small_call(
        joint_kernel,
        "make_joint",
        (images,),
        [image_spec(rows, width)] * 2
        + [image_spec(1, width), whole_spec((1, width)), whole_spec((1, width))]
        + [whole_spec(weight.shape), whole_spec((1, triple))],
        [image_spec(rows, width), image_spec(rows, width), image_spec(rows, triple)],
        [
            jax.ShapeDtypeStruct((images, rows, width), jnp.float32),
            jax.ShapeDtypeStruct((images, rows, width), jnp.bfloat16),
            jax.ShapeDtypeStruct((images, rows, triple), jnp.bfloat16),
        ],
    )(total, beside, image_bias[:, None], gain[None], shift[None], weight, joint_bias[None])


def residual_kernel(
    attended_ref, embedded_ref, weight_ref, bias_ref, gain_ref, shift_ref, residual_ref, normed_ref
):
    branch = dot_nn(attended_ref[0], weight_ref[...]) + bias_ref[...]
    residual = embedded_ref[0] + branch
    residual_ref[0] = residual
    normed = norm_inside(residual, block_eps)[0] * gain_ref[...] + shift_ref[...]
    normed_ref[0] = normed.astype(jnp.bfloat16)


def make_residual(attended, embedded, weight, bias, gain, shift):
    images, rows, width = embedded.shape
    return small_call(
        residual_kernel,
        "make_residual",
        (images,),
        [image_spec(rows, width)] * 2 + [whole_spec(weight.shape)] + [whole_spec((1, width))] * 3,
        [image_spec(rows, width)] * 2,
        [
            jax.ShapeDtypeStruct((images, rows, width), jnp.float32),
            jax.ShapeDtypeStruct((images, rows, width), jnp.bfloat16),
        ],
    )(attended, embedded, weight, bias[None], gain[None], shift[None])


def norm_back_inside(grad, values, gain, epsilon):
    normal, factor = norm_inside(values, epsilon)
    scaled = grad * gain
    back = factor * (
        scaled
        - jnp.mean(scaled, axis=-1, keepdims=True)
        - normal * jnp.mean(scaled * normal, axis=-1, keepdims=True)
    )
    return back, jnp.sum(grad * normal, axis=0, keepdims=True)


def add_rows(out_ref, rows):
    @pl.when(pl.program_id(0) == 0)
    def _():
        out_ref[...] = jnp.zeros_like(out_ref)

    out_ref[...] += jnp.concatenate(rows, axis=0)


def branch_back_kernel(
    grad_ref, residual_ref, out_grad_ref, gain_ref, weight_ref,
    resid_ref, branch_ref, att_ref, sum_ref,
):
    grad = grad_ref[0]
    out_grad = out_grad_ref[0].astype(jnp.float32)
    back, gain_grad = norm_back_inside(grad, residual_ref[0], gain_ref[...], block_eps)
    resid = out_grad + back
    resid_ref[0] = resid
    branch = resid.astype(jnp.bfloat16)
    branch_ref[0] = branch
    att_ref[0] = dot_nt(branch, weight_ref[...]).astype(jnp.bfloat16)
    add_rows(
        sum_ref,
        [
            gain_grad,
            jnp.sum(grad, axis=0, keepdims=True),
            jnp.sum(branch.astype(jnp.float32), axis=0, keepdims=True),
            jnp.sum(out_grad, axis=0, keepdims=True),
        ],
    )


def branch_back(grad, residual, out_grad, gain, weight):
    images, rows, width = residual.shape
    return small_call(
        branch_back_kernel,
        "branch_back",
        (images,),
        [image_spec(rows, width)] * 3 + [whole_spec((1, width)), whole_spec(weight.shape)],
        [image_spec(rows, width)] * 3 + [whole_spec((4, width))],
        [
            jax.ShapeDtypeStruct((images, rows, width), jnp.float32),
            jax.ShapeDtypeStruct((images, rows, width), jnp.bfloat16),
            jax.ShapeDtypeStruct((images, rows, width), jnp.bfloat16),
            jax.ShapeDtypeStruct((4, width), jnp.float32),
        ],
    )(grad, residual, out_grad, gain[None], weight)


def embed_back_kernel(
    joint_ref, weight_ref, embedded_ref, resid_ref, gain_ref, emb_ref, sum_ref, image_ref
):
    grad = dot_nt(joint_ref[0], weight_ref[...])
    back, gain_grad = norm_back_inside(grad, embedded_ref[0], gain_ref[...], block_eps)
    emb = (resid_ref[0] + back).astype(jnp.bfloat16)
    emb_ref[0] = emb
    image_ref[0] = jnp.sum(emb.astype(jnp.float32), axis=0, keepdims=True)
    add_rows(sum_ref, [gain_grad, jnp.sum(grad, axis=0, keepdims=True)])


def embed_back(joint_grad, weight, embedded, resid, gain):
    images, rows, width = embedded.shape
    return small_call(
        embed_back_kernel,
        "embed_back",
        (images,),
        [image_spec(rows, joint_grad.shape[2]), whole_spec(weight.shape)]
        + [image_spec(rows, width)] * 2
        + [whole_spec((1, width))],
        [image_spec(rows, width), whole_spec((2, width)), image_spec(1, width)],
        [
            jax.ShapeDtypeStruct((images, rows, width), jnp.bfloat16),
            jax.ShapeDtypeStruct((2, width), jnp.float32),
            jax.ShapeDtypeStruct((images, 1, width), jnp.float32),
        ],
    )(joint_grad, weight, embedded, resid, gain[None])


def mlp_kernel(
    normed_ref, residual_ref, grad_ref, up_ref, bias_ref, down_ref, down_bias_ref,
    out_ref, back_ref, up_grad_ref, down_grad_ref, bias_grad_ref, active, to_pre, turned, total,
):
    rows = normed_ref.shape[0]
    part = rows // 2

    @pl.when(pl.program_id(0) == 0)
    def _():
        total[...] = residual_ref[...] + down_bias_ref[...]
        back_ref[...] = jnp.zeros_like(back_ref)
        turned[...] = normed_ref[...].T

    up = up_ref[...]
    down = down_ref[...]
    bias_grad = jnp.zeros(bias_grad_ref.shape, jnp.float32)
    for at in range(0, rows, part):
        span = slice(at, at + part)
        pre = dot_nn(normed_ref[span], up) + bias_ref[...]
        share = 0.5 + 0.5 * lax.erf(pre * (0.5**0.5))
        slope = share + pre * (jnp.exp(-0.5 * pre * pre) * (0.5 / jnp.pi) ** 0.5)
        act = (pre * share).astype(jnp.bfloat16)
        grad = (slope * dot_nt(grad_ref[span], down)).astype(jnp.bfloat16)
        active[span] = act
        to_pre[span] = grad
        total[span] += dot_nn(act, down)
        back_ref[span] += dot_nt(grad, up)
        bias_grad += jnp.sum(grad.astype(jnp.float32), axis=0, keepdims=True)
    bias_grad_ref[...] = bias_grad
    up_grad_ref[...] = dot_nn(turned[...], to_pre[...]).astype(jnp.bfloat16)
    down_grad_ref[...] = dot_tn(active[...], grad_ref[...]).astype(jnp.bfloat16)

    @pl.when(pl.program_id(0) == pl.num_programs(0) - 1)
    def _():
        out_ref[...] = total[...].astype(jnp.bfloat16)


def mlp(normed, residual, grads, up, up_bias, down, down_bias):
    rows, width = normed.shape
    hidden = up.shape[1]
    part = 256
    whole = pl.BlockSpec((rows, width), lambda s: (0, 0))
    columns = pl.BlockSpec((width, part), lambda s: (0, s))
    lines = pl.BlockSpec((part, width), lambda s: (s, 0))
    vector = pl.BlockSpec((1, part), lambda s: (0, s))
    return pl.pallas_call(
        mlp_kernel,
        grid=(hidden // part,),
        in_specs=[
            whole, whole, whole, columns, vector, lines,
            pl.BlockSpec((1, width), lambda s: (0, 0)),
        ],
        out_specs=[whole, whole, columns, lines, vector],
        out_shape=[
            jax.ShapeDtypeStruct((rows, width), jnp.bfloat16),
            jax.ShapeDtypeStruct((rows, width), jnp.float32),
            jax.ShapeDtypeStruct((width, hidden), jnp.bfloat16),
            jax.ShapeDtypeStruct((hidden, width), jnp.bfloat16),
            jax.ShapeDtypeStruct((1, hidden), jnp.float32),
        ],
        scratch_shapes=[
            pltpu.VMEM((rows, part), jnp.bfloat16),
            pltpu.VMEM((rows, part), jnp.bfloat16),
            pltpu.VMEM((width, rows), jnp.bfloat16),
            pltpu.VMEM((rows, width), jnp.float32),
        ],
        compiler_params=grid_params(40),
        cost_estimate=pl.CostEstimate(flops=1, bytes_accessed=1, transcendentals=0),
        name="mlp",
    )(normed, residual, grads, up, up_bias[None], down, down_bias[None])


def per_device(
    pixels,
    band_count,
    band_bin,
    bin_wave,
    run_mean,
    run_var,
    weight_tokens,
    bias_token,
    hyper_in,
    hyper_qv_bias,
    hyper_out,
    hyper_out_bias,
    hyper_gain,
    hyper_shift,
    hyper_up,
    hyper_up_bias,
    hyper_down,
    hyper_down_bias,
    kernel_weight,
    bias_weight,
    bias_offset,
    norm_gain,
    norm_shift,
    w_qkv,
    qv_bias,
    w_out,
    out_bias,
    w_up,
    up_bias,
    w_down,
    down_bias,
    cotangent,
):
    pixel_data = pixels[0]
    images, band_slots, patches, pixel_cells = pixel_data.shape
    bin_total = bin_wave.shape[0]
    model_width = w_qkv.shape[0]
    head_size = model_width // HEADS
    padded = -(-patches // 16) * 16
    rows = images * padded
    cells = kernel_weight.shape[0]
    core = lax.axis_index("batch") & 1
    live_band = (
        lax.broadcasted_iota(jnp.int32, (images, band_slots), 1) < band_count[0][:, None]
    ).astype(jnp.float32)
    bin_onehot = (
        band_bin[0][..., None]
        == lax.broadcasted_iota(jnp.int32, (images, band_slots, bin_total), 2)
    ).astype(jnp.float32)
    chosen = bin_onehot * live_band[..., None]
    run_rstd = lax.rsqrt(run_var + stat_eps)
    band_mean = jnp.einsum("ibn,n->ib", chosen, run_mean, precision=highest)
    band_rstd = jnp.einsum("ibn,n->ib", chosen, run_rstd, precision=highest)
    values32 = pixel_data.astype(jnp.float32)
    band_total = jnp.sum(values32, axis=(2, 3))
    band_square = jnp.sum(values32 * values32, axis=(2, 3))
    bin_sums = jnp.einsum("ib,ibn->n", band_total, chosen, precision=highest)
    bin_squares = jnp.einsum("ib,ibn->n", band_square, chosen, precision=highest)
    bin_counts = jnp.sum(chosen, axis=(0, 1))

    grad_out = jnp.pad(cotangent[0], ((0, 0), (0, padded - patches), (0, 0)))
    band_wave = jnp.einsum("ibn,n->ib", bin_onehot, bin_wave, precision=highest)
    wave_emb = wave_embed(band_wave, hyper_in.shape[0])
    hyper_params = (
        weight_tokens,
        bias_token,
        hyper_in,
        hyper_qv_bias,
        hyper_out,
        hyper_out_bias,
        hyper_gain,
        hyper_shift,
        hyper_up,
        hyper_up_bias,
        hyper_down,
        hyper_down_bias,
    )

    def make_low():
        (band_vec, bias_vec), hyper_back = jax.vjp(
            partial(hypernet, wave_emb=wave_emb, live_band=live_band), hyper_params
        )
        band_low = band_vec.astype(jnp.bfloat16).reshape(images * band_slots, -1)
        return band_low, bias_vec, hyper_back

    def place(piece, *quarters):
        return jnp.stack([jnp.asarray(at, jnp.int32) for at in (piece,) + quarters])

    if not tuned_mesh():
        band_low, bias_vec, hyper_back = make_low()
        chip_low = jnp.concatenate([band_low, swap_batch(band_low, 1)])
        mine, other = split_pixels(pixel_data, band_mean, band_rstd, core, padded, cells)
        chip_pixels = (mine, swap_batch(other, 1))
        total, kernels = (None, None)
        for at, weight in enumerate(plain_weight_pieces(kernel_weight)):
            total, kernels = embed_piece(
                place(at, 0, 1, 2, 3), chip_low, [weight], chip_pixels, total, kernels
            )
        line_pixels = plain_line_cells(jnp.concatenate(chip_pixels, axis=1))
        line_low = lax.all_gather(
            chip_low, "batch", axis=0, axis_index_groups=same_core(), tiled=True
        )
    else:
        group = lax.axis_index("group")
        chip = lax.axis_index("batch") >> 1
        part = cells // 8
        quarter = part_of(kernel_weight, group, 4)

        def sides(block):
            return swap_group(block, 1), swap_group(block, 2)

        def corners(beside, above):
            return swap_group(beside[:part], 2), swap_group(above[part:], 1)

        def added(state, piece, weights, shifts):
            spots = place(piece, *[group ^ shift for shift in shifts])
            return embed_piece(spots, chip_low, weights, chip_pixels, *state)

        def pixel_block(hop, half):
            piece = lax.dynamic_index_in_dim(chip_pixels[half], chip ^ hop, 0, keepdims=False)
            return swap_batch(piece, 2 * hop) if hop else piece

        right1, left1 = (along_line(quarter, -1), along_line(quarter, 1))
        band_low, bias_vec, hyper_back = make_low()
        band_low, bias_vec, right1, left1, pixel_data = tie(
            band_low, bias_vec, right1, left1, pixel_data
        )
        block1 = jnp.where(chip == 3, left1, right1)
        right2, left2 = (along_line(right1, -1), along_line(left1, 1))
        beside1, above1 = sides(block1)
        mine, other = split_pixels(pixel_data, band_mean, band_rstd, core, padded, cells)
        chip_low = jnp.concatenate([band_low, swap_batch(band_low, 1)])
        mine, other, chip_low, right2, left2, beside1, above1 = tie(
            mine, other, chip_low, right2, left2, beside1, above1
        )
        block2 = jnp.where(chip == 0, right2, jnp.where(chip == 3, left2, left1))
        right3, left3 = (along_line(right2, -1), along_line(left2, 1))
        corner1 = corners(beside1, above1)
        beside2, above2 = sides(block2)
        chip_pixels = (mine, swap_batch(other, 1))
        pixels2 = [pixel_block(2, 0)]
        state = embed_piece(
            place(chip, 0, 1, 2, 3), chip_low, [kernel_weight], chip_pixels, None, None
        )
        weights1 = [block1, beside1, above1]
        spots1 = of_chip(chip, [1, 2, 3, 2])
        state = added(state, spots1, weights1, (0, 1, 2))
        state, chip_pixels, right3, left3, corner1, beside2, above2, pixels2 = tie(
            state, chip_pixels, right3, left3, corner1, beside2, above2, pixels2
        )
        block3 = jnp.where(
            chip == 0, right3, jnp.where(chip == 1, right2, jnp.where(chip == 2, left2, left3))
        )
        corner2 = corners(beside2, above2)
        beside3, above3 = sides(block3)
        pixels2.append(pixel_block(2, 1))
        pixels1 = [pixel_block(1, 0)]
        weights1.append(jnp.concatenate(corner1))
        state = added(state, spots1, weights1[3:], (3,))
        weights2 = [block2, beside2, above2]
        spots2 = of_chip(chip, [2, 0, 1, 1])
        state = added(state, spots2, weights2, (0, 1, 2))
        state, corner2, beside3, above3, pixels1, pixels2, chip_pixels, grad_out = tie(
            state, corner2, beside3, above3, pixels1, pixels2, chip_pixels, grad_out
        )
        corner3 = corners(beside3, above3)
        pixels1.append(pixel_block(1, 1))
        weights2.append(jnp.concatenate(corner2))
        state = added(state, spots2, weights2[3:], (3,))
        weights3 = [block3, beside3, above3]
        spots3 = of_chip(chip, [3, 3, 0, 0])
        state = added(state, spots3, weights3, (0, 1, 2))
        state, corner3, pixels1, chip_pixels = tie(state, corner3, pixels1, chip_pixels)
        pixels3 = [pixel_block(3, 0)]
        weights3.append(jnp.concatenate(corner3))
        total, kernels = added(state, spots3, weights3[3:], (3,))
        line_low = line_rows(chip_low)
    image_bias = jnp.dot(bias_vec, bias_weight, precision=highest) + bias_offset
    total_beside = swap_batch(total[images:], 1)
    joint_bias = jnp.concatenate([qv_bias[0], jnp.zeros_like(qv_bias[0]), qv_bias[1]])
    embedded, normed1, joint = make_joint(
        total, total_beside, image_bias, norm_gain[0], norm_shift[0], w_qkv, joint_bias
    )
    attended = attend(joint, patches, head_size)
    if tuned_mesh():
        attended, pixels3, chip_pixels = tie(attended, pixels3, chip_pixels)
        pixels3.append(pixel_block(3, 1))
    residual, normed2 = make_residual(
        attended, embedded, w_out, out_bias, norm_gain[1], norm_shift[1]
    )
    block_out, grad_n2, grad_w_up, grad_w_down, grad_up_bias = mlp(
        normed2.reshape(rows, model_width),
        residual.reshape(rows, model_width),
        grad_out.reshape(rows, model_width),
        w_up,
        up_bias,
        w_down,
        down_bias,
    )
    if tuned_mesh():
        grad_n2, pixels3, grad_w_up, grad_w_down = tie(grad_n2, pixels3, grad_w_up, grad_w_down)
    block_out = block_out.reshape(1, images, padded, model_width)[:, :, :patches]
    grad_resid, grad_branch, grad_att, branch_sum = branch_back(
        grad_n2.reshape(images, padded, model_width), residual, grad_out, norm_gain[1], w_out
    )
    grad_gain_two, grad_shift_two, grad_out_bias, grad_down_bias = branch_sum
    grad_joint, joint_sum = attend_back(joint, grad_att, patches, head_size)
    grad_emb, embed_sum, grad_image_bias = embed_back(
        grad_joint, w_qkv, embedded, grad_resid, norm_gain[0]
    )
    grad_gain_one, grad_shift_one = embed_sum
    grad_image_bias = grad_image_bias[:, 0]
    grad_qv_bias = joint_sum.reshape(3, model_width)[::2]
    attended = attended.reshape(rows, model_width)
    grad_branch = grad_branch.reshape(rows, model_width)
    half_up, half_down = core_sum(grad_w_up), core_sum(grad_w_down)
    share_up, share_down = row_share(half_up), row_share(half_down)
    grad_w_out = jnp.einsum("rd,re->de", attended, grad_branch, preferred_element_type=jnp.float32)
    grad_w_qkv = jnp.einsum(
        "rd,rj->dj",
        normed1.reshape(rows, model_width),
        grad_joint.reshape(rows, 3 * model_width),
        preferred_element_type=jnp.float32,
    )
    beside_emb = swap_batch(grad_emb, 1)
    if tuned_mesh():
        far_emb = [swap_batch(grad_emb, 2 * hop) for hop in (1, 2)]
    grad_bias_weight = jnp.einsum("ik,ie->ke", bias_vec, grad_image_bias, precision=highest)
    grad_bias_offset = jnp.sum(grad_image_bias, axis=0)
    grad_bias_vec = jnp.einsum("ie,ke->ik", grad_image_bias, bias_weight, precision=highest)

    def pack(hyper_grads):
        wide = (
            hyper_grads[0],
            hyper_grads[2],
            hyper_grads[4],
            hyper_grads[8],
            hyper_grads[10],
            grad_bias_weight,
        )
        narrow = (
            hyper_grads[1],
            hyper_grads[3],
            hyper_grads[5],
            hyper_grads[6],
            hyper_grads[7],
            hyper_grads[9],
            hyper_grads[11],
            bin_sums,
            bin_squares,
            bin_counts,
            grad_bias_offset,
            jnp.stack([grad_gain_one, grad_gain_two]),
            jnp.stack([grad_shift_one, grad_shift_two]),
            grad_qv_bias,
            grad_out_bias,
            grad_up_bias[0],
            grad_down_bias,
        )
        parts = [block_rows(part) for part in wide]
        thin = [part.reshape(-1, 128) for part in narrow]
        length = sum(part.shape[0] for part in thin)
        thin = jnp.concatenate(thin + [jnp.zeros((-length % 128, 128), jnp.float32)])
        (thin,) = tie(thin)
        parts.append(thin)
        length = sum(part.shape[0] for part in parts)
        parts.append(jnp.zeros((-length % 256, 128), jnp.float32))
        small = jnp.concatenate(parts)
        return wide, narrow, parts, small

    rates = jnp.tile(band_rstd, (1, pixel_cells // 8))
    rates = jnp.concatenate([rates, swap_batch(rates, 1)])[:, None, :]
    chip_emb = jnp.concatenate([grad_emb, beside_emb])

    def finish_low(grad_vectors):
        far = swap_batch(grad_vectors[images * band_slots :], 1)
        grad_vectors = grad_vectors[: images * band_slots] + far
        grad_vectors = grad_vectors.reshape(images, band_slots, -1)
        return hyper_back((grad_vectors, grad_bias_vec))[0]

    half_out = core_sum(grad_w_out.astype(jnp.bfloat16))
    half_qkv = core_sum(grad_w_qkv.astype(jnp.bfloat16))
    grad_vectors = None
    if tuned_mesh():
        plan = [
            (place(chip, 0, 1, 2, 3), [kernel_weight]),
            (place(spots1, group, group ^ 1, group ^ 2, group ^ 3), weights1),
            (place(spots2, group, group ^ 1, group ^ 2, group ^ 3), weights2),
            (place(spots3, group, group ^ 1, group ^ 2, group ^ 3), weights3),
        ]
        for spots, weights in plan:
            grad_vectors = band_piece(spots, chip_emb, weights, chip_pixels, grad_vectors)
        grad_vectors, far_emb, half_out, half_qkv, share_up, line_low, rates = tie(
            grad_vectors, far_emb, half_out, half_qkv, share_up, line_low, rates
        )
        far_emb.append(swap_batch(grad_emb, 6))
        share_out_rows, share_qkv = row_share(half_out), row_share(half_qkv)
        line_emb = [grad_emb, beside_emb]
        for far in far_emb[:2]:
            line_emb += [far, swap_batch(far, 1)]
        hyper_grads = finish_low(grad_vectors)
        wide, narrow, parts, small = pack(hyper_grads)
        small, block_out, far_emb, line_emb, share_down, share_out_rows, share_qkv, chip_emb = tie(
            small, block_out, far_emb, line_emb, share_down, share_out_rows, share_qkv, chip_emb
        )
        line_emb += [far_emb[2], swap_batch(far_emb[2], 1)]
        line_pixels = [pixel_block(0, 0), pixel_block(0, 1)] + pixels1 + pixels2 + pixels3
    else:
        for at, weight in enumerate(plain_weight_pieces(kernel_weight)):
            grad_vectors = band_piece(
                place(at, 0, 1, 2, 3), chip_emb, [weight], chip_pixels, grad_vectors
            )
        hyper_grads = finish_low(grad_vectors)
        wide, narrow, parts, small = pack(hyper_grads)
        share_out_rows, share_qkv = row_share(half_out), row_share(half_qkv)
        line_emb = plain_line_images(grad_emb, beside_emb)
    halves = 2 if cells % 32 == 0 else 1
    low_turned = line_low.T

    if not tuned_mesh():
        kernel_share = 0.0
        for at in range(0, line_pixels[0].shape[0], 32):
            columns = low_turned[:, at * band_slots : (at + 32) * band_slots]
            found = line_grads(
                columns, cells, [line_pixels[0][at : at + 32]], [line_emb[0][at : at + 32]], 0, 1
            )
            kernel_share += found.astype(jnp.float32)
        kernel_total = lax.psum(kernel_share.astype(jnp.bfloat16), "group").astype(jnp.float32)
        chip_back = pixel_grads(chip_emb, kernels, rates)
        other_back = swap_batch(chip_back[:, images:], 1)
        pixel_grad = join_pixels(
            chip_back[:, :images], other_back, core, patches, cells, pixel_cells, band_slots
        )
        small = lax.psum(small, ("group", "batch"))
        totals = [
            row_both(row_mine(share)) for share in (share_qkv, share_out_rows, share_up, share_down)
        ]
    else:
        def halved(value):
            rows_half = value.shape[0] // 2
            return [value[:rows_half], value[rows_half:]]

        kernel_one = line_grads(low_turned, cells, line_pixels, line_emb, 0, 2)
        small_came = swap_batch(part_of(small, 1 - core, 2), 1)
        kernel_one, small_came, line_emb = tie(kernel_one, small_came, line_emb)

        one = halved(kernel_one)
        one_came = sum_out(one, False)
        small = part_of(small, core, 2) + small_came
        small_came = [swap_batch(part_of(small, chip ^ hop, 4), 2 * hop) for hop in (1, 2, 3)]
        mine_up, mine_down = row_mine(share_up), row_mine(share_down)
        kernel_two = line_grads(low_turned, cells, line_pixels, line_emb, 1, 2)
        kernel_two, one_came, chip_emb, small_came = tie(
            kernel_two, one_came, chip_emb, small_came
        )

        one = sum_in(one, one_came, False)
        one_came = sum_out(one, True)
        two = halved(kernel_two)
        two_came = sum_out(two, False)
        small = sum(small_came, part_of(small, chip, 4))
        small_came = swap_group(small, 1)
        chip_back = pixel_grads(chip_emb, kernels, rates)
        chip_back, one_came, two_came, small_came, mine_up, mine_down, share_qkv = tie(
            chip_back, one_came, two_came, small_came, mine_up, mine_down, share_qkv
        )

        one = sum_in(one, one_came, True)
        one_came = share_out(one, True)
        two = sum_in(two, two_came, False)
        two_came = sum_out(two, True)
        small = small + small_came
        small_came = swap_group(small, 2)
        other_back = swap_batch(chip_back[:, images:], 1)
        mine_qkv, mine_out = row_mine(share_qkv), row_mine(share_out_rows)
        totals = [row_both(mine) for mine in (mine_up, mine_down)]
        other_back, one_came, two_came, small_came, totals = tie(
            other_back, one_came, two_came, small_came, totals
        )

        one = share_in(one, one_came, True)
        one_came = share_out(one, False)
        two = sum_in(two, two_came, True)
        two_came = share_out(two, True)
        small = small + small_came
        small_came = [swap_batch(small, 2 * hop) for hop in (1, 2, 3)]
        pixel_grad = join_pixels(
            chip_back[:, :images], other_back, core, patches, cells, pixel_cells, band_slots
        )
        pixel_grad, one_came, two_came, small_came, mine_qkv, mine_out = tie(
            pixel_grad, one_came, two_came, small_came, mine_qkv, mine_out
        )

        two = share_in(two, two_came, True)
        two_came = share_out(two, False)
        small = four_in_order(chip, [small] + small_came)
        small_came = swap_batch(small, 1)
        one = share_in(one, one_came, False)
        totals = [row_both(mine_qkv), row_both(mine_out)] + totals
        two_came, small_came, one, totals = tie(two_came, small_came, one, totals)
        small = in_order(core, small, small_came)
        kernel_total = jnp.concatenate(one + share_in(two, two_came, False)).astype(jnp.float32)
    pixel_grad = pixel_grad[None]

    found = []
    at = 0
    for part, like in zip(parts, wide):
        found.append(unblock_rows(small[at : at + part.shape[0]], like.shape[0]))
        at += part.shape[0]
    for like in narrow:
        count = like.size // 128
        found.append(small[at : at + count].reshape(like.shape))
        at += count
    batch_mean, batch_var = bin_stats(found[13], found[14], found[15], patches * pixel_cells)
    return (
        block_out,
        pixel_grad,
        batch_mean,
        batch_var,
        found[0],
        found[6],
        found[1],
        found[7],
        found[2],
        found[8],
        found[9],
        found[10],
        found[3],
        found[11],
        found[4],
        found[12],
        kernel_total,
        found[5],
        found[16],
        found[17],
        found[18],
        totals[0],
        found[19],
        totals[1],
        found[20],
        totals[2],
        found[21],
        totals[3],
        found[22],
    )


def solution(mesh):
    return jax.shard_map(
        per_device,
        mesh=mesh,
        in_specs=(
            P("group", "batch", None, None, None),
            P("group", "batch"),
            P("group", "batch", None),
            P(),
            P(),
            P(),
            P(),
            P(),
            P(),
            P(),
            P(),
            P(),
            P(),
            P(),
            P(),
            P(),
            P(),
            P(),
            P("batch", None, None),
            P(),
            P(),
            P(),
            P(),
            P(),
            P(),
            P(),
            P(),
            P(),
            P(),
            P(),
            P(),
            P("group", "batch", None, None),
        ),
        out_specs=(
            P("group", "batch", None, None),
            P("group", "batch", None, None, None),
            P(),
            P(),
            P(),
            P(),
            P(),
            P(),
            P(),
            P(),
            P(),
            P(),
            P(),
            P(),
            P(),
            P(),
            P("batch", None, None),
            P(),
            P(),
            P(),
            P(),
            P("group", None),
            P(),
            P("group", None),
            P(),
            P("group", None),
            P(),
            P("group", None),
            P(),
        ),
        check_vma=False,
    )
```

time: 2220 us -> 898 us (0.40)
  waiting for transfers between devices: 1370 us -> 180 us
  matrix products: 386 us -> 67.4 us
  Pallas kernels: 0 us -> 250 us
  blocking collectives: 185 us -> 0 us
  starting transfers between devices: 0.94 us -> 129 us
    unnamed x9 -> x6, waiting for transfers between devices: 817 us -> 0.1 us
    all_gather x1 -> x0, waiting for transfers between devices: 353 us -> none  [per_device(): lax.all_gather(kernel_weight, 'batch', axis=0, tiled=True)]
    dot_general x42 -> x20, matrix products: 375 us -> 61.7 us  [the longest x3 20.7 us: hypernet(): jnp.einsum('nsf,fk->nsk', inner_act, w_reduce, precision=high)]
    pallas_call x0 -> x23, Pallas kernels: none -> 250 us  [the longest x7 70.5 us: embed_piece(): pl.pallas_call(partial(embed_kernel, first, count), grid_spec=pltpu.Prefe...]
    psum x2 -> x0, blocking collectives: 185 us -> none  [the longest x1 144 us: per_device(): lax.psum((row_share[0], row_share[1], row_share[2], row_share[3]), 'batch')]
    ppermute x0 -> x74, waiting for transfers between devices: none -> 166 us  [the longest x38 104 us: swap_batch(): lax.ppermute(value, 'batch', [(at, at ^ bits) for at in range(count)])]
    ppermute x0 -> x74, starting transfers between devices: none -> 128 us  [the longest x38 75 us: swap_batch(): lax.ppermute(value, 'batch', [(at, at ^ bits) for at in range(count)])]
    psum x2, waiting for transfers between devices: 139 us -> 14.2 us  [row_mine(): return lax.psum(share, 'batch', axis_index_groups=same_core())]
  transfers between devices with their start and end apart: 8 -> 80, of which waited for: 5 -> 29; matrix products, arithmetic and copies ran while one was open for 14% -> 24% of each run, Pallas kernels for 0% -> 27%
where the time goes in v1:
time: 898 us; the launch traced here: 887 us
  Pallas kernels  250 us (28%)
  waiting for transfers between devices  180 us (20%)
  local copies, waits for them, and re-layouts  146 us (16%)
  starting transfers between devices  129 us (14%)
  other arithmetic  97.3 us (11%)
  matrix products  67.4 us (8%)
  between operations  17.4 us (2%)
    ppermute x38, waiting for transfers between devices, swap_batch(): lax.ppermute(value, 'batch', [(at, at ^ bits) for at in range(count)])  104 us
    ppermute x38, starting transfers between devices, swap_batch(): lax.ppermute(value, 'batch', [(at, at ^ bits) for at in range(count)])  75 us
    pallas_call x7, Pallas kernels, embed_piece(): pl.pallas_call(partial(embed_kernel, first, count), grid_spec=pltpu.Prefe...  70.5 us
    unnamed x386, local copies, waits for them, and re-layouts  54.7 us
    ppermute x30, waiting for transfers between devices, swap_group(): return lax.ppermute(value, 'group', [(at, at ^ bits) for at in range(4)])  50.1 us
    pallas_call x1, Pallas kernels, mlp(): pl.pallas_call(mlp_kernel, grid=(hidden // part,), in_specs=[whole, whole...  35.8 us
    pallas_call x4, Pallas kernels, band_piece(): pl.pallas_call(partial(band_kernel, first, count), grid_spec=pltpu.Prefet...  32 us
    ppermute x30, starting transfers between devices, swap_group(): return lax.ppermute(value, 'group', [(at, at ^ bits) for at in range(4)])  30.8 us
  transfers between devices with their start and end apart: 80, of which 29 were waited for; matrix products, arithmetic and copies ran while one was open for 24% of the time, Pallas kernels for 27%

profile of v1, /device:TPU:0, one launch (start us, length us, event | category | flops | bytes accessed | tf_op | source)
XLA Modules:
  0.0 886.9 jit_solution(8866521134401468485)
XLA Ops:
  29.4 11.2 %fusion.1 = f32[4,145,2048]{2,1,0:T(8,128)S(1)} fusion(f32[4,145,2048]{2,1,0:T(8,128)S(1)} %get-tuple-element.481, f32[2048]{0:T(1024)S(1)} %copy-done.132, u8[145,2048]{1,0:T(8,128)(4,1)S(1)} %get-tuple-element.412, u8[145,2048]{1,0:T(8,128)(4,1)S(1)} %get-tuple-element.411), kind=kLoop, calls=%fused_computation.6 | loop fusion | flops 80773120 | bytes 10104832 | tf_op jit(solution)/shard_map/jvp()/erfc | solution.py:123
  67.4 15.3 %split_pixels.1 = (bf16[4,4,208,512]{3,2,1,0:T(8,128)(2,1)S(1)}, bf16[4,4,208,512]{3,2,1,0:T(8,128)(2,1)}) custom-call(s32[1]{0:T(128)} %bitcast.6.core_ref, bf16[4,196,16,256]{3,2,1,0:T(8,128)(2,1)S(1)} %bitcast.279, f32[4,16,1]{2,1,0:T(8,128)S(1)} %convolution_bitcast_fusion.3.mean_ref, f32[4,16,1]{2,1,0:T(8,128)S(1)} %copy.153.rate_ref), custom_call_target="tpu_custom_call" | custom-call | flops 1 | bytes 1 | tf_op jit(solution)/shard_map/split_pixels/pallas_call | solution.py:355
  105.7 11.2 %collective-permute-done.10 = bf16[4,768,128]{2,1,0:T(8,128)(2,1)S(1)} collective-permute-done((bf16[4,768,128]{2,1,0:T(8,128)(2,1)}, bf16[4,768,128]{2,1,0:T(8,128)(2,1)S(1)}, u32[]{:S(2)}, u32[]{:S(2)}) %collective-permute-start.10) | collective-permute-done | bytes 786464 | tf_op jit(solution)/shard_map/ppermute | solution.py:140
  133.9 11.9 %embed_piece.7 = (f32[8,208,768]{2,1,0:T(8,128)}, bf16[4,8,512,768]{3,2,1,0:T(8,128)(2,1)}) custom-call(s32[5]{0:T(128)S(1)} %stack.81.at_ref, bf16[128,128]{1,0:T(8,128)(2,1)S(1)} %copy.163.low_ref, bf16[32,768,128]{2,1,0:T(8,128)(2,1)} %refs_0_.3, bf16[4,4,208,512]{3,2,1,0:T(8,128)(2,1)S(1)} %copy-done.2, ...), custom_call_target="tpu_custom_call" | custom-call | flops 1 | bytes 1 | tf_op jit(solution)/shard_map/embed_piece/pallas_call | solution.py:482
  145.7 11.9 %embed_piece.8 = (f32[8,208,768]{2,1,0:T(8,128)}, bf16[4,8,512,768]{3,2,1,0:T(8,128)(2,1)}) custom-call(s32[4]{0:T(128)S(1)} %add_add_fusion.4.at_ref, bf16[128,128]{1,0:T(8,128)(2,1)S(1)} %copy.163.low_ref, bf16[8,768,128]{2,1,0:T(8,128)(2,1)S(1)} %broadcast_select_fusion.refs_0_, ...), custom_call_target="tpu_custom_call", output_to_operand_aliasing={{0}: (7, {}), {1}: (8, {})} | custom-call | flops 1 | bytes 1 | tf_op jit(solution)/shard_map/embed_piece/pallas_call | solution.py:482
  157.6 36.1 %collective-permute-done.14.refs_5_ = bf16[4,208,512]{2,1,0:T(8,128)(2,1)S(1)} collective-permute-done((bf16[4,208,512]{2,1,0:T(8,128)(2,1)}, bf16[4,208,512]{2,1,0:T(8,128)(2,1)S(1)}, u32[]{:S(2)}, u32[]{:S(2)}) %collective-permute-start.14) | collective-permute-done | bytes 852000 | tf_op jit(solution)/shard_map/ppermute | solution.py:145
  232.9 12.3 %embed_piece.10 = (f32[8,208,768]{2,1,0:T(8,128)}, bf16[4,8,512,768]{3,2,1,0:T(8,128)(2,1)}) custom-call(s32[4]{0:T(128)S(1)} %get-tuple-element.496.at_ref, bf16[128,128]{1,0:T(8,128)(2,1)S(1)} %copy.163.low_ref, bf16[8,768,128]{2,1,0:T(8,128)(2,1)} %select_select_fusion.1.refs_0_, ...), custom_call_target="tpu_custom_call", output_to_operand_aliasing={{0}: (7, {}), {1}: (8, {})} | custom-call | flops 1 | bytes 1 | tf_op jit(solution)/shard_map/embed_piece/pallas_call | solution.py:482
  269.7 12.7 %embed_piece.12 = (f32[8,208,768]{2,1,0:T(8,128)}, bf16[4,8,512,768]{3,2,1,0:T(8,128)(2,1)}) custom-call(s32[4]{0:T(128)S(1)} %get-tuple-element.495.at_ref, bf16[128,128]{1,0:T(8,128)(2,1)S(1)} %copy.163.low_ref, bf16[8,768,128]{2,1,0:T(8,128)(2,1)} %select_select_fusion.refs_0_, ...), custom_call_target="tpu_custom_call", output_to_operand_aliasing={{0}: (7, {}), {1}: (8, {})} | custom-call | flops 1 | bytes 1 | tf_op jit(solution)/shard_map/embed_piece/pallas_call | solution.py:482
  330.8 35.8 %mlp.1 = (bf16[832,768]{1,0:T(8,128)(2,1)S(1)}, f32[832,768]{1,0:T(8,128)S(1)}, bf16[768,3072]{1,0:T(8,128)(2,1)S(1)}, bf16[3072,768]{1,0:T(8,128)(2,1)}, f32[1,3072]{1,0:T(1,128)S(1)}) custom-call(bf16[832,768]{1,0:T(8,128)(2,1)S(1)} %bitcast.285, f32[832,768]{1,0:T(8,128)S(1)} %bitcast.281, bf16[832,768]{1,0:T(8,128)(2,1)S(1)} %bitcast.280, ...), custom_call_target="tpu_custom_call" | custom-call | flops 1 | bytes 1 | tf_op jit(solution)/shard_map/mlp/pallas_call | solution.py:993
  406.7 17.0 %attend_back.1 = (bf16[4,208,2304]{2,1,0:T(8,128)(2,1)S(1)}, f32[1,2304]{1,0:T(1,128)S(1)}) custom-call(bf16[4,208,2304]{2,1,0:T(8,128)(2,1)S(1)} %copy-done.12, bf16[4,208,768]{2,1,0:T(8,128)(2,1)S(1)} %get-tuple-element.255.grad_ref), custom_call_target="tpu_custom_call" | custom-call | flops 1 | bytes 1 | tf_op jit(solution)/shard_map/attend_back/pallas_call | solution.py:754
  448.6 36.1 %collective-permute-start.33 = (bf16[128,128]{0,1:T(8,128)(2,1)}, bf16[128,128]{0,1:T(8,128)(2,1)S(1)}, u32[]{:S(2)}, u32[]{:S(2)}) collective-permute-start(bf16[128,128]{0,1:T(8,128)(2,1)} %copy-done.114), channel_id=1, source_target_pairs={{0,2},{1,3},{2,0},{3,1},{4,6},{5,7},{6,4},{7,5},{8,10},{9,11},{10,... | collective-permute-start | bytes 98312 | tf_op jit(solution)/shard_map/ppermute | solution.py:145
  508.4 8.1 band_piece.6.refs_6_
  518.7 8.4 band_piece.7
  530.3 16.2 %collective-permute-done.28.refs_11_ = bf16[4,208,768]{2,1,0:T(8,128)(2,1)} collective-permute-done((bf16[4,208,768]{2,1,0:T(8,128)(2,1)}, bf16[4,208,768]{2,1,0:T(8,128)(2,1)}, u32[]{:S(2)}, u32[]{:S(2)}) %collective-permute-start.28) | collective-permute-done | bytes 1277984 | tf_op jit(solution)/shard_map/ppermute | solution.py:145
  556.7 8.6 fusion.126
  610.9 9.6 %fusion.10 = f32[5632,128]{1,0:T(8,128)} fusion(f32[5632,128]{1,0:T(8,128)} %constant_dynamic-update-slice_fusion.10, f32[4,145,2048]{2,1,0:T(8,128)} %copy-done.61, f32[4,145,2048]{2,1,0:T(8,128)} %copy-done.60, f32[2048]{0:T(1024)S(1)} %copy-done.133, f32[4,145]{1,0:T(4,128)S(1)} %negate_multiply_fusion.2, f32[4,16,128]{2,1,0:T(8,128)S(1)} %bitcast.325, ...), kind=kOutput, calls=%fused_computation.38 | convolution fusion | flops 916418560 | bytes 11359808 | tf_op jit(solution)/shard_map/transpose(jvp(nsf,fk->nsk))/dot_general | solution.py:128
  634.5 12.2 %line_grads.2 = bf16[16,768,128]{2,1,0:T(8,128)(2,1)} custom-call(bf16[128,512]{1,0:T(8,128)(2,1)S(1)} %bitcast.287, bf16[4,208,512]{2,1,0:T(8,128)(2,1)S(1)} %dynamic-slice_bitcast_fusion.4.refs_1_, bf16[4,208,512]{2,1,0:T(8,128)(2,1)S(1)} %get-tuple-element.433.refs_2_, bf16[4,208,512]{2,1,0:T(8,128)(2,1)S(1)} %copy-done.39, ...), custom_call_target="tpu_custom_call" | custom-call | flops 1 | bytes 1 | tf_op jit(solution)/shard_map/line_grads/pallas_call | solution.py:578
  666.3 12.3 %line_grads.3 = bf16[16,768,128]{2,1,0:T(8,128)(2,1)} custom-call(bf16[128,512]{1,0:T(8,128)(2,1)S(1)} %bitcast.288, bf16[4,208,512]{2,1,0:T(8,128)(2,1)S(1)} %dynamic-slice_bitcast_fusion.4.refs_1_, bf16[4,208,512]{2,1,0:T(8,128)(2,1)S(1)} %get-tuple-element.433.refs_2_, bf16[4,208,512]{2,1,0:T(8,128)(2,1)S(1)} %copy-done.40, ...), custom_call_target="tpu_custom_call" | custom-call | flops 1 | bytes 1 | tf_op jit(solution)/shard_map/line_grads/pallas_call | solution.py:578
  684.2 10.5 %collective-permute-done.48 = f32[704,128]{1,0:T(8,128)} collective-permute-done((f32[704,128]{1,0:T(8,128)S(1)}, f32[704,128]{1,0:T(8,128)}, u32[]{:S(2)}, u32[]{:S(2)}) %collective-permute-start.48) | collective-permute-done | bytes 360480 | tf_op jit(solution)/shard_map/ppermute | solution.py:145
  707.5 13.8 %pixel_grads.1 = bf16[4,8,208,512]{3,2,1,0:T(8,128)(2,1)S(1)} custom-call(bf16[8,208,768]{2,1,0:T(8,128)(2,1)S(1)} %copy-done.8, bf16[4,8,512,768]{3,2,1,0:T(8,128)(2,1)} %get-tuple-element.303.kernel_ref, f32[8,1,512]{2,1,0:T(1,128)S(1)} %broadcast_in_dim.133.rate_ref), custom_call_target="tpu_custom_call" | custom-call | flops 1 | bytes 1 | tf_op jit(solution)/shard_map/pixel_grads/pallas_call | solution.py:526
  724.2 14.2 %all-reduce.19.cloned.1.call-done = (bf16[96,3072]{1,0:T(8,128)(2,1)}, bf16[384,768]{1,0:T(8,128)(2,1)}) async-done(((bf16[96,3072]{1,0:T(8,128)(2,1)}, bf16[384,768]{1,0:T(8,128)(2,1)}), (bf16[96,3072]{1,0:T(8,128)(2,1)}, bf16[384,768]{1,0:T(8,128)(2,1)})) %all-reduce.19.cloned.1.call-update) | async-done | bytes 1179664 | tf_op jit(solution)/shard_map/psum | solution.py:235
  791.0 18.7 %collective-permute-done.66 = f32[704,128]{1,0:T(8,128)} collective-permute-done((f32[704,128]{1,0:T(8,128)}, f32[704,128]{1,0:T(8,128)}, u32[]{:S(2)}, u32[]{:S(2)}) %collective-permute-start.66) | collective-permute-done | bytes 360480 | tf_op jit(solution)/shard_map/ppermute | solution.py:145
  816.3 14.1 %join_pixels.1 = bf16[4,196,16,256]{3,2,1,0:T(8,128)(2,1)} custom-call(s32[1]{0:T(128)} %bitcast.6.core_ref, bf16[4,4,208,512]{3,2,1,0:T(8,128)(2,1)S(1)} %copy-done.15, bf16[4,4,208,512]{3,2,1,0:T(8,128)(2,1)} %collective-permute-done.54.other_ref), custom_call_target="tpu_custom_call" | custom-call | flops 1 | bytes 1 | tf_op jit(solution)/shard_map/join_pixels/pallas_call | solution.py:414
  846.4 9.0 %collective-permute-done.70 = bf16[4,768,128]{2,1,0:T(8,128)(2,1)S(1)} collective-permute-done((bf16[4,768,128]{2,1,0:T(8,128)(2,1)S(1)}, bf16[4,768,128]{2,1,0:T(8,128)(2,1)S(1)}, u32[]{:S(2)}, u32[]{:S(2)}) %collective-permute-start.70) | collective-permute-done | bytes 786464 | tf_op jit(solution)/shard_map/ppermute | solution.py:140
  (773 shorter events, 502.2 us)
Async XLA Ops:
  7.3 540.4 %reduce-scatter.5.cloned.1.call-start = ((), (), s32[]{:S(2)}) async-start(), calls=%async_computation.4 | async-start | bytes 2949120 | tf_op jit(solution)/shard_map/reduce_scatter | solution.py:231
  102.9 90.9 %collective-permute-start.12 = (bf16[8,768,128]{2,1,0:T(8,128)(2,1)}, bf16[8,768,128]{2,1,0:T(8,128)(2,1)}, u32[]{:S(2)}, u32[]{:S(2)}) collective-permute-start(bf16[8,768,128]{2,1,0:T(8,128)(2,1)} %select_select_fusion.1.refs_0_), channel_id=1, source_target_pairs={{0,8},{8,0},{16,24},{24,16},{1,9},{9,1},{17,25},{25,17},{2,10},{10... | collective-permute-start | bytes 4718600 | tf_op jit(solution)/shard_map/ppermute | solution.py:140
  104.2 89.5 %collective-permute-start.13 = (bf16[8,768,128]{2,1,0:T(8,128)(2,1)}, bf16[8,768,128]{2,1,0:T(8,128)(2,1)}, u32[]{:S(2)}, u32[]{:S(2)}) collective-permute-start(bf16[8,768,128]{2,1,0:T(8,128)(2,1)} %select_select_fusion.1.refs_0_), channel_id=1, source_target_pairs={{0,16},{8,24},{16,0},{24,8},{1,17},{9,25},{17,1},{25,9},{2,18},{10... | collective-permute-start | bytes 4718600 | tf_op jit(solution)/shard_map/ppermute | solution.py:140
  116.9 76.9 %collective-permute-start.8 = (bf16[8,768,128]{2,1,0:T(8,128)(2,1)}, bf16[8,768,128]{2,1,0:T(8,128)(2,1)}, u32[]{:S(2)}, u32[]{:S(2)}) collective-permute-start(bf16[8,768,128]{2,1,0:T(8,128)(2,1)} %collective-permute-done.3), channel_id=1, source_target_pairs={{2,0},{3,1},{4,2},{5,3},{6,4},{7,5},{10,8},{11,9},{12,10},{13,11},... | collective-permute-start | bytes 4718600 | tf_op jit(solution)/shard_map/ppermute | solution.py:182
  119.6 74.1 %collective-permute-start.9 = (bf16[8,768,128]{2,1,0:T(8,128)(2,1)}, bf16[8,768,128]{2,1,0:T(8,128)(2,1)}, u32[]{:S(2)}, u32[]{:S(2)}) collective-permute-start(bf16[8,768,128]{2,1,0:T(8,128)(2,1)} %collective-permute-done.4), channel_id=1, source_target_pairs={{0,2},{1,3},{2,4},{3,5},{4,6},{5,7},{8,10},{9,11},{10,12},{11,13},... | collective-permute-start | bytes 4718600 | tf_op jit(solution)/shard_map/ppermute | solution.py:182
  127.3 66.4 %collective-permute-start.14 = (bf16[4,208,512]{2,1,0:T(8,128)(2,1)}, bf16[4,208,512]{2,1,0:T(8,128)(2,1)S(1)}, u32[]{:S(2)}, u32[]{:S(2)}) collective-permute-start(bf16[4,208,512]{2,1,0:T(8,128)(2,1)} %dynamic-slice_bitcast_fusion.10), channel_id=1, source_target_pairs={{0,4},{1,5},{2,6},{3,7},{4,0},{5,1},{6,2},{7,3},{8,12},{9,13},{10,... | collective-permute-start | bytes 2555912 | tf_op jit(solution)/shard_map/ppermute | solution.py:145
  200.0 52.0 %collective-permute-start.17 = (bf16[8,768,128]{2,1,0:T(8,128)(2,1)}, bf16[8,768,128]{2,1,0:T(8,128)(2,1)}, u32[]{:S(2)}, u32[]{:S(2)}) collective-permute-start(bf16[8,768,128]{2,1,0:T(8,128)(2,1)} %select_select_fusion.refs_0_), channel_id=1, source_target_pairs={{0,8},{8,0},{16,24},{24,16},{1,9},{9,1},{17,25},{25,17},{2,10},{10... | collective-permute-start | bytes 4718600 | tf_op jit(solution)/shard_map/ppermute | solution.py:140
  200.5 51.5 %collective-permute-start.18 = (bf16[8,768,128]{2,1,0:T(8,128)(2,1)}, bf16[8,768,128]{2,1,0:T(8,128)(2,1)}, u32[]{:S(2)}, u32[]{:S(2)}) collective-permute-start(bf16[8,768,128]{2,1,0:T(8,128)(2,1)} %select_select_fusion.refs_0_), channel_id=1, source_target_pairs={{0,16},{8,24},{16,0},{24,8},{1,17},{9,25},{17,1},{25,9},{2,18},{10... | collective-permute-start | bytes 4718600 | tf_op jit(solution)/shard_map/ppermute | solution.py:140
  204.2 47.8 %collective-permute-start.19 = (bf16[4,208,512]{2,1,0:T(8,128)(2,1)}, bf16[4,208,512]{2,1,0:T(8,128)(2,1)S(1)}, u32[]{:S(2)}, u32[]{:S(2)}) collective-permute-start(bf16[4,208,512]{2,1,0:T(8,128)(2,1)} %dynamic-slice_bitcast_fusion.9), channel_id=1, source_target_pairs={{0,2},{1,3},{2,0},{3,1},{4,6},{5,7},{6,4},{7,5},{8,10},{9,11},{10,... | collective-permute-start | bytes 2555912 | tf_op jit(solution)/shard_map/ppermute | solution.py:145
  321.5 45.2 %collective-permute-start.26 = (bf16[4,208,512]{2,1,0:T(8,128)(2,1)}, bf16[4,208,512]{2,1,0:T(8,128)(2,1)}, u32[]{:S(2)}, u32[]{:S(2)}) collective-permute-start(bf16[4,208,512]{2,1,0:T(8,128)(2,1)} %get-tuple-element.434), channel_id=1, source_target_pairs={{0,6},{1,7},{2,4},{3,5},{4,2},{5,3},{6,0},{7,1},{8,14},{9,15},{10,... | collective-permute-start | bytes 2555912 | tf_op jit(solution)/shard_map/ppermute | solution.py:145
  380.3 241.6 %reduce-scatter.7.cloned.1.call-start = ((), (), s32[]{:S(2)}) async-start(), calls=%async_computation.5 | async-start | bytes 2949120 | tf_op jit(solution)/shard_map/reduce_scatter | solution.py:231
  386.3 61.5 %collective-permute-start.36 = (f32[4,512]{1,0:T(4,128)}, f32[4,512]{1,0:T(4,128)}, u32[]{:S(2)}, u32[]{:S(2)}) collective-permute-start(f32[4,512]{1,0:T(4,128)} %tile.10), channel_id=1, source_target_pairs={{0,1},{1,0},{2,3},{3,2},{4,5},{5,4},{6,7},{7,6},{8,9},{9,8},{10,11... | collective-permute-start | bytes 24584 | tf_op jit(solution)/shard_map/ppermute | solution.py:145
  393.3 228.6 %reduce-scatter.9.cloned.1.call-start = ((), (), s32[]{:S(2)}) async-start(), calls=%async_computation.6 | async-start | bytes 737280 | tf_op jit(solution)/shard_map/reduce_scatter | solution.py:231
  437.9 89.3 %collective-permute-start.31 = (bf16[4,96,2304]{2,1,0:T(8,128)(2,1)}, bf16[4,96,2304]{2,1,0:T(8,128)(2,1)}, u32[]{:S(2)}, u32[]{:S(2)}) collective-permute-start(bf16[4,96,2304]{2,1,0:T(8,128)(2,1)} %dynamic-slice_bitcast_fusion.2), channel_id=1, source_target_pairs={{0,1},{1,0},{2,3},{3,2},{4,5},{5,4},{6,7},{7,6},{8,9},{9,8},{10,11... | collective-permute-start | bytes 5308424 | tf_op jit(solution)/shard_map/ppermute | solution.py:145
  438.1 51.6 %collective-permute-start.27 = (bf16[4,208,768]{2,1,0:T(8,128)(2,1)}, bf16[4,208,768]{2,1,0:T(8,128)(2,1)}, u32[]{:S(2)}, u32[]{:S(2)}) collective-permute-start(bf16[4,208,768]{2,1,0:T(8,128)(2,1)} %get-tuple-element.291.refs_9_), channel_id=1, source_target_pairs={{0,1},{1,0},{2,3},{3,2},{4,5},{5,4},{6,7},{7,6},{8,9},{9,8},{10,11... | collective-permute-start | bytes 3833864 | tf_op jit(solution)/shard_map/ppermute | solution.py:145
  443.5 73.1 %collective-permute-start.30 = (bf16[4,96,768]{2,1,0:T(8,128)(2,1)}, bf16[4,96,768]{2,1,0:T(8,128)(2,1)}, u32[]{:S(2)}, u32[]{:S(2)}) collective-permute-start(bf16[4,96,768]{2,1,0:T(8,128)(2,1)} %dynamic-slice_bitcast_fusion.11), channel_id=1, source_target_pairs={{0,1},{1,0},{2,3},{3,2},{4,5},{5,4},{6,7},{7,6},{8,9},{9,8},{10,11... | collective-permute-start | bytes 1769480 | tf_op jit(solution)/shard_map/ppermute | solution.py:145
  489.7 56.8 %collective-permute-start.28 = (bf16[4,208,768]{2,1,0:T(8,128)(2,1)}, bf16[4,208,768]{2,1,0:T(8,128)(2,1)}, u32[]{:S(2)}, u32[]{:S(2)}) collective-permute-start(bf16[4,208,768]{2,1,0:T(8,128)(2,1)} %get-tuple-element.291.refs_9_), channel_id=1, source_target_pairs={{0,2},{1,3},{2,0},{3,1},{4,6},{5,7},{6,4},{7,5},{8,10},{9,11},{10,... | collective-permute-start | bytes 3833864 | tf_op jit(solution)/shard_map/ppermute | solution.py:145
  489.8 57.9 %collective-permute-start.29 = (bf16[4,208,768]{2,1,0:T(8,128)(2,1)}, bf16[4,208,768]{2,1,0:T(8,128)(2,1)}, u32[]{:S(2)}, u32[]{:S(2)}) collective-permute-start(bf16[4,208,768]{2,1,0:T(8,128)(2,1)} %get-tuple-element.291.refs_9_), channel_id=1, source_target_pairs={{0,4},{1,5},{2,6},{3,7},{4,0},{5,1},{6,2},{7,3},{8,12},{9,13},{10,... | collective-permute-start | bytes 3833864 | tf_op jit(solution)/shard_map/ppermute | solution.py:145
  547.7 74.2 %reduce-scatter.11.cloned.1.call-start = ((), (), s32[]{:S(2)}) async-start(), calls=%async_computation.7 | async-start | bytes 2211840 | tf_op jit(solution)/shard_map/reduce_scatter | solution.py:231
  550.1 71.8 %collective-permute-start.38 = (bf16[4,208,768]{2,1,0:T(8,128)(2,1)}, bf16[4,208,768]{2,1,0:T(8,128)(2,1)}, u32[]{:S(2)}, u32[]{:S(2)}) collective-permute-start(bf16[4,208,768]{2,1,0:T(8,128)(2,1)} %get-tuple-element.291.refs_9_), channel_id=1, source_target_pairs={{0,6},{1,7},{2,4},{3,5},{4,2},{5,3},{6,0},{7,1},{8,14},{9,15},{10,... | collective-permute-start | bytes 3833864 | tf_op jit(solution)/shard_map/ppermute | solution.py:145
  554.9 67.0 %collective-permute-start.39 = (bf16[4,208,768]{2,1,0:T(8,128)(2,1)}, bf16[4,208,768]{2,1,0:T(8,128)(2,1)}, u32[]{:S(2)}, u32[]{:S(2)}) collective-permute-start(bf16[4,208,768]{2,1,0:T(8,128)(2,1)} %collective-permute-done.28.refs_11_), channel_id=1, source_target_pairs={{0,1},{1,0},{2,3},{3,2},{4,5},{5,4},{6,7},{7,6},{8,9},{9,8},{10,11... | collective-permute-start | bytes 3833864 | tf_op jit(solution)/shard_map/ppermute | solution.py:145
  555.5 66.4 %collective-permute-start.40 = (bf16[4,208,768]{2,1,0:T(8,128)(2,1)}, bf16[4,208,768]{2,1,0:T(8,128)(2,1)}, u32[]{:S(2)}, u32[]{:S(2)}) collective-permute-start(bf16[4,208,768]{2,1,0:T(8,128)(2,1)} %collective-permute-done.29.refs_13_), channel_id=1, source_target_pairs={{0,1},{1,0},{2,3},{3,2},{4,5},{5,4},{6,7},{7,6},{8,9},{9,8},{10,11... | collective-permute-start | bytes 3833864 | tf_op jit(solution)/shard_map/ppermute | solution.py:145
  555.6 182.8 %all-reduce.19.cloned.1.call-start = ((), (), s32[]{:S(2)}) async-start(), calls=%async_computation.9 | async-start | bytes 2359296 | tf_op jit(solution)/shard_map/psum | solution.py:235
  661.4 169.0 %all-reduce.17.cloned.1.call-start = ((), (), s32[]{:S(2)}) async-start(), calls=%async_computation.8 | async-start | bytes 1179648 | tf_op jit(solution)/shard_map/psum | solution.py:235
  (245 other events, 3236.4 us)
Sparse Core Ops, SparseCore 0:
  380.5 70.5 reduce-scatter.4
  454.6 37.3 reduce-scatter.6
  547.8 24.2 reduce-scatter.8
  575.8 32.4 reduce-scatter.10
  661.5 76.8 all-reduce.18
  753.8 55.0 all-reduce.16

commit v2 on v1

--- a/solution.py
+++ b/solution.py
@@ -176,9 +176,13 @@
     return lax.optimization_barrier(values)
 
 
-def along_line(value, step):
-    count = lax.axis_size("batch")
-    pairs = [(at, at + 2 * step) for at in range(count) if 0 <= at + 2 * step < count]
+def along_line(value, step, chips=(0, 1, 2, 3)):
+    pairs = [
+        (2 * at + core, 2 * (at + step) + core)
+        for at in chips
+        for core in (0, 1)
+        if 0 <= at + step < 4
+    ]
     return lax.ppermute(value, "batch", pairs)
 
 
@@ -214,17 +218,8 @@
     return jnp.concatenate([low] + [swap_batch(low, 2 * hop) for hop in (1, 2, 3)])
 
 
-def core_sum(grad):
-    core = lax.axis_index("batch") & 1
-    split = grad.reshape(4, 2, -1, grad.shape[1])
-    keep = lax.dynamic_index_in_dim(split, core, 1, keepdims=False)
-    send = lax.dynamic_index_in_dim(split, 1 - core, 1, keepdims=False)
-    came = swap_batch(send, 1)
-    return (
-        (keep.astype(jnp.float32) + came.astype(jnp.float32))
-        .astype(jnp.bfloat16)
-        .reshape(-1, grad.shape[1])
-    )
+def core_sum(keep, send):
+    return add_low(keep, swap_batch(send, 1))
 
 
 def row_share(half):
@@ -544,18 +539,17 @@
     lanes = pixel_refs[0].shape[2] // halves
     bands = lanes // cells
     columns = slice(half * lanes, (half + 1) * lanes)
+    spots = [(ref, at) for ref in grad_refs for at in range(ref.shape[0])]
     image = 0
-    for pixel_ref, grad_ref in zip(pixel_refs, grad_refs):
-        count = pixel_ref.shape[0]
-
-        @pl.loop(0, count, unroll=count if count <= 4 else 2)
-        def _(at, image=image):
-            grads = dot_tn(pixel_ref[at, :, columns], grad_ref[at]).astype(jnp.bfloat16)
-            row = pl.multiple_of((image + at) * bands, bands)
+    for pixel_ref in pixel_refs:
+        for at in range(pixel_ref.shape[0]):
+            grad_ref, where = spots[image]
+            grads = dot_tn(pixel_ref[at, :, columns], grad_ref[where]).astype(jnp.bfloat16)
             for cell in range(cells):
-                made[cell, pl.ds(row, bands), :] = grads[cell * bands : (cell + 1) * bands]
-
-        image += count
+                made[cell, image * bands : (image + 1) * bands, :] = grads[
+                    cell * bands : (cell + 1) * bands
+                ]
+            image += 1
 
     @pl.loop(0, cells, unroll=4)
     def _(cell):
@@ -572,12 +566,12 @@
 
     def body(*refs):
         pixel_refs = refs[1 : 1 + len(pixels)]
-        grad_refs = refs[1 + len(pixels) : 1 + 2 * len(pixels)]
+        grad_refs = refs[1 + len(pixels) : 1 + len(pixels) + len(grads)]
         line_kernel(half, halves, refs[0], pixel_refs, grad_refs, *refs[-2:])
 
     return pl.pallas_call(
         body,
-        in_specs=[vmem] * (1 + 2 * len(pixels)),
+        in_specs=[vmem] * (1 + len(pixels) + len(grads)),
         out_specs=vmem,
         out_shape=jax.ShapeDtypeStruct((step_cells, width, depth), jnp.bfloat16),
         scratch_shapes=[pltpu.VMEM((step_cells, images * bands, width), jnp.bfloat16)],
@@ -945,12 +939,56 @@
     )(joint_grad, weight, embedded, resid, gain[None])
 
 
+def split_rows(core, value, count, keep_ref, send_ref):
+    size = value.shape[0] // (2 * count)
+    for at in range(count):
+        first = value[2 * at * size : (2 * at + 1) * size]
+        second = value[(2 * at + 1) * size : (2 * at + 2) * size]
+        keep = jnp.where(core == 0, first, second).astype(jnp.bfloat16)
+        send = jnp.where(core == 0, second, first).astype(jnp.bfloat16)
+        keep_ref[at * size : (at + 1) * size] = keep
+        send_ref[at * size : (at + 1) * size] = send
+
+
+def rows_kernel(count, core_ref, left_ref, right_ref, keep_ref, send_ref, turned):
+    @pl.when(pl.program_id(0) == 0)
+    def _():
+        turned[...] = left_ref[...].T
+
+    split_rows(core_ref[0], dot_nn(turned[...], right_ref[...]), count, keep_ref, send_ref)
+
+
+def rows_grad(core, left, right, count=4):
+    rows, width = left.shape
+    columns = right.shape[1]
+    part = min(columns, 768)
+    half = jax.ShapeDtypeStruct((width // 2, columns), jnp.bfloat16)
+    return pl.pallas_call(
+        partial(rows_kernel, count),
+        grid_spec=pltpu.PrefetchScalarGridSpec(
+            num_scalar_prefetch=1,
+            grid=(columns // part,),
+            in_specs=[
+                pl.BlockSpec((rows, width), lambda s, core: (0, 0)),
+                pl.BlockSpec((rows, part), lambda s, core: (0, s)),
+            ],
+            out_specs=[pl.BlockSpec((width // 2, part), lambda s, core: (0, s))] * 2,
+            scratch_shapes=[pltpu.VMEM((width, rows), jnp.bfloat16)],
+        ),
+        out_shape=[half, half],
+        compiler_params=grid_params(32),
+        cost_estimate=pl.CostEstimate(flops=1, bytes_accessed=1, transcendentals=0),
+        name="rows_grad",
+    )(core.reshape(1), left, right)
+
+
 def mlp_kernel(
-    normed_ref, residual_ref, grad_ref, up_ref, bias_ref, down_ref, down_bias_ref,
-    out_ref, back_ref, up_grad_ref, down_grad_ref, bias_grad_ref, active, to_pre, turned, total,
+    core_ref, normed_ref, residual_ref, grad_ref, up_ref, bias_ref, down_ref, down_bias_ref,
+    out_ref, back_ref, up_keep_ref, up_send_ref, down_keep_ref, down_send_ref, bias_grad_ref,
+    active, to_pre, turned, total,
 ):
     rows = normed_ref.shape[0]
-    part = rows // 2
+    part = rows // MLP_PARTS
 
     @pl.when(pl.program_id(0) == 0)
     def _():
@@ -974,47 +1012,61 @@
         back_ref[span] += dot_nt(grad, up)
         bias_grad += jnp.sum(grad.astype(jnp.float32), axis=0, keepdims=True)
     bias_grad_ref[...] = bias_grad
-    up_grad_ref[...] = dot_nn(turned[...], to_pre[...]).astype(jnp.bfloat16)
-    down_grad_ref[...] = dot_tn(active[...], grad_ref[...]).astype(jnp.bfloat16)
+    core = core_ref[0]
+    split_rows(core, dot_nn(turned[...], to_pre[...]), 4, up_keep_ref, up_send_ref)
+    split_rows(core, dot_tn(active[...], grad_ref[...]), 1, down_keep_ref, down_send_ref)
 
     @pl.when(pl.program_id(0) == pl.num_programs(0) - 1)
     def _():
         out_ref[...] = total[...].astype(jnp.bfloat16)
 
 
-def mlp(normed, residual, grads, up, up_bias, down, down_bias):
+MLP_PARTS = 2
+
+
+def mlp(core, normed, residual, grads, up, up_bias, down, down_bias):
     rows, width = normed.shape
     hidden = up.shape[1]
-    part = 256
-    whole = pl.BlockSpec((rows, width), lambda s: (0, 0))
-    columns = pl.BlockSpec((width, part), lambda s: (0, s))
-    lines = pl.BlockSpec((part, width), lambda s: (s, 0))
-    vector = pl.BlockSpec((1, part), lambda s: (0, s))
+    part = hidden // 4
+    whole = pl.BlockSpec((rows, width), lambda s, core: (0, 0))
+    columns = pl.BlockSpec((width, part), lambda s, core: (0, s))
+    lines = pl.BlockSpec((part, width), lambda s, core: (s, 0))
+    vector = pl.BlockSpec((1, part), lambda s, core: (0, s))
+    up_half = jax.ShapeDtypeStruct((width // 2, hidden), jnp.bfloat16)
+    down_half = jax.ShapeDtypeStruct((hidden // 2, width), jnp.bfloat16)
     return pl.pallas_call(
         mlp_kernel,
-        grid=(hidden // part,),
-        in_specs=[
-            whole, whole, whole, columns, vector, lines,
-            pl.BlockSpec((1, width), lambda s: (0, 0)),
-        ],
-        out_specs=[whole, whole, columns, lines, vector],
+        grid_spec=pltpu.PrefetchScalarGridSpec(
+            num_scalar_prefetch=1,
+            grid=(hidden // part,),
+            in_specs=[
+                whole, whole, whole, columns, vector, lines,
+                pl.BlockSpec((1, width), lambda s, core: (0, 0)),
+            ],
+            out_specs=[whole, whole]
+            + [pl.BlockSpec((width // 2, part), lambda s, core: (0, s))] * 2
+            + [pl.BlockSpec((part // 2, width), lambda s, core: (s, 0))] * 2
+            + [vector],
+            scratch_shapes=[
+                pltpu.VMEM((rows, part), jnp.bfloat16),
+                pltpu.VMEM((rows, part), jnp.bfloat16),
+                pltpu.VMEM((width, rows), jnp.bfloat16),
+                pltpu.VMEM((rows, width), jnp.float32),
+            ],
+        ),
         out_shape=[
             jax.ShapeDtypeStruct((rows, width), jnp.bfloat16),
             jax.ShapeDtypeStruct((rows, width), jnp.float32),
-            jax.ShapeDtypeStruct((width, hidden), jnp.bfloat16),
-            jax.ShapeDtypeStruct((hidden, width), jnp.bfloat16),
+            up_half,
+            up_half,
+            down_half,
+            down_half,
             jax.ShapeDtypeStruct((1, hidden), jnp.float32),
         ],
-        scratch_shapes=[
-            pltpu.VMEM((rows, part), jnp.bfloat16),
-            pltpu.VMEM((rows, part), jnp.bfloat16),
-            pltpu.VMEM((width, rows), jnp.bfloat16),
-            pltpu.VMEM((rows, width), jnp.float32),
-        ],
-        compiler_params=grid_params(40),
+        compiler_params=grid_params(52),
         cost_estimate=pl.CostEstimate(flops=1, bytes_accessed=1, transcendentals=0),
         name="mlp",
-    )(normed, residual, grads, up, up_bias[None], down, down_bias[None])
+    )(core.reshape(1), normed, residual, grads, up, up_bias[None], down, down_bias[None])
 
 
 def per_device(
@@ -1130,7 +1182,13 @@
             return swap_group(block, 1), swap_group(block, 2)
 
         def corners(beside, above):
-            return swap_group(beside[:part], 2), swap_group(above[part:], 1)
+            return swap_group(beside[:part], 2), swap_group(above[part : 2 * part], 1)
+
+        def sides_and_corner(block, beside, above):
+            return (
+                swap_group(jnp.concatenate([block, above[part : 2 * part]]), 1),
+                swap_group(jnp.concatenate([block, beside[:part]]), 2),
+            )
 
         def added(state, piece, weights, shifts):
             spots = place(piece, *[group ^ shift for shift in shifts])
@@ -1146,7 +1204,7 @@
             band_low, bias_vec, right1, left1, pixel_data
         )
         block1 = jnp.where(chip == 3, left1, right1)
-        right2, left2 = (along_line(right1, -1), along_line(left1, 1))
+        right2, left2 = (along_line(right1, -1, (1, 2)), along_line(left1, 1, (1, 2)))
         beside1, above1 = sides(block1)
         mine, other = split_pixels(pixel_data, band_mean, band_rstd, core, padded, cells)
         chip_low = jnp.concatenate([band_low, swap_batch(band_low, 1)])
@@ -1154,9 +1212,12 @@
             mine, other, chip_low, right2, left2, beside1, above1
         )
         block2 = jnp.where(chip == 0, right2, jnp.where(chip == 3, left2, left1))
-        right3, left3 = (along_line(right2, -1), along_line(left2, 1))
-        corner1 = corners(beside1, above1)
-        beside2, above2 = sides(block2)
+        end3 = lax.ppermute(
+            jnp.where(chip == 1, right2, left2),
+            "batch",
+            [(2 + at, at) for at in range(2)] + [(4 + at, 6 + at) for at in range(2)],
+        )
+        across2, up2 = sides_and_corner(block2, beside1, above1)
         chip_pixels = (mine, swap_batch(other, 1))
         pixels2 = [pixel_block(2, 0)]
         state = embed_piece(
@@ -1165,36 +1226,32 @@
         weights1 = [block1, beside1, above1]
         spots1 = of_chip(chip, [1, 2, 3, 2])
         state = added(state, spots1, weights1, (0, 1, 2))
-        state, chip_pixels, right3, left3, corner1, beside2, above2, pixels2 = tie(
-            state, chip_pixels, right3, left3, corner1, beside2, above2, pixels2
-        )
-        block3 = jnp.where(
-            chip == 0, right3, jnp.where(chip == 1, right2, jnp.where(chip == 2, left2, left3))
-        )
-        corner2 = corners(beside2, above2)
-        beside3, above3 = sides(block3)
+        state, chip_pixels, end3, across2, up2, pixels2, bin_sums, bin_squares = tie(
+            state, chip_pixels, end3, across2, up2, pixels2, bin_sums, bin_squares
+        )
+        block3 = jnp.where(chip == 1, right2, jnp.where(chip == 2, left2, end3))
+        across3, up3 = sides_and_corner(block3, across2, up2)
         pixels2.append(pixel_block(2, 1))
         pixels1 = [pixel_block(1, 0)]
-        weights1.append(jnp.concatenate(corner1))
+        weights1.append(jnp.concatenate([up2[2 * part :], across2[2 * part :]]))
         state = added(state, spots1, weights1[3:], (3,))
-        weights2 = [block2, beside2, above2]
+        weights2 = [block2, across2, up2]
         spots2 = of_chip(chip, [2, 0, 1, 1])
         state = added(state, spots2, weights2, (0, 1, 2))
-        state, corner2, beside3, above3, pixels1, pixels2, chip_pixels, grad_out = tie(
-            state, corner2, beside3, above3, pixels1, pixels2, chip_pixels, grad_out
-        )
-        corner3 = corners(beside3, above3)
+        state, across3, up3, pixels1, pixels2, chip_pixels, grad_out = tie(
+            state, across3, up3, pixels1, pixels2, chip_pixels, grad_out
+        )
+        corner3 = corners(across3, up3)
         pixels1.append(pixel_block(1, 1))
-        weights2.append(jnp.concatenate(corner2))
+        weights2.append(jnp.concatenate([up3[2 * part :], across3[2 * part :]]))
         state = added(state, spots2, weights2[3:], (3,))
-        weights3 = [block3, beside3, above3]
+        weights3 = [block3, across3, up3]
         spots3 = of_chip(chip, [3, 3, 0, 0])
         state = added(state, spots3, weights3, (0, 1, 2))
         state, corner3, pixels1, chip_pixels = tie(state, corner3, pixels1, chip_pixels)
         pixels3 = [pixel_block(3, 0)]
         weights3.append(jnp.concatenate(corner3))
         total, kernels = added(state, spots3, weights3[3:], (3,))
-        line_low = line_rows(chip_low)
     image_bias = jnp.dot(bias_vec, bias_weight, precision=highest) + bias_offset
     total_beside = swap_batch(total[images:], 1)
     joint_bias = jnp.concatenate([qv_bias[0], jnp.zeros_like(qv_bias[0]), qv_bias[1]])
@@ -1202,13 +1259,15 @@
         total, total_beside, image_bias, norm_gain[0], norm_shift[0], w_qkv, joint_bias
     )
     attended = attend(joint, patches, head_size)
+    rates = jnp.tile(band_rstd, (1, pixel_cells // 8))
     if tuned_mesh():
-        attended, pixels3, chip_pixels = tie(attended, pixels3, chip_pixels)
-        pixels3.append(pixel_block(3, 1))
+        attended, chip_pixels, chip_low, rates = tie(attended, chip_pixels, chip_low, rates)
+        line_low = line_rows(chip_low)
     residual, normed2 = make_residual(
         attended, embedded, w_out, out_bias, norm_gain[1], norm_shift[1]
     )
-    block_out, grad_n2, grad_w_up, grad_w_down, grad_up_bias = mlp(
+    block_out, grad_n2, up_keep, up_send, down_keep, down_send, grad_up_bias = mlp(
+        core,
         normed2.reshape(rows, model_width),
         residual.reshape(rows, model_width),
         grad_out.reshape(rows, model_width),
@@ -1218,7 +1277,15 @@
         down_bias,
     )
     if tuned_mesh():
-        grad_n2, pixels3, grad_w_up, grad_w_down = tie(grad_n2, pixels3, grad_w_up, grad_w_down)
+        rates_beside = swap_batch(rates, 1)
+        grad_n2, pixels3, chip_pixels, line_low, rates_beside, up_send, down_send = tie(
+            grad_n2, pixels3, chip_pixels, line_low, rates_beside, up_send, down_send
+        )
+        pixels3.append(pixel_block(3, 1))
+    else:
+        rates_beside = swap_batch(rates, 1)
+    rates = jnp.concatenate([rates, rates_beside])[:, None, :]
+    up_came, down_came = swap_batch(up_send, 1), swap_batch(down_send, 1)
     block_out = block_out.reshape(1, images, padded, model_width)[:, :, :patches]
     grad_resid, grad_branch, grad_att, branch_sum = branch_back(
         grad_n2.reshape(images, padded, model_width), residual, grad_out, norm_gain[1], w_out
@@ -1228,23 +1295,32 @@
     grad_emb, embed_sum, grad_image_bias = embed_back(
         grad_joint, w_qkv, embedded, grad_resid, norm_gain[0]
     )
+    if tuned_mesh():
+        grad_emb, pixels3, up_keep, up_came, down_keep, down_came = tie(
+            grad_emb, pixels3, up_keep, up_came, down_keep, down_came
+        )
     grad_gain_one, grad_shift_one = embed_sum
     grad_image_bias = grad_image_bias[:, 0]
     grad_qv_bias = joint_sum.reshape(3, model_width)[::2]
     attended = attended.reshape(rows, model_width)
     grad_branch = grad_branch.reshape(rows, model_width)
-    half_up, half_down = core_sum(grad_w_up), core_sum(grad_w_down)
-    share_up, share_down = row_share(half_up), row_share(half_down)
-    grad_w_out = jnp.einsum("rd,re->de", attended, grad_branch, preferred_element_type=jnp.float32)
-    grad_w_qkv = jnp.einsum(
-        "rd,rj->dj",
+    share_up = row_share(add_low(up_keep, up_came))
+    share_down = row_share(add_low(down_keep, down_came))
+
+    def late_rows(attended, grad_branch, normed1, grad_joint):
+        out_keep, out_send = rows_grad(core, attended, grad_branch)
+        qkv_keep, qkv_send = rows_grad(core, normed1, grad_joint)
+        return core_sum(out_keep, out_send), core_sum(qkv_keep, qkv_send)
+
+    late = (
+        attended,
+        grad_branch,
         normed1.reshape(rows, model_width),
         grad_joint.reshape(rows, 3 * model_width),
-        preferred_element_type=jnp.float32,
     )
     beside_emb = swap_batch(grad_emb, 1)
     if tuned_mesh():
-        far_emb = [swap_batch(grad_emb, 2 * hop) for hop in (1, 2)]
+        far_emb = [swap_batch(grad_emb, 2), swap_batch(grad_emb, 4)]
     grad_bias_weight = jnp.einsum("ik,ie->ke", bias_vec, grad_image_bias, precision=highest)
     grad_bias_offset = jnp.sum(grad_image_bias, axis=0)
     grad_bias_vec = jnp.einsum("ie,ke->ik", grad_image_bias, bias_weight, precision=highest)
@@ -1288,8 +1364,6 @@
         small = jnp.concatenate(parts)
         return wide, narrow, parts, small
 
-    rates = jnp.tile(band_rstd, (1, pixel_cells // 8))
-    rates = jnp.concatenate([rates, swap_batch(rates, 1)])[:, None, :]
     chip_emb = jnp.concatenate([grad_emb, beside_emb])
 
     def finish_low(grad_vectors):
@@ -1298,8 +1372,6 @@
         grad_vectors = grad_vectors.reshape(images, band_slots, -1)
         return hyper_back((grad_vectors, grad_bias_vec))[0]
 
-    half_out = core_sum(grad_w_out.astype(jnp.bfloat16))
-    half_qkv = core_sum(grad_w_qkv.astype(jnp.bfloat16))
     grad_vectors = None
     if tuned_mesh():
         plan = [
@@ -1310,8 +1382,9 @@
         ]
         for spots, weights in plan:
             grad_vectors = band_piece(spots, chip_emb, weights, chip_pixels, grad_vectors)
-        grad_vectors, far_emb, half_out, half_qkv, share_up, line_low, rates = tie(
-            grad_vectors, far_emb, half_out, half_qkv, share_up, line_low, rates
+        half_out, half_qkv = late_rows(*late)
+        grad_vectors, far_emb, half_out, half_qkv, grad_emb, share_up = tie(
+            grad_vectors, far_emb, half_out, half_qkv, grad_emb, share_up
         )
         far_emb.append(swap_batch(grad_emb, 6))
         share_out_rows, share_qkv = row_share(half_out), row_share(half_qkv)
@@ -1320,16 +1393,23 @@
             line_emb += [far, swap_batch(far, 1)]
         hyper_grads = finish_low(grad_vectors)
         wide, narrow, parts, small = pack(hyper_grads)
-        small, block_out, far_emb, line_emb, share_down, share_out_rows, share_qkv, chip_emb = tie(
-            small, block_out, far_emb, line_emb, share_down, share_out_rows, share_qkv, chip_emb
-        )
+        (
+            small, block_out, far_emb, line_emb, share_up, share_down, share_out_rows, share_qkv,
+            chip_emb,
+        ) = tie(
+            small, block_out, far_emb, line_emb, share_up, share_down, share_out_rows, share_qkv,
+            chip_emb,
+        )
+        small_came = swap_batch(part_of(small, 1 - core, 2), 1)
         line_emb += [far_emb[2], swap_batch(far_emb[2], 1)]
+        small, small_came, line_emb = tie(small, small_came, line_emb)
         line_pixels = [pixel_block(0, 0), pixel_block(0, 1)] + pixels1 + pixels2 + pixels3
     else:
         for at, weight in enumerate(plain_weight_pieces(kernel_weight)):
             grad_vectors = band_piece(
                 place(at, 0, 1, 2, 3), chip_emb, [weight], chip_pixels, grad_vectors
             )
+        half_out, half_qkv = late_rows(*late)
         hyper_grads = finish_low(grad_vectors)
         wide, narrow, parts, small = pack(hyper_grads)
         share_out_rows, share_qkv = row_share(half_out), row_share(half_qkv)
@@ -1356,70 +1436,47 @@
             row_both(row_mine(share)) for share in (share_qkv, share_out_rows, share_up, share_down)
         ]
     else:
-        def halved(value):
-            rows_half = value.shape[0] // 2
-            return [value[:rows_half], value[rows_half:]]
-
-        kernel_one = line_grads(low_turned, cells, line_pixels, line_emb, 0, 2)
-        small_came = swap_batch(part_of(small, 1 - core, 2), 1)
-        kernel_one, small_came, line_emb = tie(kernel_one, small_came, line_emb)
-
-        one = halved(kernel_one)
-        one_came = sum_out(one, False)
         small = part_of(small, core, 2) + small_came
         small_came = [swap_batch(part_of(small, chip ^ hop, 4), 2 * hop) for hop in (1, 2, 3)]
-        mine_up, mine_down = row_mine(share_up), row_mine(share_down)
+        kernel_one = line_grads(low_turned, cells, line_pixels, line_emb, 0, 2)
+        kernel_one, line_emb, small_came = tie(kernel_one, line_emb, small_came)
+
         kernel_two = line_grads(low_turned, cells, line_pixels, line_emb, 1, 2)
-        kernel_two, one_came, chip_emb, small_came = tie(
-            kernel_two, one_came, chip_emb, small_came
-        )
-
-        one = sum_in(one, one_came, False)
-        one_came = sum_out(one, True)
-        two = halved(kernel_two)
-        two_came = sum_out(two, False)
+        sums = [kernel_one, kernel_two]
+        came = sum_out(sums, False)
         small = sum(small_came, part_of(small, chip, 4))
-        small_came = swap_group(small, 1)
+        small = small + swap_group(small, 1)
+        (small,) = tie(small)
+        small_came = swap_group(small, 2)
         chip_back = pixel_grads(chip_emb, kernels, rates)
-        chip_back, one_came, two_came, small_came, mine_up, mine_down, share_qkv = tie(
-            chip_back, one_came, two_came, small_came, mine_up, mine_down, share_qkv
-        )
-
-        one = sum_in(one, one_came, True)
-        one_came = share_out(one, True)
-        two = sum_in(two, two_came, False)
-        two_came = sum_out(two, True)
-        small = small + small_came
-        small_came = swap_group(small, 2)
-        other_back = swap_batch(chip_back[:, images:], 1)
-        mine_qkv, mine_out = row_mine(share_qkv), row_mine(share_out_rows)
-        totals = [row_both(mine) for mine in (mine_up, mine_down)]
-        other_back, one_came, two_came, small_came, totals = tie(
-            other_back, one_came, two_came, small_came, totals
-        )
-
-        one = share_in(one, one_came, True)
-        one_came = share_out(one, False)
-        two = sum_in(two, two_came, True)
-        two_came = share_out(two, True)
+        totals = [row_mine(share) for share in (share_qkv, share_out_rows, share_up, share_down)]
+        chip_back, came, small, small_came = tie(chip_back, came, small, small_came)
+
+        sums = sum_in(sums, came, False)
+        came = sum_out(sums, True)
         small = small + small_came
         small_came = [swap_batch(small, 2 * hop) for hop in (1, 2, 3)]
+        own_back, other_back = chip_back[:, :images], chip_back[:, images:]
+        came, own_back, other_back, totals = tie(came, own_back, other_back, totals)
+
+        sums = sum_in(sums, came, True)
+        came = share_out(sums, True)
+        other_back = swap_batch(other_back, 1)
+        came, small_came, other_back = tie(came, small_came, other_back)
+
+        sums = share_in(sums, came, True)
+        came = share_out(sums, False)
+        small = four_in_order(chip, [small] + small_came)
+        small = in_order(core, small, swap_batch(small, 1))
         pixel_grad = join_pixels(
-            chip_back[:, :images], other_back, core, patches, cells, pixel_cells, band_slots
-        )
-        pixel_grad, one_came, two_came, small_came, mine_qkv, mine_out = tie(
-            pixel_grad, one_came, two_came, small_came, mine_qkv, mine_out
-        )
-
-        two = share_in(two, two_came, True)
-        two_came = share_out(two, False)
-        small = four_in_order(chip, [small] + small_came)
-        small_came = swap_batch(small, 1)
-        one = share_in(one, one_came, False)
-        totals = [row_both(mine_qkv), row_both(mine_out)] + totals
-        two_came, small_came, one, totals = tie(two_came, small_came, one, totals)
-        small = in_order(core, small, small_came)
-        kernel_total = jnp.concatenate(one + share_in(two, two_came, False)).astype(jnp.float32)
+            own_back, other_back, core, patches, cells, pixel_cells, band_slots
+        )
+        (totals,) = tie(totals)
+        widths = [mine.shape[1] for mine in totals[:3]]
+        wide_mine = jnp.concatenate(totals[:3], axis=1)
+        wide_both = row_both(wide_mine)
+        ends = [0, widths[0], widths[0] + widths[1], sum(widths)]
+        totals = [wide_both[:, ends[at] : ends[at + 1]] for at in range(3)] + [row_both(totals[3])]
     pixel_grad = pixel_grad[None]
 
     found = []
@@ -1432,6 +1489,11 @@
         found.append(small[at : at + count].reshape(like.shape))
         at += count
     batch_mean, batch_var = bin_stats(found[13], found[14], found[15], patches * pixel_cells)
+    if tuned_mesh():
+        came, pixel_grad, found, totals, batch_mean, batch_var = tie(
+            came, pixel_grad, found, totals, batch_mean, batch_var
+        )
+        kernel_total = jnp.concatenate(share_in(sums, came, False)).astype(jnp.float32)
     return (
         block_out,
         pixel_grad,

time: 898 us -> 848 us (0.944)
  starting transfers between devices: 129 us -> 76.7 us
  local copies, waits for them, and re-layouts: 146 us -> 157 us
    ppermute x38 -> x36, waiting for transfers between devices: 104 us -> 48.5 us  [swap_batch(): lax.ppermute(value, 'batch', [(at, at ^ bits) for at in range(count)])]
    psum x2 -> x1, waiting for transfers between devices: 14.2 us -> 52.5 us  [row_mine(): return lax.psum(share, 'batch', axis_index_groups=same_core())]
    ppermute x38 -> x36, starting transfers between devices: 75 us -> 41.9 us  [swap_batch(): lax.ppermute(value, 'batch', [(at, at ^ bits) for at in range(count)])]
    convert_element_type x5 -> x1, other arithmetic: 21 us -> 8.43 us  [per_device(): jnp.concatenate(share_in(sums, came, False)).astype(jnp.float32)]
    unnamed x386 -> x428, local copies, waits for them, and re-layouts: 54.7 us -> 66.8 us
    ppermute x6 -> x4, starting transfers between devices: 22.4 us -> 11.1 us  [along_line(): return lax.ppermute(value, 'batch', pairs)]
    convert_element_type x8, other arithmetic: 9.35 us -> 20.5 us  [add_low(): (left.astype(jnp.float32) + right.astype(jnp.float32)).astype(left.dtype)]
    ppermute x30 -> x18, starting transfers between devices: 30.8 us -> 22.1 us  [swap_group(): return lax.ppermute(value, 'group', [(at, at ^ bits) for at in range(4)])]
  transfers between devices with their start and end apart: 80 -> 64, of which waited for: 29 -> 19; matrix products, arithmetic and copies ran while one was open for 24% -> 25% of each run, Pallas kernels for 27% -> 28%
where the time goes in v2:
time: 848 us; the launch traced here: 835 us
  Pallas kernels  253 us (30%)
  waiting for transfers between devices  176 us (21%)
  local copies, waits for them, and re-layouts  157 us (19%)
  other arithmetic  94.5 us (11%)
  starting transfers between devices  76.7 us (9%)
  matrix products  61 us (7%)
  between operations  16.8 us (2%)
    pallas_call x7, Pallas kernels, embed_piece(): pl.pallas_call(partial(embed_kernel, first, count), grid_spec=pltpu.Prefe...  70 us
    unnamed x428, local copies, waits for them, and re-layouts  66.8 us
    ppermute x18, waiting for transfers between devices, swap_group(): return lax.ppermute(value, 'group', [(at, at ^ bits) for at in range(4)])  55.2 us
    psum x1, waiting for transfers between devices, row_mine(): return lax.psum(share, 'batch', axis_index_groups=same_core())  52.5 us
    ppermute x36, waiting for transfers between devices, swap_batch(): lax.ppermute(value, 'batch', [(at, at ^ bits) for at in range(count)])  48.5 us
    ppermute x36, starting transfers between devices, swap_batch(): lax.ppermute(value, 'batch', [(at, at ^ bits) for at in range(count)])  41.9 us
    pallas_call x1, Pallas kernels, mlp(): pl.pallas_call(mlp_kernel, grid_spec=pltpu.PrefetchScalarGridSpec(num_sca...  33.2 us
    pallas_call x4, Pallas kernels, band_piece(): pl.pallas_call(partial(band_kernel, first, count), grid_spec=pltpu.Prefet...  29.8 us
  transfers between devices with their start and end apart: 64, of which 19 were waited for; matrix products, arithmetic and copies ran while one was open for 25% of the time, Pallas kernels for 28%

profile of v2, /device:TPU:0, one launch (start us, length us, event | category | flops | bytes accessed | tf_op | source)
XLA Modules:
  0.0 834.7 jit_solution(18342742329998537800)
XLA Ops:
  29.5 11.1 %fusion.1 = f32[4,145,2048]{2,1,0:T(8,128)S(1)} fusion(f32[4,145,2048]{2,1,0:T(8,128)S(1)} %get-tuple-element.561, f32[2048]{0:T(1024)S(1)} %copy-done.148, u8[145,2048]{1,0:T(8,128)(4,1)S(1)} %get-tuple-element.482, u8[145,2048]{1,0:T(8,128)(4,1)S(1)} %get-tuple-element.481), kind=kLoop, calls=%fused_computation.5 | loop fusion | flops 80773120 | bytes 10104832 | tf_op jit(solution)/shard_map/jvp()/erfc | solution.py:123
  63.0 15.4 %split_pixels.1 = (bf16[4,4,208,512]{3,2,1,0:T(8,128)(2,1)S(1)}, bf16[4,4,208,512]{3,2,1,0:T(8,128)(2,1)}) custom-call(s32[1]{0:T(128)} %bitcast.1.core_ref, bf16[4,196,16,256]{3,2,1,0:T(8,128)(2,1)S(1)} %bitcast.253, f32[4,16,1]{2,1,0:T(8,128)S(1)} %convolution_bitcast_fusion.3.mean_ref, f32[4,16,1]{2,1,0:T(8,128)S(1)} %copy.151.rate_ref), custom_call_target="tpu_custom_call" | custom-call | flops 1 | bytes 1 | tf_op jit(solution)/shard_map/split_pixels/pallas_call | solution.py:350
  80.2 7.8 collective-permute-done.5.refs_1_
  107.8 8.4 %collective-permute-start.11 = (bf16[4,208,512]{2,1,0:T(8,128)(2,1)}, bf16[4,208,512]{2,1,0:T(8,128)(2,1)S(1)}, u32[]{:S(2)}, u32[]{:S(2)}) collective-permute-start(bf16[4,208,512]{2,1,0:T(8,128)(2,1)} %dynamic-slice_bitcast_fusion.7), channel_id=1, source_target_pairs={{0,4},{1,5},{2,6},{3,7},{4,0},{5,1},{6,2},{7,3},{8,12},{9,13},{10,... | collective-permute-start | bytes 2555912 | tf_op jit(solution)/shard_map/ppermute | solution.py:145
  125.0 11.8 %embed_piece.7 = (f32[8,208,768]{2,1,0:T(8,128)}, bf16[4,8,512,768]{3,2,1,0:T(8,128)(2,1)}) custom-call(s32[5]{0:T(128)S(1)} %stack.81.at_ref, bf16[128,128]{1,0:T(8,128)(2,1)S(1)} %copy.161.low_ref, bf16[32,768,128]{2,1,0:T(8,128)(2,1)} %refs_0_.3, bf16[4,4,208,512]{3,2,1,0:T(8,128)(2,1)S(1)} %copy-done.2, ...), custom_call_target="tpu_custom_call" | custom-call | flops 1 | bytes 1 | tf_op jit(solution)/shard_map/embed_piece/pallas_call | solution.py:477
  136.7 11.9 %embed_piece.8 = (f32[8,208,768]{2,1,0:T(8,128)}, bf16[4,8,512,768]{3,2,1,0:T(8,128)(2,1)}) custom-call(s32[4]{0:T(128)S(1)} %add_add_fusion.4.at_ref, bf16[128,128]{1,0:T(8,128)(2,1)S(1)} %copy.161.low_ref, bf16[8,768,128]{2,1,0:T(8,128)(2,1)S(1)} %copy-done.22, ...), custom_call_target="tpu_custom_call", output_to_operand_aliasing={{0}: (7, {}), {1}: (8, {})} | custom-call | flops 1 | bytes 1 | tf_op jit(solution)/shard_map/embed_piece/pallas_call | solution.py:477
  152.7 8.7 %collective-permute-done.8 = bf16[8,768,128]{2,1,0:T(8,128)(2,1)} collective-permute-done((bf16[8,768,128]{2,1,0:T(8,128)(2,1)}, bf16[8,768,128]{2,1,0:T(8,128)(2,1)}, u32[]{:S(2)}, u32[]{:S(2)}) %collective-permute-start.8) | collective-permute-done | bytes 1572896 | tf_op jit(solution)/shard_map/ppermute | solution.py:1215
  196.8 11.9 %embed_piece.10 = (f32[8,208,768]{2,1,0:T(8,128)}, bf16[4,8,512,768]{3,2,1,0:T(8,128)(2,1)}) custom-call(s32[4]{0:T(128)S(1)} %get-tuple-element.576.at_ref, bf16[128,128]{1,0:T(8,128)(2,1)S(1)} %copy.161.low_ref, bf16[8,768,128]{2,1,0:T(8,128)(2,1)S(1)} %get-tuple-element.505.refs_0_, ...), custom_call_target="tpu_custom_call", output_to_operand_aliasing={{0}: (7, {}), {1}: (8, {})} | custom-call | flops 1 | bytes 1 | tf_op jit(solution)/shard_map/embed_piece/pallas_call | solution.py:477
  231.9 7.7 embed_piece.11
  239.6 12.3 %embed_piece.12 = (f32[8,208,768]{2,1,0:T(8,128)}, bf16[4,8,512,768]{3,2,1,0:T(8,128)(2,1)}) custom-call(s32[4]{0:T(128)S(1)} %get-tuple-element.575.at_ref, bf16[128,128]{1,0:T(8,128)(2,1)S(1)} %copy.161.low_ref, bf16[8,768,128]{2,1,0:T(8,128)(2,1)S(1)} %copy-done.17, ...), custom_call_target="tpu_custom_call", output_to_operand_aliasing={{0}: (7, {}), {1}: (8, {})} | custom-call | flops 1 | bytes 1 | tf_op jit(solution)/shard_map/embed_piece/pallas_call | solution.py:477
  299.8 33.2 %mlp.1 = (bf16[832,768]{1,0:T(8,128)(2,1)S(1)}, f32[832,768]{1,0:T(8,128)}, bf16[384,3072]{1,0:T(8,128)(2,1)}, bf16[384,3072]{1,0:T(8,128)(2,1)}, bf16[1536,768]...) custom-call(s32[1]{0:T(128)} %bitcast.1.core_ref, bf16[832,768]{1,0:T(8,128)(2,1)} %bitcast.260, ...), custom_call_target="tpu_custom_call" | custom-call | flops 1 | bytes 1 | tf_op jit(solution)/shard_map/mlp/pallas_call | solution.py:1037
  347.9 17.0 %attend_back.1 = (bf16[4,208,2304]{2,1,0:T(8,128)(2,1)S(1)}, f32[1,2304]{1,0:T(1,128)S(1)}) custom-call(bf16[4,208,2304]{2,1,0:T(8,128)(2,1)S(1)} %get-tuple-element.273.joint_ref, bf16[4,208,768]{2,1,0:T(8,128)(2,1)S(1)} %get-tuple-element.287.grad_ref), custom_call_target="tpu_custom_call" | custom-call | flops 1 | bytes 1 | tf_op jit(solution)/shard_map/attend_back/pallas_call | solution.py:748
  440.2 7.7 band_piece.6.refs_6_
  478.1 8.1 fusion.116
  533.5 9.6 %fusion.7 = f32[5632,128]{1,0:T(8,128)} fusion(f32[5632,128]{1,0:T(8,128)} %constant_dynamic-update-slice_fusion.6, f32[4,145,2048]{2,1,0:T(8,128)} %copy-done.80, f32[4,145,2048]{2,1,0:T(8,128)} %copy-done.79, f32[2048]{0:T(1024)S(1)} %copy-done.150, f32[4,145]{1,0:T(4,128)S(1)} %copy-done.154, f32[4,16,128]{2,1,0:T(8,128)S(1)} %bitcast.293, ...), kind=kOutput, calls=%fused_computation.38 | convolution fusion | flops 916418560 | bytes 11359808 | tf_op jit(solution)/shard_map/transpose(jvp(nsf,fk->nsk))/dot_general | solution.py:128
  566.6 12.4 %line_grads.2 = bf16[16,768,128]{2,1,0:T(8,128)(2,1)} custom-call(bf16[128,512]{1,0:T(8,128)(2,1)S(1)} %bitcast.263, bf16[4,208,512]{2,1,0:T(8,128)(2,1)S(1)} %dynamic-slice_bitcast_fusion.1.refs_1_, bf16[4,208,512]{2,1,0:T(8,128)(2,1)S(1)} %get-tuple-element.503.refs_2_, bf16[4,208,512]{2,1,0:T(8,128)(2,1)S(1)} %copy-done.44, ...), custom_call_target="tpu_custom_call" | custom-call | flops 1 | bytes 1 | tf_op jit(solution)/shard_map/line_grads/pallas_call | solution.py:572
  586.6 12.2 %line_grads.3 = bf16[16,768,128]{2,1,0:T(8,128)(2,1)} custom-call(bf16[128,512]{1,0:T(8,128)(2,1)S(1)} %bitcast.264, bf16[4,208,512]{2,1,0:T(8,128)(2,1)S(1)} %dynamic-slice_bitcast_fusion.1.refs_1_, bf16[4,208,512]{2,1,0:T(8,128)(2,1)S(1)} %get-tuple-element.503.refs_2_, bf16[4,208,512]{2,1,0:T(8,128)(2,1)S(1)} %copy-done.44, ...), custom_call_target="tpu_custom_call" | custom-call | flops 1 | bytes 1 | tf_op jit(solution)/shard_map/line_grads/pallas_call | solution.py:572
  607.5 38.6 %collective-permute-done.44 = f32[704,128]{1,0:T(8,128)S(1)} collective-permute-done((f32[704,128]{1,0:T(8,128)S(1)}, f32[704,128]{1,0:T(8,128)S(1)}, u32[]{:S(2)}, u32[]{:S(2)}) %collective-permute-start.44) | collective-permute-done | bytes 360480 | tf_op jit(solution)/shard_map/ppermute | solution.py:140
  649.0 13.9 %pixel_grads.1 = bf16[4,8,208,512]{3,2,1,0:T(8,128)(2,1)S(1)} custom-call(bf16[8,208,768]{2,1,0:T(8,128)(2,1)S(1)} %copy-done.14, bf16[4,8,512,768]{3,2,1,0:T(8,128)(2,1)} %get-tuple-element.352.kernel_ref, f32[8,1,512]{2,1,0:T(1,128)S(1)} %broadcast_in_dim.147.rate_ref), custom_call_target="tpu_custom_call" | custom-call | flops 1 | bytes 1 | tf_op jit(solution)/shard_map/pixel_grads/pallas_call | solution.py:521
  677.0 52.5 %all-reduce.15.cloned.1.call-done = (bf16[96,2304]{1,0:T(8,128)(2,1)}, bf16[96,768]{1,0:T(8,128)(2,1)}, bf16[96,3072]{1,0:T(8,128)(2,1)}, bf16[384,768]{1,0:T(8,128)(2,1)}) async-done(((bf16[96,2304]{1,0:T(8,128)(2,1)}, bf16[96,768]{1,0:T(8,128)(2,1)}, bf16[96,3072]{1,0:T(8,128)(2,1)}, bf16[384,768]{1,0:T(8,128)(2,1)}), (bf16[96,2304]{1,0:T(8,128)(2,1)}, bf16[96,768]{1,0:T(8,128)(2,1)}, ...) | async-done | bytes 1769488 | tf_op jit(solution)/shard_map/psum | solution.py:230
  737.4 10.7 %collective-permute-done.50 = f32[704,128]{1,0:T(8,128)S(1)} collective-permute-done((f32[704,128]{1,0:T(8,128)S(1)}, f32[704,128]{1,0:T(8,128)S(1)}, u32[]{:S(2)}, u32[]{:S(2)}) %collective-permute-start.50) | collective-permute-done | bytes 360480 | tf_op jit(solution)/shard_map/ppermute | solution.py:145
  749.2 10.8 %collective-permute-done.52 = f32[704,128]{1,0:T(8,128)S(1)} collective-permute-done((f32[704,128]{1,0:T(8,128)S(1)}, f32[704,128]{1,0:T(8,128)S(1)}, u32[]{:S(2)}, u32[]{:S(2)}) %collective-permute-start.52) | collective-permute-done | bytes 360480 | tf_op jit(solution)/shard_map/ppermute | solution.py:145
  775.2 14.2 %join_pixels.1 = bf16[4,196,16,256]{3,2,1,0:T(8,128)(2,1)} custom-call(s32[1]{0:T(128)} %bitcast.1.core_ref, bf16[4,4,208,512]{3,2,1,0:T(8,128)(2,1)S(1)} %copy-done.29, bf16[4,4,208,512]{3,2,1,0:T(8,128)(2,1)} %collective-permute-done.53.other_ref), custom_call_target="tpu_custom_call" | custom-call | flops 1 | bytes 1 | tf_op jit(solution)/shard_map/join_pixels/pallas_call | solution.py:409
  819.5 8.4 %maximum_convert_fusion = f32[32,768,128]{2,1,0:T(8,128)} fusion(bf16[16,768,128]{2,1,0:T(8,128)(2,1)} %maximum_select_fusion.1, bf16[16,768,128]{2,1,0:T(8,128)(2,1)} %maximum_select_fusion), kind=kLoop, calls=%fused_computation.4 | loop fusion | flops 6291456 | bytes 18874368 | tf_op jit(solution)/shard_map/convert_element_type | solution.py:1496
  (766 shorter events, 461.7 us)
Async XLA Ops:
  7.3 457.4 %reduce-scatter.5.cloned.1.call-start = ((), (), s32[]{:S(2)}) async-start(), calls=%async_computation.4 | async-start | bytes 2949120 | tf_op jit(solution)/shard_map/reduce_scatter | solution.py:226
  101.8 59.6 %collective-permute-start.10 = (bf16[12,768,128]{2,1,0:T(8,128)(2,1)}, bf16[12,768,128]{2,1,0:T(8,128)(2,1)}, u32[]{:S(2)}, u32[]{:S(2)}) collective-permute-start(bf16[12,768,128]{2,1,0:T(8,128)(2,1)} %get-tuple-element.533), channel_id=1, source_target_pairs={{0,16},{8,24},{16,0},{24,8},{1,17},{9,25},{17,1},{25,9},{2,18},{10... | collective-permute-start | bytes 7077896 | tf_op jit(solution)/shard_map/ppermute | solution.py:140
  102.3 59.1 %collective-permute-start.9 = (bf16[12,768,128]{2,1,0:T(8,128)(2,1)}, bf16[12,768,128]{2,1,0:T(8,128)(2,1)}, u32[]{:S(2)}, u32[]{:S(2)}) collective-permute-start(bf16[12,768,128]{2,1,0:T(8,128)(2,1)} %get-tuple-element.534), channel_id=1, source_target_pairs={{0,8},{8,0},{16,24},{24,16},{1,9},{9,1},{17,25},{25,17},{2,10},{10... | collective-permute-start | bytes 7077896 | tf_op jit(solution)/shard_map/ppermute | solution.py:140
  103.0 58.4 %collective-permute-start.8 = (bf16[8,768,128]{2,1,0:T(8,128)(2,1)}, bf16[8,768,128]{2,1,0:T(8,128)(2,1)}, u32[]{:S(2)}, u32[]{:S(2)}) collective-permute-start(bf16[8,768,128]{2,1,0:T(8,128)(2,1)} %get-tuple-element.506), channel_id=1, source_target_pairs={{2,0},{3,1},{4,6},{5,7},{10,8},{11,9},{12,14},{13,15},{18,16},{19,... | collective-permute-start | bytes 4718600 | tf_op jit(solution)/shard_map/ppermute | solution.py:1215
  107.8 44.9 %collective-permute-start.11 = (bf16[4,208,512]{2,1,0:T(8,128)(2,1)}, bf16[4,208,512]{2,1,0:T(8,128)(2,1)S(1)}, u32[]{:S(2)}, u32[]{:S(2)}) collective-permute-start(bf16[4,208,512]{2,1,0:T(8,128)(2,1)} %dynamic-slice_bitcast_fusion.7), channel_id=1, source_target_pairs={{0,4},{1,5},{2,6},{3,7},{4,0},{5,1},{6,2},{7,3},{8,12},{9,13},{10,... | collective-permute-start | bytes 2555912 | tf_op jit(solution)/shard_map/ppermute | solution.py:145
  170.5 52.9 %collective-permute-start.12 = (bf16[12,768,128]{2,1,0:T(8,128)(2,1)}, bf16[12,768,128]{2,1,0:T(8,128)(2,1)}, u32[]{:S(2)}, u32[]{:S(2)}) collective-permute-start(bf16[12,768,128]{2,1,0:T(8,128)(2,1)} %get-tuple-element.532), channel_id=1, source_target_pairs={{0,8},{8,0},{16,24},{24,16},{1,9},{9,1},{17,25},{25,17},{2,10},{10... | collective-permute-start | bytes 7077896 | tf_op jit(solution)/shard_map/ppermute | solution.py:140
  171.8 52.6 %collective-permute-start.13 = (bf16[12,768,128]{2,1,0:T(8,128)(2,1)}, bf16[12,768,128]{2,1,0:T(8,128)(2,1)}, u32[]{:S(2)}, u32[]{:S(2)}) collective-permute-start(bf16[12,768,128]{2,1,0:T(8,128)(2,1)} %get-tuple-element.531), channel_id=1, source_target_pairs={{0,16},{8,24},{16,0},{24,8},{1,17},{9,25},{17,1},{25,9},{2,18},{10... | collective-permute-start | bytes 7077896 | tf_op jit(solution)/shard_map/ppermute | solution.py:140
  265.1 69.9 %collective-permute-start.20 = (bf16[4,208,512]{2,1,0:T(8,128)(2,1)}, bf16[4,208,512]{2,1,0:T(8,128)(2,1)S(1)}, u32[]{:S(2)}, u32[]{:S(2)}) collective-permute-start(bf16[4,208,512]{2,1,0:T(8,128)(2,1)} %dynamic-slice_bitcast_fusion.3), channel_id=1, source_target_pairs={{0,6},{1,7},{2,4},{3,5},{4,2},{5,3},{6,0},{7,1},{8,14},{9,15},{10,... | collective-permute-start | bytes 2555912 | tf_op jit(solution)/shard_map/ppermute | solution.py:145
  288.9 45.3 %collective-permute-start.21 = (bf16[128,128]{0,1:T(8,128)(2,1)S(1)}, bf16[128,128]{0,1:T(8,128)(2,1)S(1)}, u32[]{:S(2)}, u32[]{:S(2)}) collective-permute-start(bf16[128,128]{0,1:T(8,128)(2,1)S(1)} %pad_maximum_fusion.10), channel_id=1, source_target_pairs={{0,2},{1,3},{2,0},{3,1},{4,6},{5,7},{6,4},{7,5},{8,10},{9,11},{10,... | collective-permute-start | bytes 98312 | tf_op jit(solution)/shard_map/ppermute | solution.py:145
  290.0 44.3 %collective-permute-start.23 = (bf16[128,128]{0,1:T(8,128)(2,1)S(1)}, bf16[128,128]{0,1:T(8,128)(2,1)S(1)}, u32[]{:S(2)}, u32[]{:S(2)}) collective-permute-start(bf16[128,128]{0,1:T(8,128)(2,1)S(1)} %pad_maximum_fusion.10), channel_id=1, source_target_pairs={{0,6},{1,7},{2,4},{3,5},{4,2},{5,3},{6,0},{7,1},{8,14},{9,15},{10,... | collective-permute-start | bytes 98312 | tf_op jit(solution)/shard_map/ppermute | solution.py:145
  375.9 168.6 %reduce-scatter.7.cloned.1.call-start = ((), (), s32[]{:S(2)}) async-start(), calls=%async_computation.5 | async-start | bytes 2949120 | tf_op jit(solution)/shard_map/reduce_scatter | solution.py:226
  380.4 164.2 %reduce-scatter.9.cloned.1.call-start = ((), (), s32[]{:S(2)}) async-start(), calls=%async_computation.6 | async-start | bytes 737280 | tf_op jit(solution)/shard_map/reduce_scatter | solution.py:226
  390.0 57.8 %collective-permute-start.32 = (bf16[384,2304]{1,0:T(8,128)(2,1)}, bf16[384,2304]{1,0:T(8,128)(2,1)}, u32[]{:S(2)}, u32[]{:S(2)}) collective-permute-start(bf16[384,2304]{1,0:T(8,128)(2,1)} %get-tuple-element.305), channel_id=1, source_target_pairs={{0,1},{1,0},{2,3},{3,2},{4,5},{5,4},{6,7},{7,6},{8,9},{9,8},{10,11... | collective-permute-start | bytes 5308424 | tf_op jit(solution)/shard_map/ppermute | solution.py:145
  396.9 67.8 %collective-permute-start.29 = (bf16[4,208,768]{2,1,0:T(8,128)(2,1)}, bf16[4,208,768]{2,1,0:T(8,128)(2,1)}, u32[]{:S(2)}, u32[]{:S(2)}) collective-permute-start(bf16[4,208,768]{2,1,0:T(8,128)(2,1)} %get-tuple-element.354.refs_9_), channel_id=1, source_target_pairs={{0,2},{1,3},{2,0},{3,1},{4,6},{5,7},{6,4},{7,5},{8,10},{9,11},{10,... | collective-permute-start | bytes 3833864 | tf_op jit(solution)/shard_map/ppermute | solution.py:145
  403.9 60.8 %collective-permute-start.30 = (bf16[4,208,768]{2,1,0:T(8,128)(2,1)}, bf16[4,208,768]{2,1,0:T(8,128)(2,1)}, u32[]{:S(2)}, u32[]{:S(2)}) collective-permute-start(bf16[4,208,768]{2,1,0:T(8,128)(2,1)} %get-tuple-element.354.refs_9_), channel_id=1, source_target_pairs={{0,4},{1,5},{2,6},{3,7},{4,0},{5,1},{6,2},{7,3},{8,12},{9,13},{10,... | collective-permute-start | bytes 3833864 | tf_op jit(solution)/shard_map/ppermute | solution.py:145
  464.8 79.8 %reduce-scatter.11.cloned.1.call-start = ((), (), s32[]{:S(2)}) async-start(), calls=%async_computation.7 | async-start | bytes 2211840 | tf_op jit(solution)/shard_map/reduce_scatter | solution.py:226
  474.3 70.2 %collective-permute-start.34 = (bf16[4,208,768]{2,1,0:T(8,128)(2,1)}, bf16[4,208,768]{2,1,0:T(8,128)(2,1)}, u32[]{:S(2)}, u32[]{:S(2)}) collective-permute-start(bf16[4,208,768]{2,1,0:T(8,128)(2,1)} %get-tuple-element.354.refs_9_), channel_id=1, source_target_pairs={{0,6},{1,7},{2,4},{3,5},{4,2},{5,3},{6,0},{7,1},{8,14},{9,15},{10,... | collective-permute-start | bytes 3833864 | tf_op jit(solution)/shard_map/ppermute | solution.py:145
  476.3 68.3 %collective-permute-start.35 = (bf16[4,208,768]{2,1,0:T(8,128)(2,1)}, bf16[4,208,768]{2,1,0:T(8,128)(2,1)}, u32[]{:S(2)}, u32[]{:S(2)}) collective-permute-start(bf16[4,208,768]{2,1,0:T(8,128)(2,1)} %collective-permute-done.29.refs_11_), channel_id=1, source_target_pairs={{0,1},{1,0},{2,3},{3,2},{4,5},{5,4},{6,7},{7,6},{8,9},{9,8},{10,11... | collective-permute-start | bytes 3833864 | tf_op jit(solution)/shard_map/ppermute | solution.py:145
  476.4 68.1 %collective-permute-start.36 = (bf16[4,208,768]{2,1,0:T(8,128)(2,1)}, bf16[4,208,768]{2,1,0:T(8,128)(2,1)}, u32[]{:S(2)}, u32[]{:S(2)}) collective-permute-start(bf16[4,208,768]{2,1,0:T(8,128)(2,1)} %collective-permute-done.30.refs_13_), channel_id=1, source_target_pairs={{0,1},{1,0},{2,3},{3,2},{4,5},{5,4},{6,7},{7,6},{8,9},{9,8},{10,11... | collective-permute-start | bytes 3833864 | tf_op jit(solution)/shard_map/ppermute | solution.py:145
  476.8 252.7 %all-reduce.15.cloned.1.call-start = ((), (), s32[]{:S(2)}) async-start(), calls=%async_computation.8 | async-start | bytes 3538944 | tf_op jit(solution)/shard_map/psum | solution.py:230
  601.7 61.3 %collective-permute-start.43 = (bf16[8,768,128]{2,1,0:T(8,128)(2,1)}, bf16[8,768,128]{2,1,0:T(8,128)(2,1)S(1)}, u32[]{:S(2)}, u32[]{:S(2)}) collective-permute-start(bf16[8,768,128]{2,1,0:T(8,128)(2,1)} %constant_dynamic-slice_fusion.2), channel_id=1, source_target_pairs={{0,16},{8,24},{16,0},{24,8},{1,17},{9,25},{17,1},{25,9},{2,18},{10... | collective-permute-start | bytes 4718600 | tf_op jit(solution)/shard_map/ppermute | solution.py:140
  604.0 60.1 %collective-permute-start.42 = (bf16[8,768,128]{2,1,0:T(8,128)(2,1)}, bf16[8,768,128]{2,1,0:T(8,128)(2,1)}, u32[]{:S(2)}, u32[]{:S(2)}) collective-permute-start(bf16[8,768,128]{2,1,0:T(8,128)(2,1)} %constant_dynamic-slice_fusion.3), channel_id=1, source_target_pairs={{0,8},{8,0},{16,24},{24,16},{1,9},{9,1},{17,25},{25,17},{2,10},{10... | collective-permute-start | bytes 4718600 | tf_op jit(solution)/shard_map/ppermute | solution.py:140
  667.2 62.3 %collective-permute-start.47 = (bf16[4,768,128]{2,1,0:T(8,128)(2,1)}, bf16[4,768,128]{2,1,0:T(8,128)(2,1)}, u32[]{:S(2)}, u32[]{:S(2)}) collective-permute-start(bf16[4,768,128]{2,1,0:T(8,128)(2,1)} %constant_dynamic-slice_fusion), channel_id=1, source_target_pairs={{0,8},{8,0},{16,24},{24,16},{1,9},{9,1},{17,25},{25,17},{2,10},{10... | collective-permute-start | bytes 2359304 | tf_op jit(solution)/shard_map/ppermute | solution.py:140
  672.6 56.9 %collective-permute-start.46 = (bf16[4,768,128]{2,1,0:T(8,128)(2,1)}, bf16[4,768,128]{2,1,0:T(8,128)(2,1)}, u32[]{:S(2)}, u32[]{:S(2)}) collective-permute-start(bf16[4,768,128]{2,1,0:T(8,128)(2,1)} %constant_dynamic-slice_fusion.1), channel_id=1, source_target_pairs={{0,16},{8,24},{16,0},{24,8},{1,17},{9,25},{17,1},{25,9},{2,18},{10... | collective-permute-start | bytes 2359304 | tf_op jit(solution)/shard_map/ppermute | solution.py:140
  (249 other events, 2946.5 us)
Sparse Core Ops, SparseCore 0:
  376.1 40.9 reduce-scatter.4
  420.6 37.3 reduce-scatter.6
  464.9 25.1 reduce-scatter.8
  493.8 32.4 reduce-scatter.10
  647.3 82.0 all-reduce.14

commit v3 on v2

--- a/solution.py
+++ b/solution.py
@@ -96,14 +96,15 @@
         )
         > 0.5
     )
-    projected = jnp.einsum("nsk,kj->nsj", sequence, w_in, precision=high)
-    query_heads = (projected[..., :model_width] + in_bias[0]).reshape(
+    projected = jnp.einsum("nsk,kj->nsj", sequence, w_in[:, model_width:], precision=high)
+    asking = sequence[:, token_rows:]
+    query_heads = (
+        jnp.einsum("nsk,kj->nsj", asking, w_in[:, :model_width], precision=high) + in_bias[0]
+    ).reshape(image_count, -1, head_count, head_size)
+    keyed = projected[..., :model_width].reshape(
         image_count, -1, head_count, head_size
     )
-    keyed = projected[..., model_width : 2 * model_width].reshape(
-        image_count, -1, head_count, head_size
-    )
-    valued = (projected[..., 2 * model_width :] + in_bias[1]).reshape(
+    valued = (projected[..., model_width:] + in_bias[1]).reshape(
         image_count, -1, head_count, head_size
     )
     scores = jnp.einsum("nqhd,nkhd->nhqk", query_heads, keyed, precision=high) * head_size ** (
@@ -115,7 +116,7 @@
         image_count, -1, model_width
     )
     first_out = layer_norm(
-        sequence + jnp.einsum("nsk,kj->nsj", mixed_heads, w_proj, precision=high) + proj_bias,
+        asking + jnp.einsum("nsk,kj->nsj", mixed_heads, w_proj, precision=high) + proj_bias,
         gain_pair[0],
         shifts[0],
         hyper_eps,
@@ -131,8 +132,8 @@
         hyper_eps,
     )
     return (
-        second_out[:, token_rows : token_rows + band_slots] + wave_emb,
-        second_out[:, token_rows + band_slots],
+        second_out[:, :band_slots] + wave_emb,
+        second_out[:, band_slots],
     )
 
 
@@ -183,6 +184,11 @@
         for core in (0, 1)
         if 0 <= at + step < 4
     ]
+    return lax.ppermute(value, "batch", pairs)
+
+
+def line_ends(value):
+    pairs = [(2 + at, at) for at in range(2)] + [(4 + at, 6 + at) for at in range(2)]
     return lax.ppermute(value, "batch", pairs)
 
 
@@ -361,7 +367,7 @@
             scratch_shapes=turn_scratch(rows, bands, lanes),
         ),
         out_shape=[side, side],
-        compiler_params=grid_params(40),
+        compiler_params=grid_params(60),
         cost_estimate=pl.CostEstimate(flops=1, bytes_accessed=1, transcendentals=0),
         name="split_pixels",
     )(core.reshape(1), pixels.transpose(0, 2, 1, 3), means[:, :, None], rates[:, :, None])
@@ -416,7 +422,7 @@
             scratch_shapes=turn_scratch(rows, bands, lanes),
         ),
         out_shape=jax.ShapeDtypeStruct((images, patches, bands, lanes), jnp.bfloat16),
-        compiler_params=grid_params(40),
+        compiler_params=grid_params(60),
         cost_estimate=pl.CostEstimate(flops=1, bytes_accessed=1, transcendentals=0),
         name="join_pixels",
     )(core.reshape(1), mine, other)
@@ -501,7 +507,7 @@
             jax.ShapeDtypeStruct((pieces, images, lanes, width), jnp.bfloat16),
         ],
         input_output_aliases={} if first else {4 + count: 0, 5 + count: 1},
-        compiler_params=grid_params(48),
+        compiler_params=grid_params(60),
         cost_estimate=pl.CostEstimate(flops=1, bytes_accessed=1, transcendentals=0),
         name="embed_piece",
     )(place, low, *weights, *pixels, *(() if first else (total, kernels)))
@@ -528,7 +534,7 @@
         ],
         out_specs=pl.BlockSpec((1, share, rows, lanes), lambda i, j: (j, i, 0, 0)),
         out_shape=jax.ShapeDtypeStruct((pieces, images, rows, lanes), jnp.bfloat16),
-        compiler_params=grid_params(40, 2),
+        compiler_params=grid_params(60, 2),
         cost_estimate=pl.CostEstimate(flops=1, bytes_accessed=1, transcendentals=0),
         name="pixel_grads",
     )(grads, kernels, rates)
@@ -575,7 +581,7 @@
         out_specs=vmem,
         out_shape=jax.ShapeDtypeStruct((step_cells, width, depth), jnp.bfloat16),
         scratch_shapes=[pltpu.VMEM((step_cells, images * bands, width), jnp.bfloat16)],
-        compiler_params=pltpu.CompilerParams(vmem_limit_bytes=48 * 1024 * 1024),
+        compiler_params=pltpu.CompilerParams(vmem_limit_bytes=60 * 1024 * 1024),
         cost_estimate=pl.CostEstimate(flops=1, bytes_accessed=1, transcendentals=0),
         name="line_grads",
     )(low_turned, *pixels, *grads)
@@ -651,7 +657,7 @@
             ],
         ),
         out_shape=jax.ShapeDtypeStruct((images * bands, depth), jnp.float32),
-        compiler_params=grid_params(40),
+        compiler_params=grid_params(60),
         cost_estimate=pl.CostEstimate(flops=1, bytes_accessed=1, transcendentals=0),
         name="band_piece",
     )(place, grads, *weights, *pixels, *(() if first else (total,)))
@@ -694,7 +700,7 @@
         in_specs=[pl.BlockSpec((1, rows, triple), lambda i: (i, 0, 0))],
         out_specs=pl.BlockSpec((1, rows, width), lambda i: (i, 0, 0)),
         out_shape=jax.ShapeDtypeStruct((images, rows, width), jnp.bfloat16),
-        compiler_params=grid_params(24),
+        compiler_params=grid_params(60),
         cost_estimate=pl.CostEstimate(flops=1, bytes_accessed=1, transcendentals=0),
         name="attend",
     )(joint)
@@ -760,7 +766,7 @@
             jax.ShapeDtypeStruct((images, rows, triple), jnp.bfloat16),
             jax.ShapeDtypeStruct((1, triple), jnp.float32),
         ],
-        compiler_params=grid_params(24),
+        compiler_params=grid_params(60),
         cost_estimate=pl.CostEstimate(flops=1, bytes_accessed=1, transcendentals=0),
         name="attend_back",
     )(joint, grads)
@@ -772,7 +778,7 @@
     return center * factor, factor
 
 
-def small_call(kernel, name, grid, in_specs, out_specs, out_shape, scratch=(), limit=40):
+def small_call(kernel, name, grid, in_specs, out_specs, out_shape, scratch=(), limit=60):
     return pl.pallas_call(
         kernel,
         grid=grid,
@@ -976,7 +982,7 @@
             scratch_shapes=[pltpu.VMEM((width, rows), jnp.bfloat16)],
         ),
         out_shape=[half, half],
-        compiler_params=grid_params(32),
+        compiler_params=grid_params(60),
         cost_estimate=pl.CostEstimate(flops=1, bytes_accessed=1, transcendentals=0),
         name="rows_grad",
     )(core.reshape(1), left, right)
@@ -1063,10 +1069,38 @@
             down_half,
             jax.ShapeDtypeStruct((1, hidden), jnp.float32),
         ],
-        compiler_params=grid_params(52),
+        compiler_params=grid_params(60),
         cost_estimate=pl.CostEstimate(flops=1, bytes_accessed=1, transcendentals=0),
         name="mlp",
     )(core.reshape(1), normed, residual, grads, up, up_bias[None], down, down_bias[None])
+
+
+def assemble_kernel(bits_ref, one_mine, one_came, two_mine, two_came, out_ref):
+    for at, ref in enumerate((one_mine, one_came, two_mine, two_came)):
+
+        @pl.when(pl.program_id(0) == at)
+        def _(ref=ref):
+            out_ref[...] = ref[...].astype(jnp.float32)
+
+
+def assemble(bits, one_mine, one_came, two_mine, two_came):
+    cells, width, depth = one_mine.shape
+    whole = pl.BlockSpec((cells, width, depth), lambda t, bits: (0, 0, 0))
+    return pl.pallas_call(
+        assemble_kernel,
+        grid_spec=pltpu.PrefetchScalarGridSpec(
+            num_scalar_prefetch=1,
+            grid=(4,),
+            in_specs=[whole] * 4,
+            out_specs=pl.BlockSpec(
+                (cells, width, depth), lambda t, bits: (t // 2 * 2 + (bits[t // 2] ^ (t % 2)), 0, 0)
+            ),
+        ),
+        out_shape=jax.ShapeDtypeStruct((4 * cells, width, depth), jnp.float32),
+        compiler_params=grid_params(60),
+        cost_estimate=pl.CostEstimate(flops=1, bytes_accessed=1, transcendentals=0),
+        name="assemble",
+    )(bits, one_mine, one_came, two_mine, two_came)
 
 
 def per_device(
@@ -1212,11 +1246,7 @@
             mine, other, chip_low, right2, left2, beside1, above1
         )
         block2 = jnp.where(chip == 0, right2, jnp.where(chip == 3, left2, left1))
-        end3 = lax.ppermute(
-            jnp.where(chip == 1, right2, left2),
-            "batch",
-            [(2 + at, at) for at in range(2)] + [(4 + at, 6 + at) for at in range(2)],
-        )
+        end3 = line_ends(jnp.where(chip == 1, right2, left2))
         across2, up2 = sides_and_corner(block2, beside1, above1)
         chip_pixels = (mine, swap_batch(other, 1))
         pixels2 = [pixel_block(2, 0)]
@@ -1308,9 +1338,7 @@
     share_down = row_share(add_low(down_keep, down_came))
 
     def late_rows(attended, grad_branch, normed1, grad_joint):
-        out_keep, out_send = rows_grad(core, attended, grad_branch)
-        qkv_keep, qkv_send = rows_grad(core, normed1, grad_joint)
-        return core_sum(out_keep, out_send), core_sum(qkv_keep, qkv_send)
+        return rows_grad(core, attended, grad_branch), rows_grad(core, normed1, grad_joint)
 
     late = (
         attended,
@@ -1320,7 +1348,7 @@
     )
     beside_emb = swap_batch(grad_emb, 1)
     if tuned_mesh():
-        far_emb = [swap_batch(grad_emb, 2), swap_batch(grad_emb, 4)]
+        right1, left1 = (along_line(grad_emb, -1), along_line(grad_emb, 1))
     grad_bias_weight = jnp.einsum("ik,ie->ke", bias_vec, grad_image_bias, precision=highest)
     grad_bias_offset = jnp.sum(grad_image_bias, axis=0)
     grad_bias_vec = jnp.einsum("ie,ke->ik", grad_image_bias, bias_weight, precision=highest)
@@ -1380,28 +1408,33 @@
             (place(spots2, group, group ^ 1, group ^ 2, group ^ 3), weights2),
             (place(spots3, group, group ^ 1, group ^ 2, group ^ 3), weights3),
         ]
-        for spots, weights in plan:
+        for spots, weights in plan[:2]:
             grad_vectors = band_piece(spots, chip_emb, weights, chip_pixels, grad_vectors)
-        half_out, half_qkv = late_rows(*late)
-        grad_vectors, far_emb, half_out, half_qkv, grad_emb, share_up = tie(
-            grad_vectors, far_emb, half_out, half_qkv, grad_emb, share_up
-        )
-        far_emb.append(swap_batch(grad_emb, 6))
+        grad_vectors, right1, left1, beside_emb, share_up, late = tie(
+            grad_vectors, right1, left1, beside_emb, share_up, late
+        )
+        right2, left2 = (along_line(right1, -1, (1, 2)), along_line(left1, 1, (1, 2)))
+        pair_out, pair_qkv = late_rows(*late)
+        far = jnp.where((chip & 1) == 0, right1, left1)
+        line_emb = [grad_emb, beside_emb, far, swap_batch(far, 1)]
+        for spots, weights in plan[2:]:
+            grad_vectors = band_piece(spots, chip_emb, weights, chip_pixels, grad_vectors)
+        grad_vectors, right2, left2, line_emb, share_down, pair_out, pair_qkv = tie(
+            grad_vectors, right2, left2, line_emb, share_down, pair_out, pair_qkv
+        )
+        half_out, half_qkv = core_sum(*pair_out), core_sum(*pair_qkv)
         share_out_rows, share_qkv = row_share(half_out), row_share(half_qkv)
-        line_emb = [grad_emb, beside_emb]
-        for far in far_emb[:2]:
-            line_emb += [far, swap_batch(far, 1)]
+        end3 = line_ends(jnp.where(chip == 1, right2, left2))
+        far = jnp.where(chip < 2, right2, left2)
+        line_emb += [far, swap_batch(far, 1)]
         hyper_grads = finish_low(grad_vectors)
         wide, narrow, parts, small = pack(hyper_grads)
-        (
-            small, block_out, far_emb, line_emb, share_up, share_down, share_out_rows, share_qkv,
-            chip_emb,
-        ) = tie(
-            small, block_out, far_emb, line_emb, share_up, share_down, share_out_rows, share_qkv,
-            chip_emb,
+        small, block_out, end3, line_emb, chip_emb = tie(
+            small, block_out, end3, line_emb, chip_emb
         )
         small_came = swap_batch(part_of(small, 1 - core, 2), 1)
-        line_emb += [far_emb[2], swap_batch(far_emb[2], 1)]
+        far = jnp.where(chip == 1, right1, jnp.where(chip == 2, left1, end3))
+        line_emb += [far, swap_batch(far, 1)]
         small, small_came, line_emb = tie(small, small_came, line_emb)
         line_pixels = [pixel_block(0, 0), pixel_block(0, 1)] + pixels1 + pixels2 + pixels3
     else:
@@ -1409,7 +1442,7 @@
             grad_vectors = band_piece(
                 place(at, 0, 1, 2, 3), chip_emb, [weight], chip_pixels, grad_vectors
             )
-        half_out, half_qkv = late_rows(*late)
+        half_out, half_qkv = [core_sum(*pair) for pair in late_rows(*late)]
         hyper_grads = finish_low(grad_vectors)
         wide, narrow, parts, small = pack(hyper_grads)
         share_out_rows, share_qkv = row_share(half_out), row_share(half_qkv)
@@ -1439,25 +1472,32 @@
         small = part_of(small, core, 2) + small_came
         small_came = [swap_batch(part_of(small, chip ^ hop, 4), 2 * hop) for hop in (1, 2, 3)]
         kernel_one = line_grads(low_turned, cells, line_pixels, line_emb, 0, 2)
-        kernel_one, line_emb, small_came = tie(kernel_one, line_emb, small_came)
-
+        mine_up, mine_down = row_mine(share_up), row_mine(share_down)
+        kernel_one, line_emb, small_came, mine_up, mine_down, share_qkv, share_out_rows = tie(
+            kernel_one, line_emb, small_came, mine_up, mine_down, share_qkv, share_out_rows
+        )
+
+        small = sum(small_came, part_of(small, chip, 4))
+        small_came = swap_group(small, 1)
         kernel_two = line_grads(low_turned, cells, line_pixels, line_emb, 1, 2)
+        kernel_two, small_came = tie(kernel_two, small_came)
+
         sums = [kernel_one, kernel_two]
         came = sum_out(sums, False)
-        small = sum(small_came, part_of(small, chip, 4))
-        small = small + swap_group(small, 1)
-        (small,) = tie(small)
+        small = small + small_came
         small_came = swap_group(small, 2)
+        mine_qkv, mine_out = row_mine(share_qkv), row_mine(share_out_rows)
         chip_back = pixel_grads(chip_emb, kernels, rates)
-        totals = [row_mine(share) for share in (share_qkv, share_out_rows, share_up, share_down)]
-        chip_back, came, small, small_came = tie(chip_back, came, small, small_came)
+        chip_back, came, small_came, mine_qkv, mine_out = tie(
+            chip_back, came, small_came, mine_qkv, mine_out
+        )
 
         sums = sum_in(sums, came, False)
         came = sum_out(sums, True)
         small = small + small_came
         small_came = [swap_batch(small, 2 * hop) for hop in (1, 2, 3)]
         own_back, other_back = chip_back[:, :images], chip_back[:, images:]
-        came, own_back, other_back, totals = tie(came, own_back, other_back, totals)
+        came, own_back, other_back = tie(came, own_back, other_back)
 
         sums = sum_in(sums, came, True)
         came = share_out(sums, True)
@@ -1471,7 +1511,7 @@
         pixel_grad = join_pixels(
             own_back, other_back, core, patches, cells, pixel_cells, band_slots
         )
-        (totals,) = tie(totals)
+        totals = [mine_qkv, mine_out, mine_up, mine_down]
         widths = [mine.shape[1] for mine in totals[:3]]
         wide_mine = jnp.concatenate(totals[:3], axis=1)
         wide_both = row_both(wide_mine)
@@ -1493,7 +1533,8 @@
         came, pixel_grad, found, totals, batch_mean, batch_var = tie(
             came, pixel_grad, found, totals, batch_mean, batch_var
         )
-        kernel_total = jnp.concatenate(share_in(sums, came, False)).astype(jnp.float32)
+        bits = jnp.stack([group & 1, group >> 1])
+        kernel_total = assemble(bits, sums[0], came[0], sums[1], came[1])
     return (
         block_out,
         pixel_grad,

time: 848 us -> 827 us (0.975)
  Pallas kernels: 253 us -> 304 us
  local copies, waits for them, and re-layouts: 157 us -> 118 us
  matrix products: 61 us -> 31 us
  other arithmetic: 94.5 us -> 76.6 us
  waiting for transfers between devices: 176 us -> 187 us
    unnamed x428 -> x318, local copies, waits for them, and re-layouts: 66.8 us -> 24.8 us
    reduce_scatter x4, waiting for transfers between devices: 0.02 us -> 40.3 us  [row_share(): return lax.psum_scatter(half, 'group', scatter_dimension=0, tiled=True)]
    psum x1 -> x2, waiting for transfers between devices: 52.5 us -> 20.5 us  [row_mine(): return lax.psum(share, 'batch', axis_index_groups=same_core())]
    ppermute x18, waiting for transfers between devices: 55.2 us -> 33.8 us  [swap_group(): return lax.ppermute(value, 'group', [(at, at ^ bits) for at in range(4)])]
    ppermute x4 -> x8, waiting for transfers between devices: 10.7 us -> 29.9 us  [along_line(): return lax.ppermute(value, 'batch', pairs)]
    ppermute x1 -> x2, waiting for transfers between devices: 8.73 us -> 27.7 us  [line_ends(): return lax.ppermute(value, 'batch', pairs)]
    dot_general x3, matrix products: 20.2 us -> 5.47 us  [hypernet(): jnp.einsum('nsf,fk->nsk', inner_act, w_reduce, precision=high)]
    ppermute x36 -> x33, waiting for transfers between devices: 48.5 us -> 34.6 us  [swap_batch(): lax.ppermute(value, 'batch', [(at, at ^ bits) for at in range(count)])]
  transfers between devices with their start and end apart: 64 -> 67, of which waited for: 19 -> 25; matrix products, arithmetic and copies ran while one was open for 25% -> 22% of each run, Pallas kernels for 28% -> 35%
where the time goes in v3:
time: 827 us; the launch traced here: 815 us
  Pallas kernels  304 us (37%)
  waiting for transfers between devices  187 us (23%)
  local copies, waits for them, and re-layouts  118 us (14%)
  starting transfers between devices  82.7 us (10%)
  other arithmetic  76.6 us (9%)
  matrix products  31 us (4%)
  between operations  16.6 us (2%)
    pallas_call x7, Pallas kernels, embed_piece(): pl.pallas_call(partial(embed_kernel, first, count), grid_spec=pltpu.Prefe...  73.8 us
    reduce_scatter x4, waiting for transfers between devices, row_share(): return lax.psum_scatter(half, 'group', scatter_dimension=0, tiled=True)  40.3 us
    pallas_call x4, Pallas kernels, band_piece(): pl.pallas_call(partial(band_kernel, first, count), grid_spec=pltpu.Prefet...  39.1 us
    ppermute x33, starting transfers between devices, swap_batch(): lax.ppermute(value, 'batch', [(at, at ^ bits) for at in range(count)])  37.5 us
    ppermute x33, waiting for transfers between devices, swap_batch(): lax.ppermute(value, 'batch', [(at, at ^ bits) for at in range(count)])  34.6 us
    ppermute x18, waiting for transfers between devices, swap_group(): return lax.ppermute(value, 'group', [(at, at ^ bits) for at in range(4)])  33.8 us
    pallas_call x1, Pallas kernels, mlp(): pl.pallas_call(mlp_kernel, grid_spec=pltpu.PrefetchScalarGridSpec(num_sca...  33.7 us
    ppermute x8, waiting for transfers between devices, along_line(): return lax.ppermute(value, 'batch', pairs)  29.9 us
  transfers between devices with their start and end apart: 67, of which 25 were waited for; matrix products, arithmetic and copies ran while one was open for 22% of the time, Pallas kernels for 35%

profile of v3, /device:TPU:0, one launch (start us, length us, event | category | flops | bytes accessed | tf_op | source)
XLA Modules:
  0.0 815.1 jit_solution(15603741131935176496)
XLA Ops:
  27.6 22.4 %collective-permute-done = bf16[8,768,128]{2,1,0:T(8,128)(2,1)} collective-permute-done((bf16[8,768,128]{2,1,0:T(8,128)(2,1)}, bf16[8,768,128]{2,1,0:T(8,128)(2,1)}, u32[]{:S(2)}, u32[]{:S(2)}) %collective-permute-start) | collective-permute-done | bytes 1572896 | tf_op jit(solution)/shard_map/ppermute | solution.py:187
  61.8 17.0 %split_pixels.1 = (bf16[4,4,208,512]{3,2,1,0:T(8,128)(2,1)}, bf16[4,4,208,512]{3,2,1,0:T(8,128)(2,1)}) custom-call(s32[1]{0:T(128)} %bitcast.1.core_ref, bf16[4,196,16,256]{3,2,1,0:T(8,128)(2,1)} %bitcast.258, f32[4,16,1]{2,1,0:T(8,128)} %convolution_bitcast_fusion.7.mean_ref, f32[4,16,1]{2,1,0:T(8,128)} %copy.149.rate_ref), custom_call_target="tpu_custom_call" | custom-call | flops 1 | bytes 1 | tf_op jit(solution)/shard_map/split_pixels/pallas_call | solution.py:356
  78.8 9.3 %collective-permute-done.5.refs_1_ = bf16[8,768,128]{2,1,0:T(8,128)(2,1)} collective-permute-done((bf16[8,768,128]{2,1,0:T(8,128)(2,1)S(1)}, bf16[8,768,128]{2,1,0:T(8,128)(2,1)}, u32[]{:S(2)}, u32[]{:S(2)}) %collective-permute-start.5) | collective-permute-done | bytes 1572896 | tf_op jit(solution)/shard_map/ppermute | solution.py:141
  125.8 12.0 %embed_piece.7 = (f32[8,208,768]{2,1,0:T(8,128)}, bf16[4,8,512,768]{3,2,1,0:T(8,128)(2,1)}) custom-call(s32[5]{0:T(128)} %stack.90.at_ref, bf16[128,128]{1,0:T(8,128)(2,1)} %copy.159.low_ref, bf16[32,768,128]{2,1,0:T(8,128)(2,1)} %refs_0_.3, bf16[4,4,208,512]{3,2,1,0:T(8,128)(2,1)} %get-tuple-element.308.refs_1_.refs_3_.refs_4_, ...), custom_call_target="tpu_custom_call" | custom-call | flops 1 | bytes 1 | tf_op jit(solution)/shard_map/embed_piece/pallas_call | solution.py:483
  137.8 12.5 %embed_piece.8 = (f32[8,208,768]{2,1,0:T(8,128)}, bf16[4,8,512,768]{3,2,1,0:T(8,128)(2,1)}) custom-call(s32[4]{0:T(128)} %add_add_fusion.4.at_ref, bf16[128,128]{1,0:T(8,128)(2,1)} %copy.159.low_ref, bf16[8,768,128]{2,1,0:T(8,128)(2,1)} %copy-done.8, ...), custom_call_target="tpu_custom_call", output_to_operand_aliasing={{0}: (7, {}), {1}: (8, {})} | custom-call | flops 1 | bytes 1 | tf_op jit(solution)/shard_map/embed_piece/pallas_call | solution.py:483
  200.8 12.5 %embed_piece.10 = (f32[8,208,768]{2,1,0:T(8,128)}, bf16[4,8,512,768]{3,2,1,0:T(8,128)(2,1)}) custom-call(s32[4]{0:T(128)} %get-tuple-element.597.at_ref, bf16[128,128]{1,0:T(8,128)(2,1)} %copy.159.low_ref, bf16[8,768,128]{2,1,0:T(8,128)(2,1)} %copy-done.2, ...), custom_call_target="tpu_custom_call", output_to_operand_aliasing={{0}: (7, {}), {1}: (8, {})} | custom-call | flops 1 | bytes 1 | tf_op jit(solution)/shard_map/embed_piece/pallas_call | solution.py:483
  242.7 12.9 %embed_piece.12 = (f32[8,208,768]{2,1,0:T(8,128)}, bf16[4,8,512,768]{3,2,1,0:T(8,128)(2,1)}) custom-call(s32[4]{0:T(128)} %get-tuple-element.596.at_ref, bf16[128,128]{1,0:T(8,128)(2,1)} %copy.159.low_ref, bf16[8,768,128]{2,1,0:T(8,128)(2,1)} %copy-done.3, bf16[12,768,128]{2,1,0:T(8,128)(2,1)} %copy-done.7, ...), custom_call_target="tpu_custom_call", output_to_operand_aliasing={{0}: (7, {}), {1}: (8, {})} | custom-call | flops 1 | bytes 1 | tf_op jit(solution)/shard_map/embed_piece/pallas_call | solution.py:483
  278.9 9.1 %make_joint.1 = (f32[4,208,768]{2,1,0:T(8,128)}, bf16[4,208,768]{2,1,0:T(8,128)(2,1)}, bf16[4,208,2304]{2,1,0:T(8,128)(2,1)}) custom-call(f32[8,208,768]{2,1,0:T(8,128)} %get-tuple-element.280.own_ref, f32[4,208,768]{2,1,0:T(8,128)} %collective-permute-done.19.beside_ref, f32[4,1,768]{2,1,0:T(1,128)} %broadcast_in_dim.126.bias_ref, ...), custom_call_target="tpu_custom_call" | custom-call | flops 1 | bytes 1 | tf_op jit(solution)/shard_map/make_joint/pallas_call | solution.py:819
  308.2 33.7 %mlp.1 = (bf16[832,768]{1,0:T(8,128)(2,1)}, f32[832,768]{1,0:T(8,128)}, bf16[384,3072]{1,0:T(8,128)(2,1)}, bf16[384,3072]{1,0:T(8,128)(2,1)}, bf16[1536,768]{1,0...) custom-call(s32[1]{0:T(128)} %bitcast.1.core_ref, bf16[832,768]{1,0:T(8,128)(2,1)} %bitcast.278, ...), custom_call_target="tpu_custom_call" | custom-call | flops 1 | bytes 1 | tf_op jit(solution)/shard_map/mlp/pallas_call | solution.py:1043
  354.8 19.2 %attend_back.1 = (bf16[4,208,2304]{2,1,0:T(8,128)(2,1)}, f32[1,2304]{1,0:T(1,128)}) custom-call(bf16[4,208,2304]{2,1,0:T(8,128)(2,1)} %get-tuple-element.282.joint_ref, bf16[4,208,768]{2,1,0:T(8,128)(2,1)} %get-tuple-element.296.grad_ref), custom_call_target="tpu_custom_call" | custom-call | flops 1 | bytes 1 | tf_op jit(solution)/shard_map/attend_back/pallas_call | solution.py:754
  374.0 10.3 %embed_back.1 = (bf16[4,208,768]{2,1,0:T(8,128)(2,1)}, f32[2,768]{1,0:T(2,128)}, f32[4,1,768]{2,1,0:T(1,128)}) custom-call(bf16[4,208,2304]{2,1,0:T(8,128)(2,1)} %get-tuple-element.297.joint_ref, bf16[768,2304]{1,0:T(8,128)(2,1)} %weight_ref.7, f32[4,208,768]{2,1,0:T(8,128)} %get-tuple-element.284.embedded_ref, f32[4,208,768]{2,1,0:T(8,128)} %get-tuple-element.298.resid_ref, ...), custom_call_target="tpu_custom_call" | custom-call | flops 1 | bytes 1 | tf_op jit(solution)/shard_map/embed_back/pallas_call | solution.py:932
  416.3 10.1 %band_piece.5.refs_6_ = f32[128,128]{1,0:T(8,128)} custom-call(s32[5]{0:T(128)} %stack.96.at_ref, bf16[8,208,768]{2,1,0:T(8,128)(2,1)} %copy-done.1, bf16[8,768,128]{2,1,0:T(8,128)(2,1)} %copy-done.8, bf16[8,768,128]{2,1,0:T(8,128)(2,1)} %collective-permute-done.5.refs_1_, bf16[8,768,128]{2,1,0:T(8,128)(2,1)} %collective-permute-done.6.refs_2_, ...), custom_call_target="tpu_custom_call" | custom-call | flops 1 | bytes 1 | tf_op jit(solution)/shard_map/band_piece/pallas_call | solution.py:639
  452.8 10.1 %band_piece.6.refs_6_ = f32[128,128]{1,0:T(8,128)} custom-call(s32[5]{0:T(128)} %stack.95.at_ref, bf16[8,208,768]{2,1,0:T(8,128)(2,1)} %copy-done.1, bf16[8,768,128]{2,1,0:T(8,128)(2,1)} %copy-done.2, bf16[12,768,128]{2,1,0:T(8,128)(2,1)} %collective-permute-done.9.refs_1_, bf16[12,768,128]{2,1,0:T(8,128)(2,1)} %copy-done.6, ...), custom_call_target="tpu_custom_call" | custom-call | flops 1 | bytes 1 | tf_op jit(solution)/shard_map/band_piece/pallas_call | solution.py:639
  467.1 10.1 %band_piece.7 = f32[128,128]{1,0:T(8,128)} custom-call(s32[5]{0:T(128)} %stack.94.at_ref, bf16[8,208,768]{2,1,0:T(8,128)(2,1)} %copy-done.1, bf16[8,768,128]{2,1,0:T(8,128)(2,1)} %copy-done.3, bf16[12,768,128]{2,1,0:T(8,128)(2,1)} %copy-done.7, bf16[12,768,128]{2,1,0:T(8,128)(2,1)} %collective-permute-done.13.refs_2_, bf16[8,768,128]{2,1,0:T(8,128)(2,1)} %copy-done.14, ...), custom_call_target="tpu_custom_call" | custom-call | flops 1 | bytes 1 | tf_op jit(solution)/shard_map/band_piece/pallas_call | solution.py:639
  530.7 20.8 %collective-permute-done.35 = bf16[4,208,768]{2,1,0:T(8,128)(2,1)} collective-permute-done((bf16[4,208,768]{2,1,0:T(8,128)(2,1)}, bf16[4,208,768]{2,1,0:T(8,128)(2,1)}, u32[]{:S(2)}, u32[]{:S(2)}) %collective-permute-start.35) | collective-permute-done | bytes 1277984 | tf_op jit(solution)/shard_map/ppermute | solution.py:192
  568.8 13.9 %line_grads.2 = bf16[16,768,128]{2,1,0:T(8,128)(2,1)} custom-call(bf16[128,512]{1,0:T(8,128)(2,1)} %bitcast.281, bf16[4,208,512]{2,1,0:T(8,128)(2,1)} %dynamic-slice_bitcast_fusion.1.refs_1_, bf16[4,208,512]{2,1,0:T(8,128)(2,1)} %get-tuple-element.523.refs_2_, bf16[4,208,512]{2,1,0:T(8,128)(2,1)} %collective-permute-done.14.refs_3_, ...), custom_call_target="tpu_custom_call" | custom-call | flops 1 | bytes 1 | tf_op jit(solution)/shard_map/line_grads/pallas_call | solution.py:578
  589.9 34.6 %reduce-scatter.9.cloned.1.call-done = bf16[96,2304]{1,0:T(8,128)(2,1)} async-done(((bf16[384,2304]{1,0:T(8,128)(2,1)}), bf16[96,2304]{1,0:T(8,128)(2,1)}) %reduce-scatter.9.cloned.1.call-update) | async-done | bytes 442384 | tf_op jit(solution)/shard_map/reduce_scatter | solution.py:232
  630.4 13.8 %line_grads.3 = bf16[16,768,128]{2,1,0:T(8,128)(2,1)} custom-call(bf16[128,512]{1,0:T(8,128)(2,1)} %bitcast.282, bf16[4,208,512]{2,1,0:T(8,128)(2,1)} %dynamic-slice_bitcast_fusion.1.refs_1_, bf16[4,208,512]{2,1,0:T(8,128)(2,1)} %get-tuple-element.523.refs_2_, bf16[4,208,512]{2,1,0:T(8,128)(2,1)} %collective-permute-done.14.refs_3_, ...), custom_call_target="tpu_custom_call" | custom-call | flops 1 | bytes 1 | tf_op jit(solution)/shard_map/line_grads/pallas_call | solution.py:578
  650.8 16.9 %pixel_grads.1 = bf16[4,8,208,512]{3,2,1,0:T(8,128)(2,1)} custom-call(bf16[8,208,768]{2,1,0:T(8,128)(2,1)} %copy-done.1, bf16[4,8,512,768]{3,2,1,0:T(8,128)(2,1)} %get-tuple-element.375.kernel_ref, f32[8,1,512]{2,1,0:T(1,128)} %broadcast_in_dim.147.rate_ref), custom_call_target="tpu_custom_call" | custom-call | flops 1 | bytes 1 | tf_op jit(solution)/shard_map/pixel_grads/pallas_call | solution.py:527
  667.7 20.5 %all-reduce.19.cloned.1.call-done = (bf16[96,2304]{1,0:T(8,128)(2,1)}, bf16[96,768]{1,0:T(8,128)(2,1)}) async-done(((bf16[96,2304]{1,0:T(8,128)(2,1)}, bf16[96,768]{1,0:T(8,128)(2,1)}), (bf16[96,2304]{1,0:T(8,128)(2,1)}, bf16[96,768]{1,0:T(8,128)(2,1)})) %all-reduce.19.cloned.1.call-update) | async-done | bytes 589840 | tf_op jit(solution)/shard_map/psum | solution.py:236
  701.8 10.2 %collective-permute-done.49 = bf16[4,768,128]{2,1,0:T(8,128)(2,1)S(1)} collective-permute-done((bf16[4,768,128]{2,1,0:T(8,128)(2,1)S(1)}, bf16[4,768,128]{2,1,0:T(8,128)(2,1)S(1)}, u32[]{:S(2)}, u32[]{:S(2)}) %collective-permute-start.49) | collective-permute-done | bytes 786464 | tf_op jit(solution)/shard_map/ppermute | solution.py:141
  723.9 10.6 %collective-permute-done.52 = f32[704,128]{1,0:T(8,128)S(1)} collective-permute-done((f32[704,128]{1,0:T(8,128)S(1)}, f32[704,128]{1,0:T(8,128)S(1)}, u32[]{:S(2)}, u32[]{:S(2)}) %collective-permute-start.52) | collective-permute-done | bytes 360480 | tf_op jit(solution)/shard_map/ppermute | solution.py:146
  737.2 9.3 %collective-permute-done.54 = f32[704,128]{1,0:T(8,128)S(1)} collective-permute-done((f32[704,128]{1,0:T(8,128)S(1)}, f32[704,128]{1,0:T(8,128)S(1)}, u32[]{:S(2)}, u32[]{:S(2)}) %collective-permute-start.54) | collective-permute-done | bytes 360480 | tf_op jit(solution)/shard_map/ppermute | solution.py:146
  761.4 14.1 %join_pixels.1 = bf16[4,196,16,256]{3,2,1,0:T(8,128)(2,1)} custom-call(s32[1]{0:T(128)} %bitcast.1.core_ref, bf16[4,4,208,512]{3,2,1,0:T(8,128)(2,1)} %get-tuple-element.401.mine_ref, bf16[4,4,208,512]{3,2,1,0:T(8,128)(2,1)} %collective-permute-done.55.other_ref), custom_call_target="tpu_custom_call" | custom-call | flops 1 | bytes 1 | tf_op jit(solution)/shard_map/join_pixels/pallas_call | solution.py:415
  (675 shorter events, 432.6 us)
Async XLA Ops:
  7.3 421.4 %reduce-scatter.5.cloned.1.call-start = ((), (), s32[]{:S(2)}) async-start(), calls=%async_computation.4 | async-start | bytes 2949120 | tf_op jit(solution)/shard_map/reduce_scatter | solution.py:232
  102.2 59.6 %collective-permute-start.10 = (bf16[12,768,128]{2,1,0:T(8,128)(2,1)}, bf16[12,768,128]{2,1,0:T(8,128)(2,1)S(1)}, u32[]{:S(2)}, u32[]{:S(2)}) collective-permute-start(bf16[12,768,128]{2,1,0:T(8,128)(2,1)} %get-tuple-element.555), channel_id=1, source_target_pairs={{0,16},{8,24},{16,0},{24,8},{1,17},{9,25},{17,1},{25,9},{2,18},{10... | collective-permute-start | bytes 7077896 | tf_op jit(solution)/shard_map/ppermute | solution.py:141
  102.7 59.1 %collective-permute-start.9 = (bf16[12,768,128]{2,1,0:T(8,128)(2,1)}, bf16[12,768,128]{2,1,0:T(8,128)(2,1)}, u32[]{:S(2)}, u32[]{:S(2)}) collective-permute-start(bf16[12,768,128]{2,1,0:T(8,128)(2,1)} %get-tuple-element.556), channel_id=1, source_target_pairs={{0,8},{8,0},{16,24},{24,16},{1,9},{9,1},{17,25},{25,17},{2,10},{10... | collective-permute-start | bytes 7077896 | tf_op jit(solution)/shard_map/ppermute | solution.py:141
  103.4 58.4 %collective-permute-start.8 = (bf16[8,768,128]{2,1,0:T(8,128)(2,1)}, bf16[8,768,128]{2,1,0:T(8,128)(2,1)}, u32[]{:S(2)}, u32[]{:S(2)}) collective-permute-start(bf16[8,768,128]{2,1,0:T(8,128)(2,1)} %get-tuple-element.526), channel_id=1, source_target_pairs={{2,0},{3,1},{4,6},{5,7},{10,8},{11,9},{12,14},{13,15},{18,16},{19,... | collective-permute-start | bytes 4718600 | tf_op jit(solution)/shard_map/ppermute | solution.py:192
  109.9 45.0 %collective-permute-start.11 = (bf16[4,208,512]{2,1,0:T(8,128)(2,1)}, bf16[4,208,512]{2,1,0:T(8,128)(2,1)}, u32[]{:S(2)}, u32[]{:S(2)}) collective-permute-start(bf16[4,208,512]{2,1,0:T(8,128)(2,1)} %dynamic-slice_bitcast_fusion.7), channel_id=1, source_target_pairs={{0,4},{1,5},{2,6},{3,7},{4,0},{5,1},{6,2},{7,3},{8,12},{9,13},{10,... | collective-permute-start | bytes 2555912 | tf_op jit(solution)/shard_map/ppermute | solution.py:146
  170.3 52.8 %collective-permute-start.12 = (bf16[12,768,128]{2,1,0:T(8,128)(2,1)}, bf16[12,768,128]{2,1,0:T(8,128)(2,1)S(1)}, u32[]{:S(2)}, u32[]{:S(2)}) collective-permute-start(bf16[12,768,128]{2,1,0:T(8,128)(2,1)} %get-tuple-element.554), channel_id=1, source_target_pairs={{0,8},{8,0},{16,24},{24,16},{1,9},{9,1},{17,25},{25,17},{2,10},{10... | collective-permute-start | bytes 7077896 | tf_op jit(solution)/shard_map/ppermute | solution.py:141
  171.6 52.6 %collective-permute-start.13 = (bf16[12,768,128]{2,1,0:T(8,128)(2,1)}, bf16[12,768,128]{2,1,0:T(8,128)(2,1)}, u32[]{:S(2)}, u32[]{:S(2)}) collective-permute-start(bf16[12,768,128]{2,1,0:T(8,128)(2,1)} %get-tuple-element.553), channel_id=1, source_target_pairs={{0,16},{8,24},{16,0},{24,8},{1,17},{9,25},{17,1},{25,9},{2,18},{10... | collective-permute-start | bytes 7077896 | tf_op jit(solution)/shard_map/ppermute | solution.py:141
  271.7 70.9 %collective-permute-start.20 = (bf16[4,208,512]{2,1,0:T(8,128)(2,1)S(1)}, bf16[4,208,512]{2,1,0:T(8,128)(2,1)S(1)}, u32[]{:S(2)}, u32[]{:S(2)}) collective-permute-start(bf16[4,208,512]{2,1,0:T(8,128)(2,1)S(1)} %dynamic-slice_bitcast_fusion.3), channel_id=1, source_target_pairs={{0,6},{1,7},{2,4},{3,5},{4,2},{5,3},{6,0},{7,1},{8,14},{9,15},{10,... | collective-permute-start | bytes 2555912 | tf_op jit(solution)/shard_map/ppermute | solution.py:146
  296.8 45.1 %collective-permute-start.21 = (bf16[128,128]{0,1:T(8,128)(2,1)S(1)}, bf16[128,128]{0,1:T(8,128)(2,1)S(1)}, u32[]{:S(2)}, u32[]{:S(2)}) collective-permute-start(bf16[128,128]{0,1:T(8,128)(2,1)S(1)} %pad_maximum_fusion.11), channel_id=1, source_target_pairs={{0,2},{1,3},{2,0},{3,1},{4,6},{5,7},{6,4},{7,5},{8,10},{9,11},{10,... | collective-permute-start | bytes 98312 | tf_op jit(solution)/shard_map/ppermute | solution.py:146
  297.9 44.0 %collective-permute-start.22 = (bf16[128,128]{0,1:T(8,128)(2,1)S(1)}, bf16[128,128]{0,1:T(8,128)(2,1)S(1)}, u32[]{:S(2)}, u32[]{:S(2)}) collective-permute-start(bf16[128,128]{0,1:T(8,128)(2,1)S(1)} %pad_maximum_fusion.11), channel_id=1, source_target_pairs={{0,4},{1,5},{2,6},{3,7},{4,0},{5,1},{6,2},{7,3},{8,12},{9,13},{10,... | collective-permute-start | bytes 98312 | tf_op jit(solution)/shard_map/ppermute | solution.py:146
  298.4 43.6 %collective-permute-start.23 = (bf16[128,128]{0,1:T(8,128)(2,1)S(1)}, bf16[128,128]{0,1:T(8,128)(2,1)S(1)}, u32[]{:S(2)}, u32[]{:S(2)}) collective-permute-start(bf16[128,128]{0,1:T(8,128)(2,1)S(1)} %pad_maximum_fusion.11), channel_id=1, source_target_pairs={{0,6},{1,7},{2,4},{3,5},{4,2},{5,3},{6,0},{7,1},{8,14},{9,15},{10,... | collective-permute-start | bytes 98312 | tf_op jit(solution)/shard_map/ppermute | solution.py:146
  389.4 87.8 %reduce-scatter.7.cloned.1.call-start = ((), (), s32[]{:S(2)}) async-start(), calls=%async_computation.5 | async-start | bytes 2949120 | tf_op jit(solution)/shard_map/reduce_scatter | solution.py:232
  394.7 188.0 %all-reduce.21.cloned.1.call-start = ((), (), s32[]{:S(2)}) async-start(), calls=%async_computation.9 | async-start | bytes 2359296 | tf_op jit(solution)/shard_map/psum | solution.py:236
  428.7 48.5 %collective-permute-start.31 = (bf16[4,208,768]{2,1,0:T(8,128)(2,1)}, bf16[4,208,768]{2,1,0:T(8,128)(2,1)}, u32[]{:S(2)}, u32[]{:S(2)}) collective-permute-start(bf16[4,208,768]{2,1,0:T(8,128)(2,1)} %collective-permute-done.29), channel_id=1, source_target_pairs={{2,0},{3,1},{4,2},{5,3},{10,8},{11,9},{12,10},{13,11},{18,16},{19,... | collective-permute-start | bytes 3833864 | tf_op jit(solution)/shard_map/ppermute | solution.py:187
  430.0 47.3 %collective-permute-start.32 = (bf16[4,208,768]{2,1,0:T(8,128)(2,1)}, bf16[4,208,768]{2,1,0:T(8,128)(2,1)}, u32[]{:S(2)}, u32[]{:S(2)}) collective-permute-start(bf16[4,208,768]{2,1,0:T(8,128)(2,1)} %collective-permute-done.30), channel_id=1, source_target_pairs={{2,4},{3,5},{4,6},{5,7},{10,12},{11,13},{12,14},{13,15},{18,20},{1... | collective-permute-start | bytes 3833864 | tf_op jit(solution)/shard_map/ppermute | solution.py:187
  433.1 44.1 %collective-permute-start.33 = (bf16[4,208,768]{2,1,0:T(8,128)(2,1)S(1)}, bf16[4,208,768]{2,1,0:T(8,128)(2,1)}, u32[]{:S(2)}, u32[]{:S(2)}) collective-permute-start(bf16[4,208,768]{2,1,0:T(8,128)(2,1)S(1)} %broadcast_select_fusion.4.refs_11_), channel_id=1, source_target_pairs={{0,1},{1,0},{2,3},{3,2},{4,5},{5,4},{6,7},{7,6},{8,9},{9,8},{10,11... | collective-permute-start | bytes 3833864 | tf_op jit(solution)/shard_map/ppermute | solution.py:146
  477.5 47.2 %collective-permute-start.42 = (bf16[384,2304]{1,0:T(8,128)(2,1)}, bf16[384,2304]{1,0:T(8,128)(2,1)}, u32[]{:S(2)}, u32[]{:S(2)}) collective-permute-start(bf16[384,2304]{1,0:T(8,128)(2,1)} %get-tuple-element.370), channel_id=1, source_target_pairs={{0,1},{1,0},{2,3},{3,2},{4,5},{5,4},{6,7},{7,6},{8,9},{9,8},{10,11... | collective-permute-start | bytes 5308424 | tf_op jit(solution)/shard_map/ppermute | solution.py:146
  482.3 69.1 %collective-permute-start.35 = (bf16[4,208,768]{2,1,0:T(8,128)(2,1)}, bf16[4,208,768]{2,1,0:T(8,128)(2,1)}, u32[]{:S(2)}, u32[]{:S(2)}) collective-permute-start(bf16[4,208,768]{2,1,0:T(8,128)(2,1)} %get-tuple-element.544), channel_id=1, source_target_pairs={{2,0},{3,1},{4,6},{5,7},{10,8},{11,9},{12,14},{13,15},{18,16},{19,... | collective-permute-start | bytes 3833864 | tf_op jit(solution)/shard_map/ppermute | solution.py:192
  483.6 67.9 %collective-permute-start.36 = (bf16[4,208,768]{2,1,0:T(8,128)(2,1)}, bf16[4,208,768]{2,1,0:T(8,128)(2,1)}, u32[]{:S(2)}, u32[]{:S(2)}) collective-permute-start(bf16[4,208,768]{2,1,0:T(8,128)(2,1)} %get-tuple-element.381.refs_13_), channel_id=1, source_target_pairs={{0,1},{1,0},{2,3},{3,2},{4,5},{5,4},{6,7},{7,6},{8,9},{9,8},{10,11... | collective-permute-start | bytes 3833864 | tf_op jit(solution)/shard_map/ppermute | solution.py:146
  484.0 104.4 %reduce-scatter.11.cloned.1.call-start = ((), (), s32[]{:S(2)}) async-start(), calls=%async_computation.7 | async-start | bytes 737280 | tf_op jit(solution)/shard_map/reduce_scatter | solution.py:232
  522.4 102.2 %reduce-scatter.9.cloned.1.call-start = ((), (), s32[]{:S(2)}) async-start(), calls=%async_computation.6 | async-start | bytes 2211840 | tf_op jit(solution)/shard_map/reduce_scatter | solution.py:232
  527.9 160.3 %all-reduce.19.cloned.1.call-start = ((), (), s32[]{:S(2)}) async-start(), calls=%async_computation.8 | async-start | bytes 1179648 | tf_op jit(solution)/shard_map/psum | solution.py:236
  629.8 60.7 %collective-permute-start.44 = (bf16[8,768,128]{2,1,0:T(8,128)(2,1)}, bf16[8,768,128]{2,1,0:T(8,128)(2,1)S(1)}, u32[]{:S(2)}, u32[]{:S(2)}) collective-permute-start(bf16[8,768,128]{2,1,0:T(8,128)(2,1)} %constant_dynamic-slice_fusion.3), channel_id=1, source_target_pairs={{0,8},{8,0},{16,24},{24,16},{1,9},{9,1},{17,25},{25,17},{2,10},{10... | collective-permute-start | bytes 4718600 | tf_op jit(solution)/shard_map/ppermute | solution.py:141
  647.0 43.5 %collective-permute-start.46 = (bf16[8,768,128]{2,1,0:T(8,128)(2,1)}, bf16[8,768,128]{2,1,0:T(8,128)(2,1)}, u32[]{:S(2)}, u32[]{:S(2)}) collective-permute-start(bf16[8,768,128]{2,1,0:T(8,128)(2,1)} %constant_dynamic-slice_fusion.2), channel_id=1, source_target_pairs={{0,16},{8,24},{16,0},{24,8},{1,17},{9,25},{17,1},{25,9},{2,18},{10... | collective-permute-start | bytes 4718600 | tf_op jit(solution)/shard_map/ppermute | solution.py:141
  (198 other events, 3430.9 us)
Sparse Core Ops, SparseCore 0:
  389.5 36.3 reduce-scatter.4
  429.5 37.3 reduce-scatter.6
  484.1 74.1 all-reduce.20
  561.5 26.7 reduce-scatter.10
  592.1 32.4 reduce-scatter.8
  648.6 39.5 all-reduce.18

commit v4 on v3

--- a/solution.py
+++ b/solution.py
@@ -367,7 +367,7 @@
             scratch_shapes=turn_scratch(rows, bands, lanes),
         ),
         out_shape=[side, side],
-        compiler_params=grid_params(60),
+        compiler_params=grid_params(40),
         cost_estimate=pl.CostEstimate(flops=1, bytes_accessed=1, transcendentals=0),
         name="split_pixels",
     )(core.reshape(1), pixels.transpose(0, 2, 1, 3), means[:, :, None], rates[:, :, None])
@@ -422,7 +422,7 @@
             scratch_shapes=turn_scratch(rows, bands, lanes),
         ),
         out_shape=jax.ShapeDtypeStruct((images, patches, bands, lanes), jnp.bfloat16),
-        compiler_params=grid_params(60),
+        compiler_params=grid_params(40),
         cost_estimate=pl.CostEstimate(flops=1, bytes_accessed=1, transcendentals=0),
         name="join_pixels",
     )(core.reshape(1), mine, other)
@@ -507,7 +507,7 @@
             jax.ShapeDtypeStruct((pieces, images, lanes, width), jnp.bfloat16),
         ],
         input_output_aliases={} if first else {4 + count: 0, 5 + count: 1},
-        compiler_params=grid_params(60),
+        compiler_params=grid_params(48),
         cost_estimate=pl.CostEstimate(flops=1, bytes_accessed=1, transcendentals=0),
         name="embed_piece",
     )(place, low, *weights, *pixels, *(() if first else (total, kernels)))
@@ -534,7 +534,7 @@
         ],
         out_specs=pl.BlockSpec((1, share, rows, lanes), lambda i, j: (j, i, 0, 0)),
         out_shape=jax.ShapeDtypeStruct((pieces, images, rows, lanes), jnp.bfloat16),
-        compiler_params=grid_params(60, 2),
+        compiler_params=grid_params(40, 2),
         cost_estimate=pl.CostEstimate(flops=1, bytes_accessed=1, transcendentals=0),
         name="pixel_grads",
     )(grads, kernels, rates)
@@ -581,7 +581,7 @@
         out_specs=vmem,
         out_shape=jax.ShapeDtypeStruct((step_cells, width, depth), jnp.bfloat16),
         scratch_shapes=[pltpu.VMEM((step_cells, images * bands, width), jnp.bfloat16)],
-        compiler_params=pltpu.CompilerParams(vmem_limit_bytes=60 * 1024 * 1024),
+        compiler_params=pltpu.CompilerParams(vmem_limit_bytes=48 * 1024 * 1024),
         cost_estimate=pl.CostEstimate(flops=1, bytes_accessed=1, transcendentals=0),
         name="line_grads",
     )(low_turned, *pixels, *grads)
@@ -657,7 +657,7 @@
             ],
         ),
         out_shape=jax.ShapeDtypeStruct((images * bands, depth), jnp.float32),
-        compiler_params=grid_params(60),
+        compiler_params=grid_params(40),
         cost_estimate=pl.CostEstimate(flops=1, bytes_accessed=1, transcendentals=0),
         name="band_piece",
     )(place, grads, *weights, *pixels, *(() if first else (total,)))
@@ -700,7 +700,7 @@
         in_specs=[pl.BlockSpec((1, rows, triple), lambda i: (i, 0, 0))],
         out_specs=pl.BlockSpec((1, rows, width), lambda i: (i, 0, 0)),
         out_shape=jax.ShapeDtypeStruct((images, rows, width), jnp.bfloat16),
-        compiler_params=grid_params(60),
+        compiler_params=grid_params(24),
         cost_estimate=pl.CostEstimate(flops=1, bytes_accessed=1, transcendentals=0),
         name="attend",
     )(joint)
@@ -766,7 +766,7 @@
             jax.ShapeDtypeStruct((images, rows, triple), jnp.bfloat16),
             jax.ShapeDtypeStruct((1, triple), jnp.float32),
         ],
-        compiler_params=grid_params(60),
+        compiler_params=grid_params(24),
         cost_estimate=pl.CostEstimate(flops=1, bytes_accessed=1, transcendentals=0),
         name="attend_back",
     )(joint, grads)
@@ -778,7 +778,7 @@
     return center * factor, factor
 
 
-def small_call(kernel, name, grid, in_specs, out_specs, out_shape, scratch=(), limit=60):
+def small_call(kernel, name, grid, in_specs, out_specs, out_shape, scratch=(), limit=40):
     return pl.pallas_call(
         kernel,
         grid=grid,
@@ -982,7 +982,7 @@
             scratch_shapes=[pltpu.VMEM((width, rows), jnp.bfloat16)],
         ),
         out_shape=[half, half],
-        compiler_params=grid_params(60),
+        compiler_params=grid_params(32),
         cost_estimate=pl.CostEstimate(flops=1, bytes_accessed=1, transcendentals=0),
         name="rows_grad",
     )(core.reshape(1), left, right)
@@ -1069,38 +1069,49 @@
             down_half,
             jax.ShapeDtypeStruct((1, hidden), jnp.float32),
         ],
-        compiler_params=grid_params(60),
+        compiler_params=grid_params(52),
         cost_estimate=pl.CostEstimate(flops=1, bytes_accessed=1, transcendentals=0),
         name="mlp",
     )(core.reshape(1), normed, residual, grads, up, up_bias[None], down, down_bias[None])
 
 
-def assemble_kernel(bits_ref, one_mine, one_came, two_mine, two_came, out_ref):
-    for at, ref in enumerate((one_mine, one_came, two_mine, two_came)):
+def assemble_kernel(bits_ref, *refs):
+    out_ref = refs[-1]
+    count = out_ref.shape[0]
+    pieces = []
+    for part in range(2):
+        mine, early, late = refs[part], refs[2 + part], refs[4 + part]
+        pieces += [(mine, 0), (mine, count), (early, 0), (late, 0)]
+    for at, (ref, first) in enumerate(pieces):
 
         @pl.when(pl.program_id(0) == at)
-        def _(ref=ref):
-            out_ref[...] = ref[...].astype(jnp.float32)
-
-
-def assemble(bits, one_mine, one_came, two_mine, two_came):
-    cells, width, depth = one_mine.shape
-    whole = pl.BlockSpec((cells, width, depth), lambda t, bits: (0, 0, 0))
+        def _(ref=ref, first=first):
+            out_ref[...] = ref[first : first + count].astype(jnp.float32)
+
+
+def assemble(bits, mine, early, late):
+    cells, width, depth = mine[0].shape
+    half = cells // 2
+
+    def whole(count):
+        return pl.BlockSpec((count, width, depth), lambda t, bits: (0, 0, 0))
+
     return pl.pallas_call(
         assemble_kernel,
         grid_spec=pltpu.PrefetchScalarGridSpec(
             num_scalar_prefetch=1,
-            grid=(4,),
-            in_specs=[whole] * 4,
+            grid=(8,),
+            in_specs=[whole(cells)] * 2 + [whole(half)] * 4,
             out_specs=pl.BlockSpec(
-                (cells, width, depth), lambda t, bits: (t // 2 * 2 + (bits[t // 2] ^ (t % 2)), 0, 0)
+                (half, width, depth),
+                lambda t, bits: (t // 4 * 4 + (bits[t // 4] ^ (t // 2 % 2)) * 2 + t % 2, 0, 0),
             ),
         ),
         out_shape=jax.ShapeDtypeStruct((4 * cells, width, depth), jnp.float32),
-        compiler_params=grid_params(60),
+        compiler_params=grid_params(40),
         cost_estimate=pl.CostEstimate(flops=1, bytes_accessed=1, transcendentals=0),
         name="assemble",
-    )(bits, one_mine, one_came, two_mine, two_came)
+    )(bits, *mine, *early, *late)
 
 
 def per_device(
@@ -1408,29 +1419,29 @@
             (place(spots2, group, group ^ 1, group ^ 2, group ^ 3), weights2),
             (place(spots3, group, group ^ 1, group ^ 2, group ^ 3), weights3),
         ]
+        pair_out, pair_qkv = late_rows(*late)
         for spots, weights in plan[:2]:
             grad_vectors = band_piece(spots, chip_emb, weights, chip_pixels, grad_vectors)
-        grad_vectors, right1, left1, beside_emb, share_up, late = tie(
-            grad_vectors, right1, left1, beside_emb, share_up, late
+        grad_vectors, right1, left1, beside_emb, share_up, pair_out, pair_qkv = tie(
+            grad_vectors, right1, left1, beside_emb, share_up, pair_out, pair_qkv
         )
         right2, left2 = (along_line(right1, -1, (1, 2)), along_line(left1, 1, (1, 2)))
-        pair_out, pair_qkv = late_rows(*late)
+        half_out, half_qkv = core_sum(*pair_out), core_sum(*pair_qkv)
         far = jnp.where((chip & 1) == 0, right1, left1)
         line_emb = [grad_emb, beside_emb, far, swap_batch(far, 1)]
         for spots, weights in plan[2:]:
             grad_vectors = band_piece(spots, chip_emb, weights, chip_pixels, grad_vectors)
-        grad_vectors, right2, left2, line_emb, share_down, pair_out, pair_qkv = tie(
-            grad_vectors, right2, left2, line_emb, share_down, pair_out, pair_qkv
-        )
-        half_out, half_qkv = core_sum(*pair_out), core_sum(*pair_qkv)
+        grad_vectors, right2, left2, line_emb, share_down, half_out, half_qkv = tie(
+            grad_vectors, right2, left2, line_emb, share_down, half_out, half_qkv
+        )
         share_out_rows, share_qkv = row_share(half_out), row_share(half_qkv)
         end3 = line_ends(jnp.where(chip == 1, right2, left2))
         far = jnp.where(chip < 2, right2, left2)
         line_emb += [far, swap_batch(far, 1)]
         hyper_grads = finish_low(grad_vectors)
         wide, narrow, parts, small = pack(hyper_grads)
-        small, block_out, end3, line_emb, chip_emb = tie(
-            small, block_out, end3, line_emb, chip_emb
+        small, block_out, end3, line_emb, chip_emb, share_out_rows, share_qkv = tie(
+            small, block_out, end3, line_emb, chip_emb, share_out_rows, share_qkv
         )
         small_came = swap_batch(part_of(small, 1 - core, 2), 1)
         far = jnp.where(chip == 1, right1, jnp.where(chip == 2, left1, end3))
@@ -1469,54 +1480,64 @@
             row_both(row_mine(share)) for share in (share_qkv, share_out_rows, share_up, share_down)
         ]
     else:
+        def small_hop(hop):
+            return swap_batch(part_of(small, chip ^ hop, 4), 2 * hop)
+
         small = part_of(small, core, 2) + small_came
-        small_came = [swap_batch(part_of(small, chip ^ hop, 4), 2 * hop) for hop in (1, 2, 3)]
+        small_came = [small_hop(1), small_hop(2)]
         kernel_one = line_grads(low_turned, cells, line_pixels, line_emb, 0, 2)
-        mine_up, mine_down = row_mine(share_up), row_mine(share_down)
-        kernel_one, line_emb, small_came, mine_up, mine_down, share_qkv, share_out_rows = tie(
-            kernel_one, line_emb, small_came, mine_up, mine_down, share_qkv, share_out_rows
-        )
-
+        kernel_one, line_emb, small, small_came = tie(kernel_one, line_emb, small, small_came)
+
+        small_came.append(small_hop(3))
+        kernel_two = line_grads(low_turned, cells, line_pixels, line_emb, 1, 2)
+        mine_up, mine_out = row_mine(share_up), row_mine(share_out_rows)
+        kernel_two, small_came, mine_up, mine_out, share_down, share_qkv = tie(
+            kernel_two, small_came, mine_up, mine_out, share_down, share_qkv
+        )
+
+        sums = [kernel_one, kernel_two]
+        mine_down, mine_qkv = row_mine(share_down), row_mine(share_qkv)
+        came = sum_out(sums, False)
         small = sum(small_came, part_of(small, chip, 4))
         small_came = swap_group(small, 1)
-        kernel_two = line_grads(low_turned, cells, line_pixels, line_emb, 1, 2)
-        kernel_two, small_came = tie(kernel_two, small_came)
-
-        sums = [kernel_one, kernel_two]
-        came = sum_out(sums, False)
-        small = small + small_came
-        small_came = swap_group(small, 2)
-        mine_qkv, mine_out = row_mine(share_qkv), row_mine(share_out_rows)
         chip_back = pixel_grads(chip_emb, kernels, rates)
-        chip_back, came, small_came, mine_qkv, mine_out = tie(
-            chip_back, came, small_came, mine_qkv, mine_out
+        chip_back, came, small_came, mine_down, mine_qkv = tie(
+            chip_back, came, small_came, mine_down, mine_qkv
         )
 
         sums = sum_in(sums, came, False)
         came = sum_out(sums, True)
         small = small + small_came
-        small_came = [swap_batch(small, 2 * hop) for hop in (1, 2, 3)]
-        own_back, other_back = chip_back[:, :images], chip_back[:, images:]
-        came, own_back, other_back = tie(came, own_back, other_back)
+        small_came = swap_group(small, 2)
+        own_back, other_back = chip_back[:, :images], swap_batch(chip_back[:, images:], 1)
+        came, own_back, other_back, small_came = tie(came, own_back, other_back, small_came)
 
         sums = sum_in(sums, came, True)
         came = share_out(sums, True)
-        other_back = swap_batch(other_back, 1)
-        came, small_came, other_back = tie(came, small_came, other_back)
+        small = small + small_came
+        small_came = [swap_batch(small, 2), swap_batch(small, 4)]
+        pixel_grad = join_pixels(
+            own_back, other_back, core, patches, cells, pixel_cells, band_slots
+        )
+        came, small, small_came, pixel_grad = tie(came, small, small_came, pixel_grad)
 
         sums = share_in(sums, came, True)
-        came = share_out(sums, False)
+        early, late = ([value[: cells // 8] for value in sums], [value[cells // 8 :] for value in sums])
+        early = share_out(early, False)
+        small_came.append(swap_batch(small, 6))
+        wide_mine = jnp.concatenate([mine_qkv, mine_out, mine_up], axis=1)
+        wide_came, down_came = swap_batch(wide_mine, 1), swap_batch(mine_down, 1)
+        early, late, small_came, wide_came, down_came = tie(
+            early, late, small_came, wide_came, down_came
+        )
+        late = share_out(late, False)
         small = four_in_order(chip, [small] + small_came)
         small = in_order(core, small, swap_batch(small, 1))
-        pixel_grad = join_pixels(
-            own_back, other_back, core, patches, cells, pixel_cells, band_slots
-        )
-        totals = [mine_qkv, mine_out, mine_up, mine_down]
-        widths = [mine.shape[1] for mine in totals[:3]]
-        wide_mine = jnp.concatenate(totals[:3], axis=1)
-        wide_both = row_both(wide_mine)
+        widths = [mine.shape[1] for mine in (mine_qkv, mine_out, mine_up)]
+        wide_both = in_order(core, wide_mine, wide_came).astype(jnp.float32)
         ends = [0, widths[0], widths[0] + widths[1], sum(widths)]
-        totals = [wide_both[:, ends[at] : ends[at + 1]] for at in range(3)] + [row_both(totals[3])]
+        totals = [wide_both[:, ends[at] : ends[at + 1]] for at in range(3)]
+        totals.append(in_order(core, mine_down, down_came).astype(jnp.float32))
     pixel_grad = pixel_grad[None]
 
     found = []
@@ -1530,11 +1551,11 @@
         at += count
     batch_mean, batch_var = bin_stats(found[13], found[14], found[15], patches * pixel_cells)
     if tuned_mesh():
-        came, pixel_grad, found, totals, batch_mean, batch_var = tie(
-            came, pixel_grad, found, totals, batch_mean, batch_var
+        late, found, totals, batch_mean, batch_var = tie(
+            late, found, totals, batch_mean, batch_var
         )
         bits = jnp.stack([group & 1, group >> 1])
-        kernel_total = assemble(bits, sums[0], came[0], sums[1], came[1])
+        kernel_total = assemble(bits, sums, early, late)
     return (
         block_out,
         pixel_grad,

time: 827 us -> 816 us (0.987)
  local copies, waits for them, and re-layouts: 118 us -> 165 us
  Pallas kernels: 304 us -> 260 us
  waiting for transfers between devices: 187 us -> 167 us
    unnamed x318 -> x404, local copies, waits for them, and re-layouts: 24.8 us -> 64.5 us
    reduce_scatter x4, waiting for transfers between devices: 40.3 us -> 7.26 us  [row_share(): return lax.psum_scatter(half, 'group', scatter_dimension=0, tiled=True)]
    ppermute x2, waiting for transfers between devices: 27.7 us -> 8.7 us  [line_ends(): return lax.ppermute(value, 'batch', pairs)]
    psum x2, waiting for transfers between devices: 20.5 us -> 38.8 us  [row_mine(): return lax.psum(share, 'batch', axis_index_groups=same_core())]
    ppermute x18 -> x20, waiting for transfers between devices: 33.8 us -> 44.5 us  [swap_group(): return lax.ppermute(value, 'group', [(at, at ^ bits) for at in range(4)])]
    ppermute x18 -> x20, starting transfers between devices: 20.5 us -> 23.9 us  [swap_group(): return lax.ppermute(value, 'group', [(at, at ^ bits) for at in range(4)])]
  transfers between devices with their start and end apart: 67 -> 69, of which waited for: 25 -> 24; matrix products, arithmetic and copies ran while one was open for 22% -> 22% of each run, Pallas kernels for 35% -> 30%
where the time goes in v4:
time: 816 us; the launch traced here: 807 us
  Pallas kernels  260 us (32%)
  waiting for transfers between devices  167 us (20%)
  local copies, waits for them, and re-layouts  165 us (20%)
  starting transfers between devices  86.3 us (11%)
  other arithmetic  78.9 us (10%)
  matrix products  33.2 us (4%)
  between operations  17 us (2%)
    pallas_call x7, Pallas kernels, embed_piece(): pl.pallas_call(partial(embed_kernel, first, count), grid_spec=pltpu.Prefe...  70 us
    unnamed x404, local copies, waits for them, and re-layouts  64.5 us
    ppermute x20, waiting for transfers between devices, swap_group(): return lax.ppermute(value, 'group', [(at, at ^ bits) for at in range(4)])  44.5 us
    psum x2, waiting for transfers between devices, row_mine(): return lax.psum(share, 'batch', axis_index_groups=same_core())  38.8 us
    ppermute x33, starting transfers between devices, swap_batch(): lax.ppermute(value, 'batch', [(at, at ^ bits) for at in range(count)])  37.4 us
    ppermute x33, waiting for transfers between devices, swap_batch(): lax.ppermute(value, 'batch', [(at, at ^ bits) for at in range(count)])  35.3 us
    pallas_call x1, Pallas kernels, mlp(): pl.pallas_call(mlp_kernel, grid_spec=pltpu.PrefetchScalarGridSpec(num_sca...  33.2 us
    ppermute x8, waiting for transfers between devices, along_line(): return lax.ppermute(value, 'batch', pairs)  31.9 us
  transfers between devices with their start and end apart: 69, of which 24 were waited for; matrix products, arithmetic and copies ran while one was open for 22% of the time, Pallas kernels for 30%

profile of v4, /device:TPU:0, one launch (start us, length us, event | category | flops | bytes accessed | tf_op | source)
XLA Modules:
  0.0 806.8 jit_solution(2361129252353850210)
XLA Ops:
  27.8 22.1 %collective-permute-done = bf16[8,768,128]{2,1,0:T(8,128)(2,1)} collective-permute-done((bf16[8,768,128]{2,1,0:T(8,128)(2,1)}, bf16[8,768,128]{2,1,0:T(8,128)(2,1)}, u32[]{:S(2)}, u32[]{:S(2)}) %collective-permute-start) | collective-permute-done | bytes 1572896 | tf_op jit(solution)/shard_map/ppermute | solution.py:187
  63.4 15.3 %split_pixels.1 = (bf16[4,4,208,512]{3,2,1,0:T(8,128)(2,1)S(1)}, bf16[4,4,208,512]{3,2,1,0:T(8,128)(2,1)}) custom-call(s32[1]{0:T(128)} %bitcast.1.core_ref, bf16[4,196,16,256]{3,2,1,0:T(8,128)(2,1)S(1)} %bitcast.255, f32[4,16,1]{2,1,0:T(8,128)S(1)} %convolution_bitcast_fusion.7.mean_ref, f32[4,16,1]{2,1,0:T(8,128)S(1)} %copy.149.rate_ref), custom_call_target="tpu_custom_call" | custom-call | flops 1 | bytes 1 | tf_op jit(solution)/shard_map/split_pixels/pallas_call | solution.py:356
  108.0 8.3 %collective-permute-start.11 = (bf16[4,208,512]{2,1,0:T(8,128)(2,1)}, bf16[4,208,512]{2,1,0:T(8,128)(2,1)S(1)}, u32[]{:S(2)}, u32[]{:S(2)}) collective-permute-start(bf16[4,208,512]{2,1,0:T(8,128)(2,1)} %dynamic-slice_bitcast_fusion.7), channel_id=1, source_target_pairs={{0,4},{1,5},{2,6},{3,7},{4,0},{5,1},{6,2},{7,3},{8,12},{9,13},{10,... | collective-permute-start | bytes 2555912 | tf_op jit(solution)/shard_map/ppermute | solution.py:146
  125.2 11.7 %embed_piece.7 = (f32[8,208,768]{2,1,0:T(8,128)}, bf16[4,8,512,768]{3,2,1,0:T(8,128)(2,1)}) custom-call(s32[5]{0:T(128)S(1)} %stack.90.at_ref, bf16[128,128]{1,0:T(8,128)(2,1)S(1)} %copy.159.low_ref, bf16[32,768,128]{2,1,0:T(8,128)(2,1)} %refs_0_.3, bf16[4,4,208,512]{3,2,1,0:T(8,128)(2,1)S(1)} %copy-done.2, ...), custom_call_target="tpu_custom_call" | custom-call | flops 1 | bytes 1 | tf_op jit(solution)/shard_map/embed_piece/pallas_call | solution.py:483
  136.9 11.9 %embed_piece.8 = (f32[8,208,768]{2,1,0:T(8,128)}, bf16[4,8,512,768]{3,2,1,0:T(8,128)(2,1)}) custom-call(s32[4]{0:T(128)S(1)} %add_add_fusion.4.at_ref, bf16[128,128]{1,0:T(8,128)(2,1)S(1)} %copy.159.low_ref, bf16[8,768,128]{2,1,0:T(8,128)(2,1)S(1)} %copy-done.19, ...), custom_call_target="tpu_custom_call", output_to_operand_aliasing={{0}: (7, {}), {1}: (8, {})} | custom-call | flops 1 | bytes 1 | tf_op jit(solution)/shard_map/embed_piece/pallas_call | solution.py:483
  152.9 8.7 %collective-permute-done.8 = bf16[8,768,128]{2,1,0:T(8,128)(2,1)} collective-permute-done((bf16[8,768,128]{2,1,0:T(8,128)(2,1)}, bf16[8,768,128]{2,1,0:T(8,128)(2,1)}, u32[]{:S(2)}, u32[]{:S(2)}) %collective-permute-start.8) | collective-permute-done | bytes 1572896 | tf_op jit(solution)/shard_map/ppermute | solution.py:192
  197.8 11.9 %embed_piece.10 = (f32[8,208,768]{2,1,0:T(8,128)}, bf16[4,8,512,768]{3,2,1,0:T(8,128)(2,1)}) custom-call(s32[4]{0:T(128)S(1)} %get-tuple-element.622.at_ref, bf16[128,128]{1,0:T(8,128)(2,1)S(1)} %copy.159.low_ref, bf16[8,768,128]{2,1,0:T(8,128)(2,1)S(1)} %get-tuple-element.547.refs_0_, ...), custom_call_target="tpu_custom_call", output_to_operand_aliasing={{0}: (7, {}), {1}: (8, {})} | custom-call | flops 1 | bytes 1 | tf_op jit(solution)/shard_map/embed_piece/pallas_call | solution.py:483
  232.0 7.7 embed_piece.11
  239.7 12.3 %embed_piece.12 = (f32[8,208,768]{2,1,0:T(8,128)}, bf16[4,8,512,768]{3,2,1,0:T(8,128)(2,1)}) custom-call(s32[4]{0:T(128)S(1)} %get-tuple-element.621.at_ref, bf16[128,128]{1,0:T(8,128)(2,1)S(1)} %copy.159.low_ref, bf16[8,768,128]{2,1,0:T(8,128)(2,1)S(1)} %copy-done.14, ...), custom_call_target="tpu_custom_call", output_to_operand_aliasing={{0}: (7, {}), {1}: (8, {})} | custom-call | flops 1 | bytes 1 | tf_op jit(solution)/shard_map/embed_piece/pallas_call | solution.py:483
  299.9 33.2 %mlp.1 = (bf16[832,768]{1,0:T(8,128)(2,1)S(1)}, f32[832,768]{1,0:T(8,128)}, bf16[384,3072]{1,0:T(8,128)(2,1)}, bf16[384,3072]{1,0:T(8,128)(2,1)}, bf16[1536,768]...) custom-call(s32[1]{0:T(128)} %bitcast.1.core_ref, bf16[832,768]{1,0:T(8,128)(2,1)} %bitcast.262, ...), custom_call_target="tpu_custom_call" | custom-call | flops 1 | bytes 1 | tf_op jit(solution)/shard_map/mlp/pallas_call | solution.py:1043
  351.5 17.0 %attend_back.1 = (bf16[4,208,2304]{2,1,0:T(8,128)(2,1)S(1)}, f32[1,2304]{1,0:T(1,128)S(1)}) custom-call(bf16[4,208,2304]{2,1,0:T(8,128)(2,1)S(1)} %get-tuple-element.293.joint_ref, bf16[4,208,768]{2,1,0:T(8,128)(2,1)S(1)} %copy-done.59), custom_call_target="tpu_custom_call" | custom-call | flops 1 | bytes 1 | tf_op jit(solution)/shard_map/attend_back/pallas_call | solution.py:754
  406.8 8.5 %band_piece.4.refs_6_ = f32[128,128]{1,0:T(8,128)S(1)} custom-call(s32[5]{0:T(128)S(1)} %stack.90.at_ref, bf16[8,208,768]{2,1,0:T(8,128)(2,1)S(1)} %constant_dynamic-update-slice_fusion.2.grad_ref, bf16[32,768,128]{2,1,0:T(8,128)(2,1)} %refs_0_.3, bf16[4,4,208,512]{3,2,1,0:T(8,128)(2,1)S(1)} %copy-done.6, ...), custom_call_target="tpu_custom_call" | custom-call | flops 1 | bytes 1 | tf_op jit(solution)/shard_map/band_piece/pallas_call | solution.py:639
  418.4 7.6 band_piece.5.refs_6_
  440.5 8.1 %band_piece.6.refs_6_ = f32[128,128]{1,0:T(8,128)S(1)} custom-call(s32[5]{0:T(128)S(1)} %copy-done.78, bf16[8,208,768]{2,1,0:T(8,128)(2,1)S(1)} %copy-done.9, bf16[8,768,128]{2,1,0:T(8,128)(2,1)S(1)} %get-tuple-element.547.refs_0_, bf16[12,768,128]{2,1,0:T(8,128)(2,1)} %collective-permute-done.9.refs_1_, ...), custom_call_target="tpu_custom_call" | custom-call | flops 1 | bytes 1 | tf_op jit(solution)/shard_map/band_piece/pallas_call | solution.py:639
  449.2 7.6 band_piece.7
  551.7 12.4 %line_grads.2 = bf16[16,768,128]{2,1,0:T(8,128)(2,1)} custom-call(bf16[128,512]{1,0:T(8,128)(2,1)S(1)} %bitcast.265, bf16[4,208,512]{2,1,0:T(8,128)(2,1)S(1)} %dynamic-slice_bitcast_fusion.1.refs_1_, bf16[4,208,512]{2,1,0:T(8,128)(2,1)S(1)} %get-tuple-element.545.refs_2_, bf16[4,208,512]{2,1,0:T(8,128)(2,1)S(1)} %copy-done.46, ...), custom_call_target="tpu_custom_call" | custom-call | flops 1 | bytes 1 | tf_op jit(solution)/shard_map/line_grads/pallas_call | solution.py:578
  581.9 12.2 %line_grads.3 = bf16[16,768,128]{2,1,0:T(8,128)(2,1)} custom-call(bf16[128,512]{1,0:T(8,128)(2,1)S(1)} %bitcast.266, bf16[4,208,512]{2,1,0:T(8,128)(2,1)S(1)} %dynamic-slice_bitcast_fusion.1.refs_1_, bf16[4,208,512]{2,1,0:T(8,128)(2,1)S(1)} %get-tuple-element.545.refs_2_, bf16[4,208,512]{2,1,0:T(8,128)(2,1)S(1)} %copy-done.47, ...), custom_call_target="tpu_custom_call" | custom-call | flops 1 | bytes 1 | tf_op jit(solution)/shard_map/line_grads/pallas_call | solution.py:578
  594.1 9.3 %all-reduce.21.cloned.1.call-done = (bf16[96,3072]{1,0:T(8,128)(2,1)}, bf16[96,768]{1,0:T(8,128)(2,1)}) async-done(((bf16[96,3072]{1,0:T(8,128)(2,1)}, bf16[96,768]{1,0:T(8,128)(2,1)}), (bf16[96,3072]{1,0:T(8,128)(2,1)}, bf16[96,768]{1,0:T(8,128)(2,1)})) %all-reduce.21.cloned.1.call-update) | async-done | bytes 737296 | tf_op jit(solution)/shard_map/psum | solution.py:236
  612.4 13.7 %pixel_grads.1 = bf16[4,8,208,512]{3,2,1,0:T(8,128)(2,1)S(1)} custom-call(bf16[8,208,768]{2,1,0:T(8,128)(2,1)S(1)} %copy-done.10, bf16[4,8,512,768]{3,2,1,0:T(8,128)(2,1)} %get-tuple-element.382.kernel_ref, f32[8,1,512]{2,1,0:T(1,128)S(1)} %broadcast_in_dim.147.rate_ref), custom_call_target="tpu_custom_call" | custom-call | flops 1 | bytes 1 | tf_op jit(solution)/shard_map/pixel_grads/pallas_call | solution.py:527
  629.0 29.4 %all-reduce.19.cloned.1.call-done = (bf16[384,768]{1,0:T(8,128)(2,1)}, bf16[96,2304]{1,0:T(8,128)(2,1)}) async-done(((bf16[384,768]{1,0:T(8,128)(2,1)}, bf16[96,2304]{1,0:T(8,128)(2,1)}), (bf16[384,768]{1,0:T(8,128)(2,1)}, bf16[96,2304]{1,0:T(8,128)(2,1)})) %all-reduce.19.cloned.1.call-update) | async-done | bytes 1032208 | tf_op jit(solution)/shard_map/psum | solution.py:236
  676.4 25.4 %collective-permute-done.50 = f32[704,128]{1,0:T(8,128)S(1)} collective-permute-done((f32[704,128]{1,0:T(8,128)S(1)}, f32[704,128]{1,0:T(8,128)S(1)}, u32[]{:S(2)}, u32[]{:S(2)}) %collective-permute-start.50) | collective-permute-done | bytes 360480 | tf_op jit(solution)/shard_map/ppermute | solution.py:141
  712.4 14.1 %join_pixels.1 = bf16[4,196,16,256]{3,2,1,0:T(8,128)(2,1)} custom-call(s32[1]{0:T(128)} %bitcast.1.core_ref, bf16[4,4,208,512]{3,2,1,0:T(8,128)(2,1)S(1)} %copy-done.28, bf16[4,4,208,512]{3,2,1,0:T(8,128)(2,1)} %collective-permute-done.49.other_ref), custom_call_target="tpu_custom_call" | custom-call | flops 1 | bytes 1 | tf_op jit(solution)/shard_map/join_pixels/pallas_call | solution.py:415
  736.0 10.7 %collective-permute-done.57 = f32[704,128]{1,0:T(8,128)} collective-permute-done((f32[704,128]{1,0:T(8,128)}, f32[704,128]{1,0:T(8,128)}, u32[]{:S(2)}, u32[]{:S(2)}) %collective-permute-start.57) | collective-permute-done | bytes 360480 | tf_op jit(solution)/shard_map/ppermute | solution.py:146
  791.9 7.8 assemble.1
  (765 shorter events, 462.6 us)
Async XLA Ops:
  7.3 418.8 %reduce-scatter.5.cloned.1.call-start = ((), (), s32[]{:S(2)}) async-start(), calls=%async_computation.4 | async-start | bytes 2949120 | tf_op jit(solution)/shard_map/reduce_scatter | solution.py:232
  102.0 59.6 %collective-permute-start.10 = (bf16[12,768,128]{2,1,0:T(8,128)(2,1)}, bf16[12,768,128]{2,1,0:T(8,128)(2,1)}, u32[]{:S(2)}, u32[]{:S(2)}) collective-permute-start(bf16[12,768,128]{2,1,0:T(8,128)(2,1)} %get-tuple-element.581), channel_id=1, source_target_pairs={{0,16},{8,24},{16,0},{24,8},{1,17},{9,25},{17,1},{25,9},{2,18},{10... | collective-permute-start | bytes 7077896 | tf_op jit(solution)/shard_map/ppermute | solution.py:141
  102.5 59.1 %collective-permute-start.9 = (bf16[12,768,128]{2,1,0:T(8,128)(2,1)}, bf16[12,768,128]{2,1,0:T(8,128)(2,1)}, u32[]{:S(2)}, u32[]{:S(2)}) collective-permute-start(bf16[12,768,128]{2,1,0:T(8,128)(2,1)} %get-tuple-element.582), channel_id=1, source_target_pairs={{0,8},{8,0},{16,24},{24,16},{1,9},{9,1},{17,25},{25,17},{2,10},{10... | collective-permute-start | bytes 7077896 | tf_op jit(solution)/shard_map/ppermute | solution.py:141
  103.2 58.4 %collective-permute-start.8 = (bf16[8,768,128]{2,1,0:T(8,128)(2,1)}, bf16[8,768,128]{2,1,0:T(8,128)(2,1)}, u32[]{:S(2)}, u32[]{:S(2)}) collective-permute-start(bf16[8,768,128]{2,1,0:T(8,128)(2,1)} %get-tuple-element.548), channel_id=1, source_target_pairs={{2,0},{3,1},{4,6},{5,7},{10,8},{11,9},{12,14},{13,15},{18,16},{19,... | collective-permute-start | bytes 4718600 | tf_op jit(solution)/shard_map/ppermute | solution.py:192
  108.0 44.9 %collective-permute-start.11 = (bf16[4,208,512]{2,1,0:T(8,128)(2,1)}, bf16[4,208,512]{2,1,0:T(8,128)(2,1)S(1)}, u32[]{:S(2)}, u32[]{:S(2)}) collective-permute-start(bf16[4,208,512]{2,1,0:T(8,128)(2,1)} %dynamic-slice_bitcast_fusion.7), channel_id=1, source_target_pairs={{0,4},{1,5},{2,6},{3,7},{4,0},{5,1},{6,2},{7,3},{8,12},{9,13},{10,... | collective-permute-start | bytes 2555912 | tf_op jit(solution)/shard_map/ppermute | solution.py:146
  170.6 52.9 %collective-permute-start.12 = (bf16[12,768,128]{2,1,0:T(8,128)(2,1)}, bf16[12,768,128]{2,1,0:T(8,128)(2,1)}, u32[]{:S(2)}, u32[]{:S(2)}) collective-permute-start(bf16[12,768,128]{2,1,0:T(8,128)(2,1)} %get-tuple-element.580), channel_id=1, source_target_pairs={{0,8},{8,0},{16,24},{24,16},{1,9},{9,1},{17,25},{25,17},{2,10},{10... | collective-permute-start | bytes 7077896 | tf_op jit(solution)/shard_map/ppermute | solution.py:141
  171.9 52.6 %collective-permute-start.13 = (bf16[12,768,128]{2,1,0:T(8,128)(2,1)}, bf16[12,768,128]{2,1,0:T(8,128)(2,1)}, u32[]{:S(2)}, u32[]{:S(2)}) collective-permute-start(bf16[12,768,128]{2,1,0:T(8,128)(2,1)} %get-tuple-element.579), channel_id=1, source_target_pairs={{0,16},{8,24},{16,0},{24,8},{1,17},{9,25},{17,1},{25,9},{2,18},{10... | collective-permute-start | bytes 7077896 | tf_op jit(solution)/shard_map/ppermute | solution.py:141
  177.7 41.0 %collective-permute-start.15 = (bf16[4,208,512]{2,1,0:T(8,128)(2,1)}, bf16[4,208,512]{2,1,0:T(8,128)(2,1)}, u32[]{:S(2)}, u32[]{:S(2)}) collective-permute-start(bf16[4,208,512]{2,1,0:T(8,128)(2,1)} %dynamic-slice_bitcast_fusion.5), channel_id=1, source_target_pairs={{0,4},{1,5},{2,6},{3,7},{4,0},{5,1},{6,2},{7,3},{8,12},{9,13},{10,... | collective-permute-start | bytes 2555912 | tf_op jit(solution)/shard_map/ppermute | solution.py:146
  265.2 69.7 %collective-permute-start.20 = (bf16[4,208,512]{2,1,0:T(8,128)(2,1)}, bf16[4,208,512]{2,1,0:T(8,128)(2,1)S(1)}, u32[]{:S(2)}, u32[]{:S(2)}) collective-permute-start(bf16[4,208,512]{2,1,0:T(8,128)(2,1)} %dynamic-slice_bitcast_fusion.3), channel_id=1, source_target_pairs={{0,6},{1,7},{2,4},{3,5},{4,2},{5,3},{6,0},{7,1},{8,14},{9,15},{10,... | collective-permute-start | bytes 2555912 | tf_op jit(solution)/shard_map/ppermute | solution.py:146
  290.0 44.2 %collective-permute-start.21 = (bf16[128,128]{0,1:T(8,128)(2,1)S(1)}, bf16[128,128]{0,1:T(8,128)(2,1)S(1)}, u32[]{:S(2)}, u32[]{:S(2)}) collective-permute-start(bf16[128,128]{0,1:T(8,128)(2,1)S(1)} %pad_maximum_fusion.11), channel_id=1, source_target_pairs={{0,2},{1,3},{2,0},{3,1},{4,6},{5,7},{6,4},{7,5},{8,10},{9,11},{10,... | collective-permute-start | bytes 98312 | tf_op jit(solution)/shard_map/ppermute | solution.py:146
  291.1 43.0 %collective-permute-start.22 = (bf16[128,128]{0,1:T(8,128)(2,1)S(1)}, bf16[128,128]{0,1:T(8,128)(2,1)S(1)}, u32[]{:S(2)}, u32[]{:S(2)}) collective-permute-start(bf16[128,128]{0,1:T(8,128)(2,1)S(1)} %pad_maximum_fusion.11), channel_id=1, source_target_pairs={{0,4},{1,5},{2,6},{3,7},{4,0},{5,1},{6,2},{7,3},{8,12},{9,13},{10,... | collective-permute-start | bytes 98312 | tf_op jit(solution)/shard_map/ppermute | solution.py:146
  291.1 43.0 %collective-permute-start.23 = (bf16[128,128]{0,1:T(8,128)(2,1)S(1)}, bf16[128,128]{0,1:T(8,128)(2,1)S(1)}, u32[]{:S(2)}, u32[]{:S(2)}) collective-permute-start(bf16[128,128]{0,1:T(8,128)(2,1)S(1)} %pad_maximum_fusion.11), channel_id=1, source_target_pairs={{0,6},{1,7},{2,4},{3,5},{4,2},{5,3},{6,0},{7,1},{8,14},{9,15},{10,... | collective-permute-start | bytes 98312 | tf_op jit(solution)/shard_map/ppermute | solution.py:146
  294.5 41.3 %collective-permute-start.24 = (f32[4,512]{1,0:T(4,128)S(1)}, f32[4,512]{1,0:T(4,128)S(1)}, u32[]{:S(2)}, u32[]{:S(2)}) collective-permute-start(f32[4,512]{1,0:T(4,128)S(1)} %tile.10), channel_id=1, source_target_pairs={{0,1},{1,0},{2,3},{3,2},{4,5},{5,4},{6,7},{7,6},{8,9},{9,8},{10,11... | collective-permute-start | bytes 24584 | tf_op jit(solution)/shard_map/ppermute | solution.py:146
  335.8 41.2 %collective-permute-start.26 = (bf16[384,3072]{1,0:T(8,128)(2,1)}, bf16[384,3072]{1,0:T(8,128)(2,1)}, u32[]{:S(2)}, u32[]{:S(2)}) collective-permute-start(bf16[384,3072]{1,0:T(8,128)(2,1)} %get-tuple-element.315), channel_id=1, source_target_pairs={{0,1},{1,0},{2,3},{3,2},{4,5},{5,4},{6,7},{7,6},{8,9},{9,8},{10,11... | collective-permute-start | bytes 7077896 | tf_op jit(solution)/shard_map/ppermute | solution.py:146
  336.2 40.7 %collective-permute-start.27 = (bf16[1536,768]{1,0:T(8,128)(2,1)}, bf16[1536,768]{1,0:T(8,128)(2,1)}, u32[]{:S(2)}, u32[]{:S(2)}) collective-permute-start(bf16[1536,768]{1,0:T(8,128)(2,1)} %get-tuple-element.317), channel_id=1, source_target_pairs={{0,1},{1,0},{2,3},{3,2},{4,5},{5,4},{6,7},{7,6},{8,9},{9,8},{10,11... | collective-permute-start | bytes 7077896 | tf_op jit(solution)/shard_map/ppermute | solution.py:146
  380.9 81.7 %reduce-scatter.7.cloned.1.call-start = ((), (), s32[]{:S(2)}) async-start(), calls=%async_computation.5 | async-start | bytes 2949120 | tf_op jit(solution)/shard_map/reduce_scatter | solution.py:232
  385.4 137.5 %reduce-scatter.9.cloned.1.call-start = ((), (), s32[]{:S(2)}) async-start(), calls=%async_computation.6 | async-start | bytes 737280 | tf_op jit(solution)/shard_map/reduce_scatter | solution.py:232
  467.2 63.0 %reduce-scatter.11.cloned.1.call-start = ((), (), s32[]{:S(2)}) async-start(), calls=%async_computation.7 | async-start | bytes 2211840 | tf_op jit(solution)/shard_map/reduce_scatter | solution.py:232
  475.0 47.9 %collective-permute-start.37 = (bf16[4,208,768]{2,1,0:T(8,128)(2,1)}, bf16[4,208,768]{2,1,0:T(8,128)(2,1)}, u32[]{:S(2)}, u32[]{:S(2)}) collective-permute-start(bf16[4,208,768]{2,1,0:T(8,128)(2,1)} %get-tuple-element.566), channel_id=1, source_target_pairs={{2,0},{3,1},{4,6},{5,7},{10,8},{11,9},{12,14},{13,15},{18,16},{19,... | collective-permute-start | bytes 3833864 | tf_op jit(solution)/shard_map/ppermute | solution.py:192
  476.4 46.5 %collective-permute-start.38 = (bf16[4,208,768]{2,1,0:T(8,128)(2,1)}, bf16[4,208,768]{2,1,0:T(8,128)(2,1)}, u32[]{:S(2)}, u32[]{:S(2)}) collective-permute-start(bf16[4,208,768]{2,1,0:T(8,128)(2,1)} %get-tuple-element.388.refs_13_), channel_id=1, source_target_pairs={{0,1},{1,0},{2,3},{3,2},{4,5},{5,4},{6,7},{7,6},{8,9},{9,8},{10,11... | collective-permute-start | bytes 3833864 | tf_op jit(solution)/shard_map/ppermute | solution.py:146
  476.9 126.5 %all-reduce.21.cloned.1.call-start = ((), (), s32[]{:S(2)}) async-start(), calls=%async_computation.9 | async-start | bytes 1474560 | tf_op jit(solution)/shard_map/psum | solution.py:236
  545.8 112.6 %all-reduce.19.cloned.1.call-start = ((), (), s32[]{:S(2)}) async-start(), calls=%async_computation.8 | async-start | bytes 2064384 | tf_op jit(solution)/shard_map/psum | solution.py:236
  579.4 79.1 %collective-permute-start.43 = (bf16[8,768,128]{2,1,0:T(8,128)(2,1)}, bf16[8,768,128]{2,1,0:T(8,128)(2,1)}, u32[]{:S(2)}, u32[]{:S(2)}) collective-permute-start(bf16[8,768,128]{2,1,0:T(8,128)(2,1)} %constant_dynamic-slice_fusion.4), channel_id=1, source_target_pairs={{0,8},{8,0},{16,24},{24,16},{1,9},{9,1},{17,25},{25,17},{2,10},{10... | collective-permute-start | bytes 4718600 | tf_op jit(solution)/shard_map/ppermute | solution.py:141
  606.1 52.3 %collective-permute-start.45 = (bf16[8,768,128]{2,1,0:T(8,128)(2,1)}, bf16[8,768,128]{2,1,0:T(8,128)(2,1)S(1)}, u32[]{:S(2)}, u32[]{:S(2)}) collective-permute-start(bf16[8,768,128]{2,1,0:T(8,128)(2,1)} %constant_dynamic-slice_fusion.2), channel_id=1, source_target_pairs={{0,16},{8,24},{16,0},{24,8},{1,17},{9,25},{17,1},{25,9},{2,18},{10... | collective-permute-start | bytes 4718600 | tf_op jit(solution)/shard_map/ppermute | solution.py:141
  (241 other events, 2737.8 us)
Sparse Core Ops, SparseCore 0:
  381.1 37.3 reduce-scatter.4
  422.1 37.3 reduce-scatter.6
  467.3 26.5 reduce-scatter.8
  497.7 32.4 reduce-scatter.10
  545.9 57.4 all-reduce.20
  607.7 50.6 all-reduce.18

commit v5 on v4

--- a/solution.py
+++ b/solution.py
@@ -432,9 +432,10 @@
 def embed_kernel(first, count, at_ref, low_ref, *refs):
     weight_refs, pixel_refs = refs[:count], refs[count : count + 2]
     if first:
-        total_ref, kernel_ref, weight_now = refs[count + 2 :]
+        total_refs, kernel_ref, weight_now = refs[count + 2 : count + 4], *refs[count + 4 :]
     else:
-        before_ref, _, total_ref, kernel_ref, weight_now = refs[count + 2 :]
+        before_refs = refs[count + 2 : count + 4]
+        total_refs, kernel_ref, weight_now = refs[count + 5 : count + 7], *refs[count + 7 :]
     share = pixel_refs[0].shape[1]
     images = 2 * share
     cells = weight_now.shape[0]
@@ -442,10 +443,11 @@
 
     @pl.when(pl.program_id(0) == 0)
     def _():
-        if first:
-            total_ref[...] = jnp.zeros_like(total_ref)
-        else:
-            total_ref[...] = before_ref[...]
+        for at, total_ref in enumerate(total_refs):
+            if first:
+                total_ref[...] = jnp.zeros_like(total_ref)
+            else:
+                total_ref[...] = before_refs[at][...]
 
     for at in range(count):
 
@@ -462,7 +464,7 @@
             ]
     for image in range(images):
         block = pixel_refs[image // share][0, image % share]
-        total_ref[image] += dot_nn(block, kernel_ref[0, image])
+        total_refs[image // share][image % share] += dot_nn(block, kernel_ref[0, image])
 
 
 def embed_piece(place, low, weights, pixels, total, kernels):
@@ -475,12 +477,12 @@
     bands = lanes // (4 * step)
     first = total is None
     any_spec = pl.BlockSpec(memory_space=pl.ANY)
-    whole_total = pl.BlockSpec((images, rows, width), lambda t, at: (0, 0, 0))
+    whole_total = pl.BlockSpec((share, rows, width), lambda t, at: (0, 0, 0))
     if count == 1:
         weight_specs = [pl.BlockSpec((step, width, depth), lambda t, at: (t, 0, 0))]
     else:
         weight_specs = [pl.BlockSpec((step, width, depth), lambda t, at: (0, 0, 0))] * count
-    return pl.pallas_call(
+    own, other, kernels = pl.pallas_call(
         partial(embed_kernel, first, count),
         grid_spec=pltpu.PrefetchScalarGridSpec(
             num_scalar_prefetch=1,
@@ -493,8 +495,9 @@
                 ),
             ]
             * 2
-            + ([] if first else [whole_total, any_spec]),
+            + ([] if first else [whole_total, whole_total, any_spec]),
             out_specs=[
+                whole_total,
                 whole_total,
                 pl.BlockSpec(
                     (1, images, step * bands, width), lambda t, at: (at[0], 0, at[1 + t], 0)
@@ -503,14 +506,16 @@
             scratch_shapes=[pltpu.VMEM((step, width, depth), jnp.bfloat16)],
         ),
         out_shape=[
-            jax.ShapeDtypeStruct((images, rows, width), jnp.float32),
+            jax.ShapeDtypeStruct((share, rows, width), jnp.float32),
+            jax.ShapeDtypeStruct((share, rows, width), jnp.float32),
             jax.ShapeDtypeStruct((pieces, images, lanes, width), jnp.bfloat16),
         ],
-        input_output_aliases={} if first else {4 + count: 0, 5 + count: 1},
+        input_output_aliases={} if first else {4 + count: 0, 5 + count: 1, 6 + count: 2},
         compiler_params=grid_params(48),
         cost_estimate=pl.CostEstimate(flops=1, bytes_accessed=1, transcendentals=0),
         name="embed_piece",
-    )(place, low, *weights, *pixels, *(() if first else (total, kernels)))
+    )(place, low, *weights, *pixels, *(() if first else (*total, kernels)))
+    return (own, other), kernels
 
 
 def pixel_grad_kernel(grad_ref, kernel_ref, rate_ref, out_ref):
@@ -520,21 +525,21 @@
         ).astype(jnp.bfloat16)
 
 
-def pixel_grads(grads, kernels, rates):
+def pixel_grads(grads, kernels, rates, half):
     pieces, images, lanes, width = kernels.shape
     rows = grads.shape[1]
     share = images // 2
     return pl.pallas_call(
         pixel_grad_kernel,
-        grid=(2, pieces),
+        grid=(pieces,),
         in_specs=[
-            pl.BlockSpec((share, rows, width), lambda i, j: (i, 0, 0)),
-            pl.BlockSpec((1, share, lanes, width), lambda i, j: (j, i, 0, 0)),
-            pl.BlockSpec((share, 1, lanes), lambda i, j: (i, 0, 0)),
+            pl.BlockSpec((share, rows, width), lambda j: (half, 0, 0)),
+            pl.BlockSpec((1, share, lanes, width), lambda j: (j, half, 0, 0)),
+            pl.BlockSpec((share, 1, lanes), lambda j: (half, 0, 0)),
         ],
-        out_specs=pl.BlockSpec((1, share, rows, lanes), lambda i, j: (j, i, 0, 0)),
-        out_shape=jax.ShapeDtypeStruct((pieces, images, rows, lanes), jnp.bfloat16),
-        compiler_params=grid_params(40, 2),
+        out_specs=pl.BlockSpec((1, share, rows, lanes), lambda j: (j, 0, 0, 0)),
+        out_shape=jax.ShapeDtypeStruct((pieces, share, rows, lanes), jnp.bfloat16),
+        compiler_params=grid_params(40),
         cost_estimate=pl.CostEstimate(flops=1, bytes_accessed=1, transcendentals=0),
         name="pixel_grads",
     )(grads, kernels, rates)
@@ -1294,7 +1299,8 @@
         weights3.append(jnp.concatenate(corner3))
         total, kernels = added(state, spots3, weights3[3:], (3,))
     image_bias = jnp.dot(bias_vec, bias_weight, precision=highest) + bias_offset
-    total_beside = swap_batch(total[images:], 1)
+    total, total_other = total
+    total_beside = swap_batch(total_other, 1)
     joint_bias = jnp.concatenate([qv_bias[0], jnp.zeros_like(qv_bias[0]), qv_bias[1]])
     embedded, normed1, joint = make_joint(
         total, total_beside, image_bias, norm_gain[0], norm_shift[0], w_qkv, joint_bias
@@ -1345,6 +1351,9 @@
     grad_qv_bias = joint_sum.reshape(3, model_width)[::2]
     attended = attended.reshape(rows, model_width)
     grad_branch = grad_branch.reshape(rows, model_width)
+    beside_emb = swap_batch(grad_emb, 1)
+    if tuned_mesh():
+        right1, left1 = (along_line(grad_emb, -1), along_line(grad_emb, 1))
     share_up = row_share(add_low(up_keep, up_came))
     share_down = row_share(add_low(down_keep, down_came))
 
@@ -1357,9 +1366,6 @@
         normed1.reshape(rows, model_width),
         grad_joint.reshape(rows, 3 * model_width),
     )
-    beside_emb = swap_batch(grad_emb, 1)
-    if tuned_mesh():
-        right1, left1 = (along_line(grad_emb, -1), along_line(grad_emb, 1))
     grad_bias_weight = jnp.einsum("ik,ie->ke", bias_vec, grad_image_bias, precision=highest)
     grad_bias_offset = jnp.sum(grad_image_bias, axis=0)
     grad_bias_vec = jnp.einsum("ie,ke->ik", grad_image_bias, bias_weight, precision=highest)
@@ -1440,14 +1446,13 @@
         line_emb += [far, swap_batch(far, 1)]
         hyper_grads = finish_low(grad_vectors)
         wide, narrow, parts, small = pack(hyper_grads)
-        small, block_out, end3, line_emb, chip_emb, share_out_rows, share_qkv = tie(
-            small, block_out, end3, line_emb, chip_emb, share_out_rows, share_qkv
-        )
+        line_pixels = [pixel_block(0, 0), pixel_block(0, 1)]
+        small, end3, line_emb, line_pixels = tie(small, end3, line_emb, line_pixels)
         small_came = swap_batch(part_of(small, 1 - core, 2), 1)
         far = jnp.where(chip == 1, right1, jnp.where(chip == 2, left1, end3))
         line_emb += [far, swap_batch(far, 1)]
         small, small_came, line_emb = tie(small, small_came, line_emb)
-        line_pixels = [pixel_block(0, 0), pixel_block(0, 1)] + pixels1 + pixels2 + pixels3
+        line_pixels += pixels1 + pixels2 + pixels3
     else:
         for at, weight in enumerate(plain_weight_pieces(kernel_weight)):
             grad_vectors = band_piece(
@@ -1470,10 +1475,10 @@
             )
             kernel_share += found.astype(jnp.float32)
         kernel_total = lax.psum(kernel_share.astype(jnp.bfloat16), "group").astype(jnp.float32)
-        chip_back = pixel_grads(chip_emb, kernels, rates)
-        other_back = swap_batch(chip_back[:, images:], 1)
+        own_back = pixel_grads(chip_emb, kernels, rates, 0)
+        other_back = swap_batch(pixel_grads(chip_emb, kernels, rates, 1), 1)
         pixel_grad = join_pixels(
-            chip_back[:, :images], other_back, core, patches, cells, pixel_cells, band_slots
+            own_back, other_back, core, patches, cells, pixel_cells, band_slots
         )
         small = lax.psum(small, ("group", "batch"))
         totals = [
@@ -1486,31 +1491,37 @@
         small = part_of(small, core, 2) + small_came
         small_came = [small_hop(1), small_hop(2)]
         kernel_one = line_grads(low_turned, cells, line_pixels, line_emb, 0, 2)
-        kernel_one, line_emb, small, small_came = tie(kernel_one, line_emb, small, small_came)
+        kernel_one, line_emb, small, small_came, share_out_rows, share_qkv = tie(
+            kernel_one, line_emb, small, small_came, share_out_rows, share_qkv
+        )
 
         small_came.append(small_hop(3))
         kernel_two = line_grads(low_turned, cells, line_pixels, line_emb, 1, 2)
-        mine_up, mine_out = row_mine(share_up), row_mine(share_out_rows)
-        kernel_two, small_came, mine_up, mine_out, share_down, share_qkv = tie(
-            kernel_two, small_came, mine_up, mine_out, share_down, share_qkv
-        )
+        kernel_two, small_came = tie(kernel_two, small_came)
 
         sums = [kernel_one, kernel_two]
-        mine_down, mine_qkv = row_mine(share_down), row_mine(share_qkv)
+        mine_qkv, mine_out, mine_up, mine_down = [
+            row_mine(share) for share in (share_qkv, share_out_rows, share_up, share_down)
+        ]
         came = sum_out(sums, False)
         small = sum(small_came, part_of(small, chip, 4))
         small_came = swap_group(small, 1)
-        chip_back = pixel_grads(chip_emb, kernels, rates)
-        chip_back, came, small_came, mine_down, mine_qkv = tie(
-            chip_back, came, small_came, mine_down, mine_qkv
+        own_back = pixel_grads(chip_emb, kernels, rates, 0)
+        other_back = pixel_grads(chip_emb, kernels, rates, 1)
+        own_back, other_back, came, small_came, mine_qkv, mine_out, mine_up, mine_down = tie(
+            own_back, other_back, came, small_came, mine_qkv, mine_out, mine_up, mine_down
         )
 
         sums = sum_in(sums, came, False)
         came = sum_out(sums, True)
         small = small + small_came
         small_came = swap_group(small, 2)
-        own_back, other_back = chip_back[:, :images], swap_batch(chip_back[:, images:], 1)
-        came, own_back, other_back, small_came = tie(came, own_back, other_back, small_came)
+        other_back = swap_batch(other_back, 1)
+        wide_mine = jnp.concatenate([mine_qkv, mine_out, mine_up], axis=1)
+        wide_came = swap_batch(wide_mine, 1)
+        came, other_back, small_came, wide_came, block_out = tie(
+            came, other_back, small_came, wide_came, block_out
+        )
 
         sums = sum_in(sums, came, True)
         came = share_out(sums, True)
@@ -1519,25 +1530,24 @@
         pixel_grad = join_pixels(
             own_back, other_back, core, patches, cells, pixel_cells, band_slots
         )
-        came, small, small_came, pixel_grad = tie(came, small, small_came, pixel_grad)
+        down_came = swap_batch(mine_down, 1)
+        came, small, small_came, pixel_grad, down_came = tie(
+            came, small, small_came, pixel_grad, down_came
+        )
 
         sums = share_in(sums, came, True)
         early, late = ([value[: cells // 8] for value in sums], [value[cells // 8 :] for value in sums])
         early = share_out(early, False)
         small_came.append(swap_batch(small, 6))
-        wide_mine = jnp.concatenate([mine_qkv, mine_out, mine_up], axis=1)
-        wide_came, down_came = swap_batch(wide_mine, 1), swap_batch(mine_down, 1)
-        early, late, small_came, wide_came, down_came = tie(
-            early, late, small_came, wide_came, down_came
-        )
-        late = share_out(late, False)
-        small = four_in_order(chip, [small] + small_came)
-        small = in_order(core, small, swap_batch(small, 1))
         widths = [mine.shape[1] for mine in (mine_qkv, mine_out, mine_up)]
         wide_both = in_order(core, wide_mine, wide_came).astype(jnp.float32)
         ends = [0, widths[0], widths[0] + widths[1], sum(widths)]
         totals = [wide_both[:, ends[at] : ends[at + 1]] for at in range(3)]
         totals.append(in_order(core, mine_down, down_came).astype(jnp.float32))
+        early, late, small_came, totals = tie(early, late, small_came, totals)
+        late = share_out(late, False)
+        small = four_in_order(chip, [small] + small_came)
+        small = in_order(core, small, swap_batch(small, 1))
     pixel_grad = pixel_grad[None]
 
     found = []
@@ -1551,9 +1561,7 @@
         at += count
     batch_mean, batch_var = bin_stats(found[13], found[14], found[15], patches * pixel_cells)
     if tuned_mesh():
-        late, found, totals, batch_mean, batch_var = tie(
-            late, found, totals, batch_mean, batch_var
-        )
+        late, found, batch_mean, batch_var = tie(late, found, batch_mean, batch_var)
         bits = jnp.stack([group & 1, group >> 1])
         kernel_total = assemble(bits, sums, early, late)
     return (

time: 816 us -> 808 us (level)
  waiting for transfers between devices: 167 us -> 141 us
  local copies, waits for them, and re-layouts: 165 us -> 185 us
    unnamed x404 -> x428, local copies, waits for them, and re-layouts: 64.5 us -> 87 us
    ppermute x33, waiting for transfers between devices: 35.3 us -> 17.7 us  [swap_batch(): lax.ppermute(value, 'batch', [(at, at ^ bits) for at in range(count)])]
    slice x2 -> x0, local copies, waits for them, and re-layouts: 10.5 us -> none  [the longest x1 7.02 us: per_device(): chip_back[:, images:]]
    psum x2 -> x1, waiting for transfers between devices: 38.8 us -> 36.4 us  [row_mine(): return lax.psum(share, 'batch', axis_index_groups=same_core())]
  transfers between devices with their start and end apart: 69 -> 68, of which waited for: 24 -> 22; matrix products, arithmetic and copies ran while one was open for 22% -> 24% of each run, Pallas kernels for 30% -> 30%
where the time goes in v5:
time: 808 us; the launch traced here: 798 us
  Pallas kernels  257 us (32%)
  local copies, waits for them, and re-layouts  185 us (23%)
  waiting for transfers between devices  141 us (17%)
  starting transfers between devices  87 us (11%)
  other arithmetic  79.2 us (10%)
  matrix products  32.7 us (4%)
  between operations  16.6 us (2%)
    unnamed x428, local copies, waits for them, and re-layouts  87 us
    pallas_call x7, Pallas kernels, embed_piece(): pl.pallas_call(partial(embed_kernel, first, count), grid_spec=pltpu.Prefe...  64.8 us
    ppermute x20, waiting for transfers between devices, swap_group(): return lax.ppermute(value, 'group', [(at, at ^ bits) for at in range(4)])  48 us
    ppermute x33, starting transfers between devices, swap_batch(): lax.ppermute(value, 'batch', [(at, at ^ bits) for at in range(count)])  39.7 us
    psum x1, waiting for transfers between devices, row_mine(): return lax.psum(share, 'batch', axis_index_groups=same_core())  36.4 us
    pallas_call x1, Pallas kernels, mlp(): pl.pallas_call(mlp_kernel, grid_spec=pltpu.PrefetchScalarGridSpec(num_sca...  33.5 us
    pallas_call x4, Pallas kernels, band_piece(): pl.pallas_call(partial(band_kernel, first, count), grid_spec=pltpu.Prefet...  31.8 us
    ppermute x8, waiting for transfers between devices, along_line(): return lax.ppermute(value, 'batch', pairs)  30.3 us
  transfers between devices with their start and end apart: 68, of which 22 were waited for; matrix products, arithmetic and copies ran while one was open for 24% of the time, Pallas kernels for 30%

profile of v5, /device:TPU:0, one launch (start us, length us, event | category | flops | bytes accessed | tf_op | source)
XLA Modules:
  0.0 798.0 jit_solution(15243333104073919341)
XLA Ops:
  27.8 22.1 %collective-permute-done = bf16[8,768,128]{2,1,0:T(8,128)(2,1)} collective-permute-done((bf16[8,768,128]{2,1,0:T(8,128)(2,1)}, bf16[8,768,128]{2,1,0:T(8,128)(2,1)}, u32[]{:S(2)}, u32[]{:S(2)}) %collective-permute-start) | collective-permute-done | bytes 1572896 | tf_op jit(solution)/shard_map/ppermute | solution.py:187
  63.4 15.3 %split_pixels.1 = (bf16[4,4,208,512]{3,2,1,0:T(8,128)(2,1)S(1)}, bf16[4,4,208,512]{3,2,1,0:T(8,128)(2,1)}) custom-call(s32[1]{0:T(128)} %bitcast.core_ref, bf16[4,196,16,256]{3,2,1,0:T(8,128)(2,1)S(1)} %bitcast.255, f32[4,16,1]{2,1,0:T(8,128)S(1)} %convolution_bitcast_fusion.7.mean_ref, f32[4,16,1]{2,1,0:T(8,128)S(1)} %copy.155.rate_ref), custom_call_target="tpu_custom_call" | custom-call | flops 1 | bytes 1 | tf_op jit(solution)/shard_map/split_pixels/pallas_call | solution.py:356
  80.6 7.6 collective-permute-done.5.refs_1_
  108.0 8.4 %collective-permute-start.11 = (bf16[4,208,512]{2,1,0:T(8,128)(2,1)}, bf16[4,208,512]{2,1,0:T(8,128)(2,1)S(1)}, u32[]{:S(2)}, u32[]{:S(2)}) collective-permute-start(bf16[4,208,512]{2,1,0:T(8,128)(2,1)} %dynamic-slice_bitcast_fusion.7), channel_id=1, source_target_pairs={{0,4},{1,5},{2,6},{3,7},{4,0},{5,1},{6,2},{7,3},{8,12},{9,13},{10,... | collective-permute-start | bytes 2555912 | tf_op jit(solution)/shard_map/ppermute | solution.py:146
  123.2 10.2 %embed_piece.7 = (f32[4,208,768]{2,1,0:T(8,128)S(1)}, f32[4,208,768]{2,1,0:T(8,128)S(1)}, bf16[4,8,512,768]{3,2,1,0:T(8,128)(2,1)}) custom-call(s32[5]{0:T(128)S(1)} %stack.90.at_ref, bf16[128,128]{1,0:T(8,128)(2,1)S(1)} %copy.165.low_ref, bf16[32,768,128]{2,1,0:T(8,128)(2,1)} %refs_0_.3, bf16[4,4,208,512]{3,2,1,0:T(8,128)(2,1)} %copy-done.1, ...), custom_call_target="tpu_custom_call" | custom-call | flops 1 | bytes 1 | tf_op jit(solution)/shard_map/embed_piece/pallas_call | solution.py:485
  136.3 11.8 %embed_piece.8 = (f32[4,208,768]{2,1,0:T(8,128)}, f32[4,208,768]{2,1,0:T(8,128)}, bf16[4,8,512,768]{3,2,1,0:T(8,128)(2,1)}) custom-call(s32[4]{0:T(128)S(1)} %add_add_fusion.4.at_ref, bf16[128,128]{1,0:T(8,128)(2,1)S(1)} %copy.165.low_ref, bf16[8,768,128]{2,1,0:T(8,128)(2,1)S(1)} %copy-done.25, ...), custom_call_target="tpu_custom_call", output_to_operand_aliasing={{0}: (7, {}), {1}: (8, {}), {2}: (9, {})} | custom-call | flops 1 | bytes 1 | tf_op jit(solution)/shard_map/embed_piece/pallas_call | solution.py:485
  152.9 8.7 %collective-permute-done.8 = bf16[8,768,128]{2,1,0:T(8,128)(2,1)} collective-permute-done((bf16[8,768,128]{2,1,0:T(8,128)(2,1)}, bf16[8,768,128]{2,1,0:T(8,128)(2,1)}, u32[]{:S(2)}, u32[]{:S(2)}) %collective-permute-start.8) | collective-permute-done | bytes 1572896 | tf_op jit(solution)/shard_map/ppermute | solution.py:192
  198.0 11.8 %embed_piece.10 = (f32[4,208,768]{2,1,0:T(8,128)}, f32[4,208,768]{2,1,0:T(8,128)}, bf16[4,8,512,768]{3,2,1,0:T(8,128)(2,1)}) custom-call(s32[4]{0:T(128)S(1)} %get-tuple-element.638.at_ref, bf16[128,128]{1,0:T(8,128)(2,1)S(1)} %copy.165.low_ref, ...), custom_call_target="tpu_custom_call", output_to_operand_aliasing={{0}: (7, {}), {1}: (8, {}), {2}: (9, {})} | custom-call | flops 1 | bytes 1 | tf_op jit(solution)/shard_map/embed_piece/pallas_call | solution.py:485
  211.4 7.4 collective-permute-done.15.refs_6_
  239.9 12.2 %embed_piece.12 = (f32[4,208,768]{2,1,0:T(8,128)}, f32[4,208,768]{2,1,0:T(8,128)}, bf16[4,8,512,768]{3,2,1,0:T(8,128)(2,1)}) custom-call(s32[4]{0:T(128)S(1)} %get-tuple-element.637.at_ref, bf16[128,128]{1,0:T(8,128)(2,1)S(1)} %copy.165.low_ref, bf16[8,768,128]{2,1,0:T(8,128)(2,1)S(1)} %copy-done.18, ...), custom_call_target="tpu_custom_call", output_to_operand_aliasing={{0}: (7, {}), {1}: (8, {}), {2}: (9, {})} | custom-call | flops 1 | bytes 1 | tf_op jit(solution)/shard_map/embed_piece/pallas_call | solution.py:485
  304.8 33.5 %mlp.1 = (bf16[832,768]{1,0:T(8,128)(2,1)S(1)}, f32[832,768]{1,0:T(8,128)}, bf16[384,3072]{1,0:T(8,128)(2,1)}, bf16[384,3072]{1,0:T(8,128)(2,1)}, bf16[1536,768]...) custom-call(s32[1]{0:T(128)} %bitcast.core_ref, bf16[832,768]{1,0:T(8,128)(2,1)} %bitcast.262, ...), custom_call_target="tpu_custom_call" | custom-call | flops 1 | bytes 1 | tf_op jit(solution)/shard_map/mlp/pallas_call | solution.py:1048
  354.0 17.0 %attend_back.1 = (bf16[4,208,2304]{2,1,0:T(8,128)(2,1)S(1)}, f32[1,2304]{1,0:T(1,128)S(1)}) custom-call(bf16[4,208,2304]{2,1,0:T(8,128)(2,1)S(1)} %copy-done.21, bf16[4,208,768]{2,1,0:T(8,128)(2,1)S(1)} %get-tuple-element.327.grad_ref), custom_call_target="tpu_custom_call" | custom-call | flops 1 | bytes 1 | tf_op jit(solution)/shard_map/attend_back/pallas_call | solution.py:759
  412.7 8.5 %band_piece.4.refs_6_ = f32[128,128]{1,0:T(8,128)S(1)} custom-call(s32[5]{0:T(128)S(1)} %stack.90.at_ref, bf16[8,208,768]{2,1,0:T(8,128)(2,1)S(1)} %constant_dynamic-update-slice_fusion.2.grad_ref, bf16[32,768,128]{2,1,0:T(8,128)(2,1)} %refs_0_.3, bf16[4,4,208,512]{3,2,1,0:T(8,128)(2,1)S(1)} %copy-done.2, ...), custom_call_target="tpu_custom_call" | custom-call | flops 1 | bytes 1 | tf_op jit(solution)/shard_map/band_piece/pallas_call | solution.py:644
  424.3 7.7 band_piece.5.refs_6_
  448.3 8.0 %band_piece.6.refs_6_ = f32[128,128]{1,0:T(8,128)S(1)} custom-call(s32[5]{0:T(128)S(1)} %copy-done.86, bf16[8,208,768]{2,1,0:T(8,128)(2,1)S(1)} %copy-done.13, bf16[8,768,128]{2,1,0:T(8,128)(2,1)S(1)} %get-tuple-element.563.refs_0_, bf16[12,768,128]{2,1,0:T(8,128)(2,1)} %collective-permute-done.9.refs_1_, ...), custom_call_target="tpu_custom_call" | custom-call | flops 1 | bytes 1 | tf_op jit(solution)/shard_map/band_piece/pallas_call | solution.py:644
  456.4 7.6 band_piece.7
  528.3 8.5 %concatenate.127 = f32[128,128]{1,0:T(8,128)S(1)} concatenate(f32[1,128]{1,0:T(1,128)} %bitcast.310, f32[2,128]{1,0:T(2,128)S(1)} %pad_add_fusion.7, f32[1,128]{1,0:T(1,128)} %bitcast.309, f32[2,128]{1,0:T(2,128)} %pad_add_fusion.6, f32[2,128]{1,0:T(2,128)} %pad_add_fusion.5, f32[16,128]{1,0:T(8,128)} %bitcast.293, f32[1,128]{1,0:T(1,128)} %bitcast.308, f32[4,128]{1,0:T(4,128)} %bitcast.304, ...), dimensions={0} | concatenate | bytes 131072 | tf_op jit(solution)/shard_map/concatenate | solution.py:1404
  561.9 12.3 %line_grads.2 = bf16[16,768,128]{2,1,0:T(8,128)(2,1)} custom-call(bf16[128,512]{1,0:T(8,128)(2,1)S(1)} %bitcast.265, bf16[4,208,512]{2,1,0:T(8,128)(2,1)S(1)} %dynamic-slice_bitcast_fusion.1.refs_1_, bf16[4,208,512]{2,1,0:T(8,128)(2,1)S(1)} %get-tuple-element.372.refs_2_, bf16[4,208,512]{2,1,0:T(8,128)(2,1)S(1)} %copy-done.54, ...), custom_call_target="tpu_custom_call" | custom-call | flops 1 | bytes 1 | tf_op jit(solution)/shard_map/line_grads/pallas_call | solution.py:583
  584.7 12.2 %line_grads.3 = bf16[16,768,128]{2,1,0:T(8,128)(2,1)} custom-call(bf16[128,512]{1,0:T(8,128)(2,1)S(1)} %bitcast.266, bf16[4,208,512]{2,1,0:T(8,128)(2,1)S(1)} %dynamic-slice_bitcast_fusion.1.refs_1_, bf16[4,208,512]{2,1,0:T(8,128)(2,1)S(1)} %get-tuple-element.372.refs_2_, bf16[4,208,512]{2,1,0:T(8,128)(2,1)S(1)} %copy-done.55, ...), custom_call_target="tpu_custom_call" | custom-call | flops 1 | bytes 1 | tf_op jit(solution)/shard_map/line_grads/pallas_call | solution.py:583
  613.2 7.6 pixel_grads.2.mine_ref
  626.0 36.4 %all-reduce.17.cloned.1.call-done = (bf16[96,2304]{1,0:T(8,128)(2,1)}, bf16[96,768]{1,0:T(8,128)(2,1)}, bf16[96,3072]{1,0:T(8,128)(2,1)}, bf16[384,768]{1,0:T(8,128)(2,1)}) async-done(((bf16[96,2304]{1,0:T(8,128)(2,1)}, bf16[96,768]{1,0:T(8,128)(2,1)}, bf16[96,3072]{1,0:T(8,128)(2,1)}, bf16[384,768]{1,0:T(8,128)(2,1)}), (bf16[96,2304]{1,0:T(8,128)(2,1)}, bf16[96,768]{1,0:T(8,128)(2,1)}, ...) | async-done | bytes 1769488 | tf_op jit(solution)/shard_map/psum | solution.py:236
  679.3 23.4 %collective-permute-done.50 = f32[704,128]{1,0:T(8,128)} collective-permute-done((f32[704,128]{1,0:T(8,128)}, f32[704,128]{1,0:T(8,128)}, u32[]{:S(2)}, u32[]{:S(2)}) %collective-permute-start.50) | collective-permute-done | bytes 360480 | tf_op jit(solution)/shard_map/ppermute | solution.py:141
  712.9 13.9 %join_pixels.1 = bf16[4,196,16,256]{3,2,1,0:T(8,128)(2,1)} custom-call(s32[1]{0:T(128)} %bitcast.core_ref, bf16[4,4,208,512]{3,2,1,0:T(8,128)(2,1)S(1)} %copy-done.36, bf16[4,4,208,512]{3,2,1,0:T(8,128)(2,1)} %collective-permute-done.49.other_ref), custom_call_target="tpu_custom_call" | custom-call | flops 1 | bytes 1 | tf_op jit(solution)/shard_map/join_pixels/pallas_call | solution.py:415
  783.7 7.6 assemble.1
  (785 shorter events, 462.0 us)
Async XLA Ops:
  7.3 424.7 %reduce-scatter.5.cloned.1.call-start = ((), (), s32[]{:S(2)}) async-start(), calls=%async_computation.4 | async-start | bytes 2949120 | tf_op jit(solution)/shard_map/reduce_scatter | solution.py:232
  102.0 59.6 %collective-permute-start.10 = (bf16[12,768,128]{2,1,0:T(8,128)(2,1)}, bf16[12,768,128]{2,1,0:T(8,128)(2,1)}, u32[]{:S(2)}, u32[]{:S(2)}) collective-permute-start(bf16[12,768,128]{2,1,0:T(8,128)(2,1)} %get-tuple-element.597), channel_id=1, source_target_pairs={{0,16},{8,24},{16,0},{24,8},{1,17},{9,25},{17,1},{25,9},{2,18},{10... | collective-permute-start | bytes 7077896 | tf_op jit(solution)/shard_map/ppermute | solution.py:141
  102.5 59.1 %collective-permute-start.9 = (bf16[12,768,128]{2,1,0:T(8,128)(2,1)}, bf16[12,768,128]{2,1,0:T(8,128)(2,1)}, u32[]{:S(2)}, u32[]{:S(2)}) collective-permute-start(bf16[12,768,128]{2,1,0:T(8,128)(2,1)} %get-tuple-element.598), channel_id=1, source_target_pairs={{0,8},{8,0},{16,24},{24,16},{1,9},{9,1},{17,25},{25,17},{2,10},{10... | collective-permute-start | bytes 7077896 | tf_op jit(solution)/shard_map/ppermute | solution.py:141
  103.2 58.4 %collective-permute-start.8 = (bf16[8,768,128]{2,1,0:T(8,128)(2,1)}, bf16[8,768,128]{2,1,0:T(8,128)(2,1)}, u32[]{:S(2)}, u32[]{:S(2)}) collective-permute-start(bf16[8,768,128]{2,1,0:T(8,128)(2,1)} %get-tuple-element.564), channel_id=1, source_target_pairs={{2,0},{3,1},{4,6},{5,7},{10,8},{11,9},{12,14},{13,15},{18,16},{19,... | collective-permute-start | bytes 4718600 | tf_op jit(solution)/shard_map/ppermute | solution.py:192
  108.0 44.9 %collective-permute-start.11 = (bf16[4,208,512]{2,1,0:T(8,128)(2,1)}, bf16[4,208,512]{2,1,0:T(8,128)(2,1)S(1)}, u32[]{:S(2)}, u32[]{:S(2)}) collective-permute-start(bf16[4,208,512]{2,1,0:T(8,128)(2,1)} %dynamic-slice_bitcast_fusion.7), channel_id=1, source_target_pairs={{0,4},{1,5},{2,6},{3,7},{4,0},{5,1},{6,2},{7,3},{8,12},{9,13},{10,... | collective-permute-start | bytes 2555912 | tf_op jit(solution)/shard_map/ppermute | solution.py:146
  170.6 52.9 %collective-permute-start.12 = (bf16[12,768,128]{2,1,0:T(8,128)(2,1)}, bf16[12,768,128]{2,1,0:T(8,128)(2,1)}, u32[]{:S(2)}, u32[]{:S(2)}) collective-permute-start(bf16[12,768,128]{2,1,0:T(8,128)(2,1)} %get-tuple-element.596), channel_id=1, source_target_pairs={{0,8},{8,0},{16,24},{24,16},{1,9},{9,1},{17,25},{25,17},{2,10},{10... | collective-permute-start | bytes 7077896 | tf_op jit(solution)/shard_map/ppermute | solution.py:141
  171.9 52.6 %collective-permute-start.13 = (bf16[12,768,128]{2,1,0:T(8,128)(2,1)}, bf16[12,768,128]{2,1,0:T(8,128)(2,1)}, u32[]{:S(2)}, u32[]{:S(2)}) collective-permute-start(bf16[12,768,128]{2,1,0:T(8,128)(2,1)} %get-tuple-element.595), channel_id=1, source_target_pairs={{0,16},{8,24},{16,0},{24,8},{1,17},{9,25},{17,1},{25,9},{2,18},{10... | collective-permute-start | bytes 7077896 | tf_op jit(solution)/shard_map/ppermute | solution.py:141
  177.7 41.1 %collective-permute-start.15 = (bf16[4,208,512]{2,1,0:T(8,128)(2,1)}, bf16[4,208,512]{2,1,0:T(8,128)(2,1)}, u32[]{:S(2)}, u32[]{:S(2)}) collective-permute-start(bf16[4,208,512]{2,1,0:T(8,128)(2,1)} %dynamic-slice_bitcast_fusion.5), channel_id=1, source_target_pairs={{0,4},{1,5},{2,6},{3,7},{4,0},{5,1},{6,2},{7,3},{8,12},{9,13},{10,... | collective-permute-start | bytes 2555912 | tf_op jit(solution)/shard_map/ppermute | solution.py:146
  264.4 76.4 %collective-permute-start.20 = (bf16[4,208,512]{2,1,0:T(8,128)(2,1)}, bf16[4,208,512]{2,1,0:T(8,128)(2,1)S(1)}, u32[]{:S(2)}, u32[]{:S(2)}) collective-permute-start(bf16[4,208,512]{2,1,0:T(8,128)(2,1)} %dynamic-slice_bitcast_fusion.3), channel_id=1, source_target_pairs={{0,6},{1,7},{2,4},{3,5},{4,2},{5,3},{6,0},{7,1},{8,14},{9,15},{10,... | collective-permute-start | bytes 2555912 | tf_op jit(solution)/shard_map/ppermute | solution.py:146
  294.9 44.4 %collective-permute-start.21 = (bf16[128,128]{0,1:T(8,128)(2,1)S(1)}, bf16[128,128]{0,1:T(8,128)(2,1)S(1)}, u32[]{:S(2)}, u32[]{:S(2)}) collective-permute-start(bf16[128,128]{0,1:T(8,128)(2,1)S(1)} %pad_maximum_fusion.11), channel_id=1, source_target_pairs={{0,2},{1,3},{2,0},{3,1},{4,6},{5,7},{6,4},{7,5},{8,10},{9,11},{10,... | collective-permute-start | bytes 98312 | tf_op jit(solution)/shard_map/ppermute | solution.py:146
  296.1 43.2 %collective-permute-start.22 = (bf16[128,128]{0,1:T(8,128)(2,1)S(1)}, bf16[128,128]{0,1:T(8,128)(2,1)S(1)}, u32[]{:S(2)}, u32[]{:S(2)}) collective-permute-start(bf16[128,128]{0,1:T(8,128)(2,1)S(1)} %pad_maximum_fusion.11), channel_id=1, source_target_pairs={{0,4},{1,5},{2,6},{3,7},{4,0},{5,1},{6,2},{7,3},{8,12},{9,13},{10,... | collective-permute-start | bytes 98312 | tf_op jit(solution)/shard_map/ppermute | solution.py:146
  296.1 43.2 %collective-permute-start.23 = (bf16[128,128]{0,1:T(8,128)(2,1)S(1)}, bf16[128,128]{0,1:T(8,128)(2,1)}, u32[]{:S(2)}, u32[]{:S(2)}) collective-permute-start(bf16[128,128]{0,1:T(8,128)(2,1)S(1)} %pad_maximum_fusion.11), channel_id=1, source_target_pairs={{0,6},{1,7},{2,4},{3,5},{4,2},{5,3},{6,0},{7,1},{8,14},{9,15},{10,... | collective-permute-start | bytes 98312 | tf_op jit(solution)/shard_map/ppermute | solution.py:146
  299.4 42.4 %collective-permute-start.24 = (f32[4,512]{1,0:T(4,128)S(1)}, f32[4,512]{1,0:T(4,128)S(1)}, u32[]{:S(2)}, u32[]{:S(2)}) collective-permute-start(f32[4,512]{1,0:T(4,128)S(1)} %tile.10), channel_id=1, source_target_pairs={{0,1},{1,0},{2,3},{3,2},{4,5},{5,4},{6,7},{7,6},{8,9},{9,8},{10,11... | collective-permute-start | bytes 24584 | tf_op jit(solution)/shard_map/ppermute | solution.py:146
  341.8 41.5 %collective-permute-start.26 = (bf16[384,3072]{1,0:T(8,128)(2,1)}, bf16[384,3072]{1,0:T(8,128)(2,1)}, u32[]{:S(2)}, u32[]{:S(2)}) collective-permute-start(bf16[384,3072]{1,0:T(8,128)(2,1)} %get-tuple-element.335), channel_id=1, source_target_pairs={{0,1},{1,0},{2,3},{3,2},{4,5},{5,4},{6,7},{7,6},{8,9},{9,8},{10,11... | collective-permute-start | bytes 7077896 | tf_op jit(solution)/shard_map/ppermute | solution.py:146
  342.2 41.1 %collective-permute-start.27 = (bf16[1536,768]{1,0:T(8,128)(2,1)}, bf16[1536,768]{1,0:T(8,128)(2,1)}, u32[]{:S(2)}, u32[]{:S(2)}) collective-permute-start(bf16[1536,768]{1,0:T(8,128)(2,1)} %get-tuple-element.337), channel_id=1, source_target_pairs={{0,1},{1,0},{2,3},{3,2},{4,5},{5,4},{6,7},{7,6},{8,9},{9,8},{10,11... | collective-permute-start | bytes 7077896 | tf_op jit(solution)/shard_map/ppermute | solution.py:146
  387.3 81.4 %reduce-scatter.7.cloned.1.call-start = ((), (), s32[]{:S(2)}) async-start(), calls=%async_computation.5 | async-start | bytes 2949120 | tf_op jit(solution)/shard_map/reduce_scatter | solution.py:232
  391.8 182.4 %reduce-scatter.9.cloned.1.call-start = ((), (), s32[]{:S(2)}) async-start(), calls=%async_computation.6 | async-start | bytes 737280 | tf_op jit(solution)/shard_map/reduce_scatter | solution.py:232
  471.7 102.6 %reduce-scatter.11.cloned.1.call-start = ((), (), s32[]{:S(2)}) async-start(), calls=%async_computation.7 | async-start | bytes 2211840 | tf_op jit(solution)/shard_map/reduce_scatter | solution.py:232
  480.6 58.5 %collective-permute-start.37 = (bf16[4,208,768]{2,1,0:T(8,128)(2,1)}, bf16[4,208,768]{2,1,0:T(8,128)(2,1)}, u32[]{:S(2)}, u32[]{:S(2)}) collective-permute-start(bf16[4,208,768]{2,1,0:T(8,128)(2,1)} %get-tuple-element.582), channel_id=1, source_target_pairs={{2,0},{3,1},{4,6},{5,7},{10,8},{11,9},{12,14},{13,15},{18,16},{19,... | collective-permute-start | bytes 3833864 | tf_op jit(solution)/shard_map/ppermute | solution.py:192
  481.9 57.2 %collective-permute-start.38 = (bf16[4,208,768]{2,1,0:T(8,128)(2,1)}, bf16[4,208,768]{2,1,0:T(8,128)(2,1)}, u32[]{:S(2)}, u32[]{:S(2)}) collective-permute-start(bf16[4,208,768]{2,1,0:T(8,128)(2,1)} %get-tuple-element.406.refs_13_), channel_id=1, source_target_pairs={{0,1},{1,0},{2,3},{3,2},{4,5},{5,4},{6,7},{7,6},{8,9},{9,8},{10,11... | collective-permute-start | bytes 3833864 | tf_op jit(solution)/shard_map/ppermute | solution.py:146
  482.6 179.8 %all-reduce.17.cloned.1.call-start = ((), (), s32[]{:S(2)}) async-start(), calls=%async_computation.8 | async-start | bytes 3538944 | tf_op jit(solution)/shard_map/psum | solution.py:236
  582.1 43.9 %collective-permute-start.43 = (bf16[8,768,128]{2,1,0:T(8,128)(2,1)}, bf16[8,768,128]{2,1,0:T(8,128)(2,1)}, u32[]{:S(2)}, u32[]{:S(2)}) collective-permute-start(bf16[8,768,128]{2,1,0:T(8,128)(2,1)} %constant_dynamic-slice_fusion.4), channel_id=1, source_target_pairs={{0,8},{8,0},{16,24},{24,16},{1,9},{9,1},{17,25},{25,17},{2,10},{10... | collective-permute-start | bytes 4718600 | tf_op jit(solution)/shard_map/ppermute | solution.py:141
  599.7 62.7 %collective-permute-start.45 = (bf16[8,768,128]{2,1,0:T(8,128)(2,1)}, bf16[8,768,128]{2,1,0:T(8,128)(2,1)S(1)}, u32[]{:S(2)}, u32[]{:S(2)}) collective-permute-start(bf16[8,768,128]{2,1,0:T(8,128)(2,1)} %constant_dynamic-slice_fusion.2), channel_id=1, source_target_pairs={{0,16},{8,24},{16,0},{24,8},{1,17},{9,25},{17,1},{25,9},{2,18},{10... | collective-permute-start | bytes 4718600 | tf_op jit(solution)/shard_map/ppermute | solution.py:141
  662.4 40.3 %collective-permute-start.49 = (bf16[4,4,208,512]{3,2,1,0:T(8,128)(2,1)}, bf16[4,4,208,512]{3,2,1,0:T(8,128)(2,1)}, u32[]{:S(2)}, u32[]{:S(2)}) collective-permute-start(bf16[4,4,208,512]{3,2,1,0:T(8,128)(2,1)} %copy-done.49), channel_id=1, source_target_pairs={{0,1},{1,0},{2,3},{3,2},{4,5},{5,4},{6,7},{7,6},{8,9},{9,8},{10,11... | collective-permute-start | bytes 10223624 | tf_op jit(solution)/shard_map/ppermute | solution.py:146
  (252 other events, 2666.6 us)
Sparse Core Ops, SparseCore 0:
  387.4 37.2 reduce-scatter.4
  428.4 37.3 reduce-scatter.6
  471.8 25.8 reduce-scatter.8
  501.4 32.4 reduce-scatter.10
  579.4 82.9 all-reduce.16

commit v6 on v5

--- a/solution.py
+++ b/solution.py
@@ -281,6 +281,26 @@
 
 def unblock_rows(value, rows):
     return value.reshape(-1, rows, 128).transpose(1, 0, 2).reshape(rows, -1)
+
+
+THIN_ROWS = 16
+
+
+def encode(values):
+    wide = lax.reduce_precision(values[:, :-THIN_ROWS], 8, 7)
+    thin = values[:, -THIN_ROWS:]
+    first = lax.reduce_precision(thin, 8, 7)
+    second = lax.reduce_precision(thin - first, 8, 7)
+    third = lax.reduce_precision(thin - first - second, 8, 7)
+    return jnp.concatenate([wide, first, second, third], axis=1).astype(jnp.bfloat16)
+
+
+def decode(values):
+    values = values.astype(jnp.float32)
+    rows = values.shape[1] - 3 * THIN_ROWS
+    ends = [rows + at * THIN_ROWS for at in range(4)]
+    first, second, third = [values[:, ends[at] : ends[at + 1]] for at in range(3)]
+    return jnp.concatenate([values[:, :rows], first + second + third], axis=1)
 
 
 def grid_params(mebibytes, semantics=1):
@@ -1399,14 +1419,13 @@
             grad_down_bias,
         )
         parts = [block_rows(part) for part in wide]
-        thin = [part.reshape(-1, 128) for part in narrow]
+        thin = [part.reshape(-1) for part in narrow]
         length = sum(part.shape[0] for part in thin)
-        thin = jnp.concatenate(thin + [jnp.zeros((-length % 128, 128), jnp.float32)])
+        thin = jnp.concatenate(thin + [jnp.zeros((-length % 16384,), jnp.float32)])
         (thin,) = tie(thin)
-        parts.append(thin)
-        length = sum(part.shape[0] for part in parts)
-        parts.append(jnp.zeros((-length % 256, 128), jnp.float32))
-        small = jnp.concatenate(parts)
+        thin = thin.reshape(8, -1, 128)
+        (thin,) = tie(thin)
+        small = jnp.concatenate([jnp.concatenate(parts).reshape(8, -1, 128), thin], axis=1)
         return wide, narrow, parts, small
 
     chip_emb = jnp.concatenate([grad_emb, beside_emb])
@@ -1448,7 +1467,7 @@
         wide, narrow, parts, small = pack(hyper_grads)
         line_pixels = [pixel_block(0, 0), pixel_block(0, 1)]
         small, end3, line_emb, line_pixels = tie(small, end3, line_emb, line_pixels)
-        small_came = swap_batch(part_of(small, 1 - core, 2), 1)
+        small_came = swap_batch(encode(part_of(small, 1 - core, 2)), 1)
         far = jnp.where(chip == 1, right1, jnp.where(chip == 2, left1, end3))
         line_emb += [far, swap_batch(far, 1)]
         small, small_came, line_emb = tie(small, small_came, line_emb)
@@ -1486,9 +1505,9 @@
         ]
     else:
         def small_hop(hop):
-            return swap_batch(part_of(small, chip ^ hop, 4), 2 * hop)
-
-        small = part_of(small, core, 2) + small_came
+            return swap_batch(encode(part_of(small, chip ^ hop, 4)), 2 * hop)
+
+        small = part_of(small, core, 2) + decode(small_came)
         small_came = [small_hop(1), small_hop(2)]
         kernel_one = line_grads(low_turned, cells, line_pixels, line_emb, 0, 2)
         kernel_one, line_emb, small, small_came, share_out_rows, share_qkv = tie(
@@ -1504,7 +1523,7 @@
             row_mine(share) for share in (share_qkv, share_out_rows, share_up, share_down)
         ]
         came = sum_out(sums, False)
-        small = sum(small_came, part_of(small, chip, 4))
+        small = encode(sum([decode(one) for one in small_came], part_of(small, chip, 4)))
         small_came = swap_group(small, 1)
         own_back = pixel_grads(chip_emb, kernels, rates, 0)
         other_back = pixel_grads(chip_emb, kernels, rates, 1)
@@ -1514,26 +1533,26 @@
 
         sums = sum_in(sums, came, False)
         came = sum_out(sums, True)
-        small = small + small_came
+        small = encode(decode(small) + decode(small_came))
         small_came = swap_group(small, 2)
         other_back = swap_batch(other_back, 1)
-        wide_mine = jnp.concatenate([mine_qkv, mine_out, mine_up], axis=1)
-        wide_came = swap_batch(wide_mine, 1)
-        came, other_back, small_came, wide_came, block_out = tie(
-            came, other_back, small_came, wide_came, block_out
+        came, other_back, small_came, block_out, mine_qkv, mine_out, mine_up, mine_down = tie(
+            came, other_back, small_came, block_out, mine_qkv, mine_out, mine_up, mine_down
         )
 
         sums = sum_in(sums, came, True)
         came = share_out(sums, True)
-        small = small + small_came
+        small = encode(decode(small) + decode(small_came))
         small_came = [swap_batch(small, 2), swap_batch(small, 4)]
         pixel_grad = join_pixels(
             own_back, other_back, core, patches, cells, pixel_cells, band_slots
         )
+        wide_mine = jnp.concatenate([mine_qkv, mine_out, mine_up], axis=1)
+        wide_came = swap_batch(wide_mine, 1)
+        came, small, small_came, pixel_grad, wide_came, mine_down = tie(
+            came, small, small_came, pixel_grad, wide_came, mine_down
+        )
         down_came = swap_batch(mine_down, 1)
-        came, small, small_came, pixel_grad, down_came = tie(
-            came, small, small_came, pixel_grad, down_came
-        )
 
         sums = share_in(sums, came, True)
         early, late = ([value[: cells // 8] for value in sums], [value[cells // 8 :] for value in sums])
@@ -1547,18 +1566,20 @@
         early, late, small_came, totals = tie(early, late, small_came, totals)
         late = share_out(late, False)
         small = four_in_order(chip, [small] + small_came)
-        small = in_order(core, small, swap_batch(small, 1))
+        small = decode(in_order(core, small, swap_batch(small, 1)))
     pixel_grad = pixel_grad[None]
 
     found = []
     at = 0
+    wide_rows = small[:, :-THIN_ROWS].reshape(-1, 128)
+    thin_flat = small[:, -THIN_ROWS:].reshape(-1)
     for part, like in zip(parts, wide):
-        found.append(unblock_rows(small[at : at + part.shape[0]], like.shape[0]))
+        found.append(unblock_rows(wide_rows[at : at + part.shape[0]], like.shape[0]))
         at += part.shape[0]
+    at = 0
     for like in narrow:
-        count = like.size // 128
-        found.append(small[at : at + count].reshape(like.shape))
-        at += count
+        found.append(thin_flat[at : at + like.size].reshape(like.shape))
+        at += like.size
     batch_mean, batch_var = bin_stats(found[13], found[14], found[15], patches * pixel_cells)
     if tuned_mesh():
         late, found, batch_mean, batch_var = tie(late, found, batch_mean, batch_var)

time: 808 us -> 797 us (0.986)
  local copies, waits for them, and re-layouts: 185 us -> 172 us
    ppermute x20, waiting for transfers between devices: 48 us -> 61.9 us  [swap_group(): return lax.ppermute(value, 'group', [(at, at ^ bits) for at in range(4)])]
    psum x1, waiting for transfers between devices: 36.4 us -> 23.4 us  [row_mine(): return lax.psum(share, 'batch', axis_index_groups=same_core())]
    dynamic_slice x8 -> x5, local copies, waits for them, and re-layouts: 14.8 us -> 6.07 us  [part_of(): return lax.dynamic_slice_in_dim(value, index * rows, rows)]
    unnamed x428 -> x427, local copies, waits for them, and re-layouts: 87 us -> 93.8 us
  transfers between devices with their start and end apart: 68 -> 68, of which waited for: 22 -> 21; matrix products, arithmetic and copies ran while one was open for 24% -> 24% of each run, Pallas kernels for 30% -> 31%
where the time goes in v6:
time: 797 us; the launch traced here: 787 us
  Pallas kernels  258 us (32%)
  local copies, waits for them, and re-layouts  172 us (22%)
  waiting for transfers between devices  140 us (18%)
  starting transfers between devices  84.9 us (11%)
  other arithmetic  83.7 us (11%)
  matrix products  31.6 us (4%)
  between operations  17.1 us (2%)
    unnamed x427, local copies, waits for them, and re-layouts  93.8 us
    pallas_call x7, Pallas kernels, embed_piece(): pl.pallas_call(partial(embed_kernel, first, count), grid_spec=pltpu.Prefe...  64.9 us
    ppermute x20, waiting for transfers between devices, swap_group(): return lax.ppermute(value, 'group', [(at, at ^ bits) for at in range(4)])  61.9 us
    ppermute x33, starting transfers between devices, swap_batch(): lax.ppermute(value, 'batch', [(at, at ^ bits) for at in range(count)])  37 us
    pallas_call x1, Pallas kernels, mlp(): pl.pallas_call(mlp_kernel, grid_spec=pltpu.PrefetchScalarGridSpec(num_sca...  33.5 us
    pallas_call x4, Pallas kernels, band_piece(): pl.pallas_call(partial(band_kernel, first, count), grid_spec=pltpu.Prefet...  31.8 us
    ppermute x8, waiting for transfers between devices, along_line(): return lax.ppermute(value, 'batch', pairs)  30 us
    pallas_call x2, Pallas kernels, line_grads(): pl.pallas_call(body, in_specs=[vmem] * (1 + len(pixels) + len(grads)), ou...  24.8 us
  transfers between devices with their start and end apart: 68, of which 21 were waited for; matrix products, arithmetic and copies ran while one was open for 24% of the time, Pallas kernels for 31%

profile of v6, /device:TPU:0, one launch (start us, length us, event | category | flops | bytes accessed | tf_op | source)
XLA Modules:
  0.0 786.7 jit_solution(7303217598715648616)
XLA Ops:
  27.8 21.9 %collective-permute-done = bf16[8,768,128]{2,1,0:T(8,128)(2,1)} collective-permute-done((bf16[8,768,128]{2,1,0:T(8,128)(2,1)}, bf16[8,768,128]{2,1,0:T(8,128)(2,1)}, u32[]{:S(2)}, u32[]{:S(2)}) %collective-permute-start) | collective-permute-done | bytes 1572896 | tf_op jit(solution)/shard_map/ppermute | solution.py:187
  63.2 15.4 %split_pixels.1 = (bf16[4,4,208,512]{3,2,1,0:T(8,128)(2,1)S(1)}, bf16[4,4,208,512]{3,2,1,0:T(8,128)(2,1)}) custom-call(s32[1]{0:T(128)} %bitcast.core_ref, bf16[4,196,16,256]{3,2,1,0:T(8,128)(2,1)S(1)} %bitcast.224, f32[4,16,1]{2,1,0:T(8,128)S(1)} %convolution_bitcast_fusion.7.mean_ref, f32[4,16,1]{2,1,0:T(8,128)S(1)} %copy.191.rate_ref), custom_call_target="tpu_custom_call" | custom-call | flops 1 | bytes 1 | tf_op jit(solution)/shard_map/split_pixels/pallas_call | solution.py:376
  80.4 7.5 collective-permute-done.5.refs_1_
  107.8 8.4 %collective-permute-start.11 = (bf16[4,208,512]{2,1,0:T(8,128)(2,1)}, bf16[4,208,512]{2,1,0:T(8,128)(2,1)S(1)}, u32[]{:S(2)}, u32[]{:S(2)}) collective-permute-start(bf16[4,208,512]{2,1,0:T(8,128)(2,1)} %dynamic-slice_bitcast_fusion.7), channel_id=1, source_target_pairs={{0,4},{1,5},{2,6},{3,7},{4,0},{5,1},{6,2},{7,3},{8,12},{9,13},{10,... | collective-permute-start | bytes 2555912 | tf_op jit(solution)/shard_map/ppermute | solution.py:146
  123.0 10.2 %embed_piece.7 = (f32[4,208,768]{2,1,0:T(8,128)S(1)}, f32[4,208,768]{2,1,0:T(8,128)S(1)}, bf16[4,8,512,768]{3,2,1,0:T(8,128)(2,1)}) custom-call(s32[5]{0:T(128)S(1)} %stack.90.at_ref, bf16[128,128]{1,0:T(8,128)(2,1)S(1)} %copy.201.low_ref, bf16[32,768,128]{2,1,0:T(8,128)(2,1)} %refs_0_.3, bf16[4,4,208,512]{3,2,1,0:T(8,128)(2,1)} %copy-done.1, ...), custom_call_target="tpu_custom_call" | custom-call | flops 1 | bytes 1 | tf_op jit(solution)/shard_map/embed_piece/pallas_call | solution.py:505
  136.1 11.8 %embed_piece.8 = (f32[4,208,768]{2,1,0:T(8,128)}, f32[4,208,768]{2,1,0:T(8,128)}, bf16[4,8,512,768]{3,2,1,0:T(8,128)(2,1)}) custom-call(s32[4]{0:T(128)S(1)} %add_add_fusion.3.at_ref, bf16[128,128]{1,0:T(8,128)(2,1)S(1)} %copy.201.low_ref, bf16[8,768,128]{2,1,0:T(8,128)(2,1)S(1)} %copy-done.25, ...), custom_call_target="tpu_custom_call", output_to_operand_aliasing={{0}: (7, {}), {1}: (8, {}), {2}: (9, {})} | custom-call | flops 1 | bytes 1 | tf_op jit(solution)/shard_map/embed_piece/pallas_call | solution.py:505
  152.6 8.7 %collective-permute-done.8 = bf16[8,768,128]{2,1,0:T(8,128)(2,1)} collective-permute-done((bf16[8,768,128]{2,1,0:T(8,128)(2,1)}, bf16[8,768,128]{2,1,0:T(8,128)(2,1)}, u32[]{:S(2)}, u32[]{:S(2)}) %collective-permute-start.8) | collective-permute-done | bytes 1572896 | tf_op jit(solution)/shard_map/ppermute | solution.py:192
  197.8 11.7 %embed_piece.10 = (f32[4,208,768]{2,1,0:T(8,128)}, f32[4,208,768]{2,1,0:T(8,128)}, bf16[4,8,512,768]{3,2,1,0:T(8,128)(2,1)}) custom-call(s32[4]{0:T(128)S(1)} %get-tuple-element.702.at_ref, bf16[128,128]{1,0:T(8,128)(2,1)S(1)} %copy.201.low_ref, ...), custom_call_target="tpu_custom_call", output_to_operand_aliasing={{0}: (7, {}), {1}: (8, {}), {2}: (9, {})} | custom-call | flops 1 | bytes 1 | tf_op jit(solution)/shard_map/embed_piece/pallas_call | solution.py:505
  239.7 12.2 %embed_piece.12 = (f32[4,208,768]{2,1,0:T(8,128)}, f32[4,208,768]{2,1,0:T(8,128)}, bf16[4,8,512,768]{3,2,1,0:T(8,128)(2,1)}) custom-call(s32[4]{0:T(128)S(1)} %get-tuple-element.701.at_ref, bf16[128,128]{1,0:T(8,128)(2,1)S(1)} %copy.201.low_ref, bf16[8,768,128]{2,1,0:T(8,128)(2,1)S(1)} %copy-done.18, ...), custom_call_target="tpu_custom_call", output_to_operand_aliasing={{0}: (7, {}), {1}: (8, {}), {2}: (9, {})} | custom-call | flops 1 | bytes 1 | tf_op jit(solution)/shard_map/embed_piece/pallas_call | solution.py:505
  304.7 33.5 %mlp.1 = (bf16[832,768]{1,0:T(8,128)(2,1)S(1)}, f32[832,768]{1,0:T(8,128)}, bf16[384,3072]{1,0:T(8,128)(2,1)}, bf16[384,3072]{1,0:T(8,128)(2,1)}, bf16[1536,768]...) custom-call(s32[1]{0:T(128)} %bitcast.core_ref, bf16[832,768]{1,0:T(8,128)(2,1)} %bitcast.231, ...), custom_call_target="tpu_custom_call" | custom-call | flops 1 | bytes 1 | tf_op jit(solution)/shard_map/mlp/pallas_call | solution.py:1068
  353.9 17.0 %attend_back.1 = (bf16[4,208,2304]{2,1,0:T(8,128)(2,1)S(1)}, f32[1,2304]{1,0:T(1,128)S(1)}) custom-call(bf16[4,208,2304]{2,1,0:T(8,128)(2,1)S(1)} %copy-done.21, bf16[4,208,768]{2,1,0:T(8,128)(2,1)S(1)} %get-tuple-element.331.grad_ref), custom_call_target="tpu_custom_call" | custom-call | flops 1 | bytes 1 | tf_op jit(solution)/shard_map/attend_back/pallas_call | solution.py:779
  412.8 8.5 %band_piece.4.refs_6_ = f32[128,128]{1,0:T(8,128)S(1)} custom-call(s32[5]{0:T(128)S(1)} %stack.90.at_ref, bf16[8,208,768]{2,1,0:T(8,128)(2,1)S(1)} %constant_dynamic-update-slice_fusion.2.grad_ref, bf16[32,768,128]{2,1,0:T(8,128)(2,1)} %refs_0_.3, bf16[4,4,208,512]{3,2,1,0:T(8,128)(2,1)S(1)} %copy-done.2, ...), custom_call_target="tpu_custom_call" | custom-call | flops 1 | bytes 1 | tf_op jit(solution)/shard_map/band_piece/pallas_call | solution.py:664
  424.4 7.6 band_piece.5.refs_6_
  448.6 8.0 %band_piece.6.refs_6_ = f32[128,128]{1,0:T(8,128)S(1)} custom-call(s32[5]{0:T(128)S(1)} %copy-done.86, bf16[8,208,768]{2,1,0:T(8,128)(2,1)S(1)} %copy-done.13, bf16[8,768,128]{2,1,0:T(8,128)(2,1)S(1)} %get-tuple-element.604.refs_0_, bf16[12,768,128]{2,1,0:T(8,128)(2,1)} %collective-permute-done.9.refs_1_, ...), custom_call_target="tpu_custom_call" | custom-call | flops 1 | bytes 1 | tf_op jit(solution)/shard_map/band_piece/pallas_call | solution.py:664
  456.7 7.6 band_piece.7
  567.2 12.5 %line_grads.2 = bf16[16,768,128]{2,1,0:T(8,128)(2,1)} custom-call(bf16[128,512]{1,0:T(8,128)(2,1)S(1)} %bitcast.234, bf16[4,208,512]{2,1,0:T(8,128)(2,1)S(1)} %dynamic-slice_bitcast_fusion.1.refs_1_, bf16[4,208,512]{2,1,0:T(8,128)(2,1)S(1)} %get-tuple-element.376.refs_2_, bf16[4,208,512]{2,1,0:T(8,128)(2,1)S(1)} %copy-done.54, ...), custom_call_target="tpu_custom_call" | custom-call | flops 1 | bytes 1 | tf_op jit(solution)/shard_map/line_grads/pallas_call | solution.py:603
  588.0 12.3 %line_grads.3 = bf16[16,768,128]{2,1,0:T(8,128)(2,1)} custom-call(bf16[128,512]{1,0:T(8,128)(2,1)S(1)} %bitcast.235, bf16[4,208,512]{2,1,0:T(8,128)(2,1)S(1)} %dynamic-slice_bitcast_fusion.1.refs_1_, bf16[4,208,512]{2,1,0:T(8,128)(2,1)S(1)} %get-tuple-element.376.refs_2_, bf16[4,208,512]{2,1,0:T(8,128)(2,1)S(1)} %copy-done.55, ...), custom_call_target="tpu_custom_call" | custom-call | flops 1 | bytes 1 | tf_op jit(solution)/shard_map/line_grads/pallas_call | solution.py:603
  605.0 7.4 pixel_grads.3
  614.1 7.5 pixel_grads.2.mine_ref
  625.5 12.4 %collective-permute-done.45 = bf16[8,768,128]{2,1,0:T(8,128)(2,1)} collective-permute-done((bf16[8,768,128]{2,1,0:T(8,128)(2,1)S(1)}, bf16[8,768,128]{2,1,0:T(8,128)(2,1)}, u32[]{:S(2)}, u32[]{:S(2)}) %collective-permute-start.45) | collective-permute-done | bytes 1572896 | tf_op jit(solution)/shard_map/ppermute | solution.py:141
  637.9 23.4 %all-reduce.17.cloned.1.call-done = (bf16[96,2304]{1,0:T(8,128)(2,1)}, bf16[96,768]{1,0:T(8,128)(2,1)}, bf16[96,3072]{1,0:T(8,128)(2,1)}, bf16[384,768]{1,0:T(8,128)(2,1)}) async-done(((bf16[96,2304]{1,0:T(8,128)(2,1)}, bf16[96,768]{1,0:T(8,128)(2,1)}, bf16[96,3072]{1,0:T(8,128)(2,1)}, bf16[384,768]{1,0:T(8,128)(2,1)}), (bf16[96,2304]{1,0:T(8,128)(2,1)}, bf16[96,768]{1,0:T(8,128)(2,1)}, ...) | async-done | bytes 1769488 | tf_op jit(solution)/shard_map/psum | solution.py:236
  671.6 21.4 %collective-permute-done.50 = bf16[1,736,128]{2,1,0:T(8,128)(2,1)S(1)} collective-permute-done((bf16[1,736,128]{2,1,0:T(8,128)(2,1)S(1)}, bf16[1,736,128]{2,1,0:T(8,128)(2,1)S(1)}, u32[]{:S(2)}, u32[]{:S(2)}) %collective-permute-start.50) | collective-permute-done | bytes 188448 | tf_op jit(solution)/shard_map/ppermute | solution.py:141
  702.1 14.1 %join_pixels.1 = bf16[4,196,16,256]{3,2,1,0:T(8,128)(2,1)} custom-call(s32[1]{0:T(128)} %bitcast.core_ref, bf16[4,4,208,512]{3,2,1,0:T(8,128)(2,1)S(1)} %copy-done.36, bf16[4,4,208,512]{3,2,1,0:T(8,128)(2,1)} %collective-permute-done.49.other_ref), custom_call_target="tpu_custom_call" | custom-call | flops 1 | bytes 1 | tf_op jit(solution)/shard_map/join_pixels/pallas_call | solution.py:435
  772.2 7.6 assemble.1
  (827 shorter events, 460.8 us)
Async XLA Ops:
  7.3 424.8 %reduce-scatter.5.cloned.1.call-start = ((), (), s32[]{:S(2)}) async-start(), calls=%async_computation.4 | async-start | bytes 2949120 | tf_op jit(solution)/shard_map/reduce_scatter | solution.py:232
  10.1 39.6 %collective-permute-start = (bf16[8,768,128]{2,1,0:T(8,128)(2,1)}, bf16[8,768,128]{2,1,0:T(8,128)(2,1)}, u32[]{:S(2)}, u32[]{:S(2)}) collective-permute-start(bf16[8,768,128]{2,1,0:T(8,128)(2,1)} %constant_dynamic-slice_fusion.7), channel_id=1, source_target_pairs={{2,0},{3,1},{4,2},{5,3},{6,4},{7,5},{10,8},{11,9},{12,10},{13,11},... | collective-permute-start | bytes 4718600 | tf_op jit(solution)/shard_map/ppermute | solution.py:187
  101.8 59.6 %collective-permute-start.10 = (bf16[12,768,128]{2,1,0:T(8,128)(2,1)}, bf16[12,768,128]{2,1,0:T(8,128)(2,1)}, u32[]{:S(2)}, u32[]{:S(2)}) collective-permute-start(bf16[12,768,128]{2,1,0:T(8,128)(2,1)} %get-tuple-element.629), channel_id=1, source_target_pairs={{0,16},{8,24},{16,0},{24,8},{1,17},{9,25},{17,1},{25,9},{2,18},{10... | collective-permute-start | bytes 7077896 | tf_op jit(solution)/shard_map/ppermute | solution.py:141
  102.3 59.1 %collective-permute-start.9 = (bf16[12,768,128]{2,1,0:T(8,128)(2,1)}, bf16[12,768,128]{2,1,0:T(8,128)(2,1)}, u32[]{:S(2)}, u32[]{:S(2)}) collective-permute-start(bf16[12,768,128]{2,1,0:T(8,128)(2,1)} %get-tuple-element.630), channel_id=1, source_target_pairs={{0,8},{8,0},{16,24},{24,16},{1,9},{9,1},{17,25},{25,17},{2,10},{10... | collective-permute-start | bytes 7077896 | tf_op jit(solution)/shard_map/ppermute | solution.py:141
  103.0 58.4 %collective-permute-start.8 = (bf16[8,768,128]{2,1,0:T(8,128)(2,1)}, bf16[8,768,128]{2,1,0:T(8,128)(2,1)}, u32[]{:S(2)}, u32[]{:S(2)}) collective-permute-start(bf16[8,768,128]{2,1,0:T(8,128)(2,1)} %get-tuple-element.605), channel_id=1, source_target_pairs={{2,0},{3,1},{4,6},{5,7},{10,8},{11,9},{12,14},{13,15},{18,16},{19,... | collective-permute-start | bytes 4718600 | tf_op jit(solution)/shard_map/ppermute | solution.py:192
  107.8 44.9 %collective-permute-start.11 = (bf16[4,208,512]{2,1,0:T(8,128)(2,1)}, bf16[4,208,512]{2,1,0:T(8,128)(2,1)S(1)}, u32[]{:S(2)}, u32[]{:S(2)}) collective-permute-start(bf16[4,208,512]{2,1,0:T(8,128)(2,1)} %dynamic-slice_bitcast_fusion.7), channel_id=1, source_target_pairs={{0,4},{1,5},{2,6},{3,7},{4,0},{5,1},{6,2},{7,3},{8,12},{9,13},{10,... | collective-permute-start | bytes 2555912 | tf_op jit(solution)/shard_map/ppermute | solution.py:146
  170.4 52.9 %collective-permute-start.12 = (bf16[12,768,128]{2,1,0:T(8,128)(2,1)}, bf16[12,768,128]{2,1,0:T(8,128)(2,1)}, u32[]{:S(2)}, u32[]{:S(2)}) collective-permute-start(bf16[12,768,128]{2,1,0:T(8,128)(2,1)} %get-tuple-element.628), channel_id=1, source_target_pairs={{0,8},{8,0},{16,24},{24,16},{1,9},{9,1},{17,25},{25,17},{2,10},{10... | collective-permute-start | bytes 7077896 | tf_op jit(solution)/shard_map/ppermute | solution.py:141
  171.7 52.6 %collective-permute-start.13 = (bf16[12,768,128]{2,1,0:T(8,128)(2,1)}, bf16[12,768,128]{2,1,0:T(8,128)(2,1)}, u32[]{:S(2)}, u32[]{:S(2)}) collective-permute-start(bf16[12,768,128]{2,1,0:T(8,128)(2,1)} %get-tuple-element.627), channel_id=1, source_target_pairs={{0,16},{8,24},{16,0},{24,8},{1,17},{9,25},{17,1},{25,9},{2,18},{10... | collective-permute-start | bytes 7077896 | tf_op jit(solution)/shard_map/ppermute | solution.py:141
  177.5 41.1 %collective-permute-start.15 = (bf16[4,208,512]{2,1,0:T(8,128)(2,1)}, bf16[4,208,512]{2,1,0:T(8,128)(2,1)}, u32[]{:S(2)}, u32[]{:S(2)}) collective-permute-start(bf16[4,208,512]{2,1,0:T(8,128)(2,1)} %dynamic-slice_bitcast_fusion.5), channel_id=1, source_target_pairs={{0,4},{1,5},{2,6},{3,7},{4,0},{5,1},{6,2},{7,3},{8,12},{9,13},{10,... | collective-permute-start | bytes 2555912 | tf_op jit(solution)/shard_map/ppermute | solution.py:146
  264.3 76.4 %collective-permute-start.20 = (bf16[4,208,512]{2,1,0:T(8,128)(2,1)}, bf16[4,208,512]{2,1,0:T(8,128)(2,1)S(1)}, u32[]{:S(2)}, u32[]{:S(2)}) collective-permute-start(bf16[4,208,512]{2,1,0:T(8,128)(2,1)} %dynamic-slice_bitcast_fusion.3), channel_id=1, source_target_pairs={{0,6},{1,7},{2,4},{3,5},{4,2},{5,3},{6,0},{7,1},{8,14},{9,15},{10,... | collective-permute-start | bytes 2555912 | tf_op jit(solution)/shard_map/ppermute | solution.py:146
  294.8 44.5 %collective-permute-start.21 = (bf16[128,128]{0,1:T(8,128)(2,1)S(1)}, bf16[128,128]{0,1:T(8,128)(2,1)S(1)}, u32[]{:S(2)}, u32[]{:S(2)}) collective-permute-start(bf16[128,128]{0,1:T(8,128)(2,1)S(1)} %pad_maximum_fusion.19), channel_id=1, source_target_pairs={{0,2},{1,3},{2,0},{3,1},{4,6},{5,7},{6,4},{7,5},{8,10},{9,11},{10,... | collective-permute-start | bytes 98312 | tf_op jit(solution)/shard_map/ppermute | solution.py:146
  296.0 43.3 %collective-permute-start.22 = (bf16[128,128]{0,1:T(8,128)(2,1)S(1)}, bf16[128,128]{0,1:T(8,128)(2,1)S(1)}, u32[]{:S(2)}, u32[]{:S(2)}) collective-permute-start(bf16[128,128]{0,1:T(8,128)(2,1)S(1)} %pad_maximum_fusion.19), channel_id=1, source_target_pairs={{0,4},{1,5},{2,6},{3,7},{4,0},{5,1},{6,2},{7,3},{8,12},{9,13},{10,... | collective-permute-start | bytes 98312 | tf_op jit(solution)/shard_map/ppermute | solution.py:146
  296.0 43.3 %collective-permute-start.23 = (bf16[128,128]{0,1:T(8,128)(2,1)S(1)}, bf16[128,128]{0,1:T(8,128)(2,1)}, u32[]{:S(2)}, u32[]{:S(2)}) collective-permute-start(bf16[128,128]{0,1:T(8,128)(2,1)S(1)} %pad_maximum_fusion.19), channel_id=1, source_target_pairs={{0,6},{1,7},{2,4},{3,5},{4,2},{5,3},{6,0},{7,1},{8,14},{9,15},{10,... | collective-permute-start | bytes 98312 | tf_op jit(solution)/shard_map/ppermute | solution.py:146
  299.3 42.3 %collective-permute-start.24 = (f32[4,512]{1,0:T(4,128)S(1)}, f32[4,512]{1,0:T(4,128)S(1)}, u32[]{:S(2)}, u32[]{:S(2)}) collective-permute-start(f32[4,512]{1,0:T(4,128)S(1)} %tile.10), channel_id=1, source_target_pairs={{0,1},{1,0},{2,3},{3,2},{4,5},{5,4},{6,7},{7,6},{8,9},{9,8},{10,11... | collective-permute-start | bytes 24584 | tf_op jit(solution)/shard_map/ppermute | solution.py:146
  341.6 41.7 %collective-permute-start.26 = (bf16[384,3072]{1,0:T(8,128)(2,1)}, bf16[384,3072]{1,0:T(8,128)(2,1)}, u32[]{:S(2)}, u32[]{:S(2)}) collective-permute-start(bf16[384,3072]{1,0:T(8,128)(2,1)} %get-tuple-element.339), channel_id=1, source_target_pairs={{0,1},{1,0},{2,3},{3,2},{4,5},{5,4},{6,7},{7,6},{8,9},{9,8},{10,11... | collective-permute-start | bytes 7077896 | tf_op jit(solution)/shard_map/ppermute | solution.py:146
  342.1 41.3 %collective-permute-start.27 = (bf16[1536,768]{1,0:T(8,128)(2,1)}, bf16[1536,768]{1,0:T(8,128)(2,1)}, u32[]{:S(2)}, u32[]{:S(2)}) collective-permute-start(bf16[1536,768]{1,0:T(8,128)(2,1)} %get-tuple-element.341), channel_id=1, source_target_pairs={{0,1},{1,0},{2,3},{3,2},{4,5},{5,4},{6,7},{7,6},{8,9},{9,8},{10,11... | collective-permute-start | bytes 7077896 | tf_op jit(solution)/shard_map/ppermute | solution.py:146
  387.4 81.6 %reduce-scatter.7.cloned.1.call-start = ((), (), s32[]{:S(2)}) async-start(), calls=%async_computation.5 | async-start | bytes 2949120 | tf_op jit(solution)/shard_map/reduce_scatter | solution.py:232
  391.8 187.9 %reduce-scatter.9.cloned.1.call-start = ((), (), s32[]{:S(2)}) async-start(), calls=%async_computation.6 | async-start | bytes 737280 | tf_op jit(solution)/shard_map/reduce_scatter | solution.py:232
  392.1 39.9 %collective-permute-start.29 = (bf16[4,208,768]{2,1,0:T(8,128)(2,1)}, bf16[4,208,768]{2,1,0:T(8,128)(2,1)}, u32[]{:S(2)}, u32[]{:S(2)}) collective-permute-start(bf16[4,208,768]{2,1,0:T(8,128)(2,1)} %copy-done.37), channel_id=1, source_target_pairs={{2,0},{3,1},{4,2},{5,3},{6,4},{7,5},{10,8},{11,9},{12,10},{13,11},... | collective-permute-start | bytes 3833864 | tf_op jit(solution)/shard_map/ppermute | solution.py:187
  471.8 107.9 %reduce-scatter.11.cloned.1.call-start = ((), (), s32[]{:S(2)}) async-start(), calls=%async_computation.7 | async-start | bytes 2211840 | tf_op jit(solution)/shard_map/reduce_scatter | solution.py:232
  480.7 68.5 %collective-permute-start.37 = (bf16[4,208,768]{2,1,0:T(8,128)(2,1)}, bf16[4,208,768]{2,1,0:T(8,128)(2,1)}, u32[]{:S(2)}, u32[]{:S(2)}) collective-permute-start(bf16[4,208,768]{2,1,0:T(8,128)(2,1)} %get-tuple-element.614), channel_id=1, source_target_pairs={{2,0},{3,1},{4,6},{5,7},{10,8},{11,9},{12,14},{13,15},{18,16},{19,... | collective-permute-start | bytes 3833864 | tf_op jit(solution)/shard_map/ppermute | solution.py:192
  482.2 67.0 %collective-permute-start.38 = (bf16[4,208,768]{2,1,0:T(8,128)(2,1)}, bf16[4,208,768]{2,1,0:T(8,128)(2,1)}, u32[]{:S(2)}, u32[]{:S(2)}) collective-permute-start(bf16[4,208,768]{2,1,0:T(8,128)(2,1)} %get-tuple-element.410.refs_13_), channel_id=1, source_target_pairs={{0,1},{1,0},{2,3},{3,2},{4,5},{5,4},{6,7},{7,6},{8,9},{9,8},{10,11... | collective-permute-start | bytes 3833864 | tf_op jit(solution)/shard_map/ppermute | solution.py:146
  482.8 178.5 %all-reduce.17.cloned.1.call-start = ((), (), s32[]{:S(2)}) async-start(), calls=%async_computation.8 | async-start | bytes 3538944 | tf_op jit(solution)/shard_map/psum | solution.py:236
  585.3 40.1 %collective-permute-start.43 = (bf16[8,768,128]{2,1,0:T(8,128)(2,1)S(1)}, bf16[8,768,128]{2,1,0:T(8,128)(2,1)}, u32[]{:S(2)}, u32[]{:S(2)}) collective-permute-start(bf16[8,768,128]{2,1,0:T(8,128)(2,1)S(1)} %constant_dynamic-slice_fusion.4), channel_id=1, source_target_pairs={{0,8},{8,0},{16,24},{24,16},{1,9},{9,1},{17,25},{25,17},{2,10},{10... | collective-permute-start | bytes 4718600 | tf_op jit(solution)/shard_map/ppermute | solution.py:141
  (245 other events, 2649.8 us)
Sparse Core Ops, SparseCore 0:
  387.5 37.3 reduce-scatter.4
  428.5 37.3 reduce-scatter.6
  472.0 25.6 reduce-scatter.8
  501.4 32.4 reduce-scatter.10
  583.8 77.4 all-reduce.16
